TPU v7x, 32 devices: a whole 2x2x4 slice. The times are simulated.
32 devices in a mesh: pipe: 8 (over y, x, core), fsdp: 4 (over z).
Axes of the slice: x: 2, y: 2, z: 4, core: 2. Of those that a mesh axis runs over, the one named last changes fastest.
Arguments:
- handoff_gradient: bfloat16 [8, 768, 8192], P('pipe', 'fsdp'), may hold values from -12 to 12
- output_weight: bfloat16 [8, 8192, 8192], P('pipe', 'fsdp'), may hold values from -0.0625 to 0.0625
- adapter_down: bfloat16 [8, 16, 8192], P('pipe', None, 'fsdp'), may hold values from -0.0625 to 0.0625
- adapter_up: bfloat16 [8, 16, 8192], P('pipe', None, 'fsdp'), may hold values from -0.29882812 to 0.29882812
- stored_queries: bfloat16 [8, 768, 8192], P('pipe', None, 'fsdp'), may hold values from -64 to 64
- stored_keys: bfloat16 [8, 768, 1024], P('pipe', None, 'fsdp'), may hold values from -3 to 3
- stored_values: bfloat16 [8, 768, 1024], P('pipe', None, 'fsdp'), may hold values from -6 to 6
- segments: int32 [8, 768], P('pipe'), may hold values from 0 to 7, never falling along the last dimension, each value on 1 to 384 neighbouring positions
Outputs:
- query_gradient: bfloat16 [8, 768, 8192], P('pipe', None, 'fsdp')
- key_gradient: bfloat16 [8, 768, 1024], P('pipe', None, 'fsdp')
- value_gradient: bfloat16 [8, 768, 1024], P('pipe', None, 'fsdp')
- down_map_gradient: float32 [8, 16, 8192], P('pipe', None, 'fsdp')
- up_map_gradient: float32 [8, 16, 8192], P('pipe', None, 'fsdp')
Inputs may be any that keep to these rules, and one draw needn't show every extreme that they name: `segments`: ids never fall along a micro-batch.
All inputs are finite; a program needn't handle non-finite values.
Results may differ from a plain program's by a relative error of at most 0.015.
The roundings to bfloat16 on the way count: a program that leaves them out, or rounds other values in their place, can miss the bound.
Values may be sent and summed in bfloat16 or wider, within the bound.
No kernel may reach another device: no remote copies, remote signals or barrier semaphores. Data moves between devices by JAX's collectives and lax.ppermute only.
A program may use at most 128 MiB of HBM per device.

v0:
```python
import math

import jax
import jax.numpy as jnp
from jax import lax
from jax.sharding import PartitionSpec as P

HEAD_SIZE = 128


adapter_scale = 2.0


def swapped(block, axis, distance):
    count = lax.axis_size(axis)
    route = []
    for low in range(count):
        high = low | 1 << distance
        if high != low and high < count:
            route += [(low, high), (high, low)]
    return lax.ppermute(block, axis, route)


def shifted(block, axis, distance):
    devices = range(lax.axis_size(axis))
    route = [((i - distance) % len(devices), i) for i in devices]
    return lax.ppermute(block, axis, route)


def attend(query_block, key_head, value_head, context_gradient, allowed):
    inv_scale = 1.0 / math.sqrt(query_block.shape[-1])
    scores = (
        jnp.einsum("bngd,snd->ngbs", query_block, key_head, preferred_element_type=jnp.float32)
        * inv_scale
    )
    scores = jnp.where(allowed[None, None], scores, -jnp.inf)
    row_max = jnp.max(scores, axis=-1, keepdims=True)
    expanded = jnp.exp(scores - row_max)
    attn_probs = expanded / jnp.sum(expanded, axis=-1, keepdims=True)
    probs_low = attn_probs.astype(jnp.bfloat16)
    context_rows = jnp.einsum(
        "ngbs,snd->bngd", probs_low, value_head, preferred_element_type=jnp.float32
    )
    context_rows = lax.optimization_barrier(context_rows.astype(jnp.bfloat16))
    grad_probs = jnp.einsum(
        "bngd,snd->ngbs", context_gradient, value_head, preferred_element_type=jnp.float32
    )
    row_delta = jnp.sum(
        context_gradient.astype(jnp.float32) * context_rows.astype(jnp.float32), axis=-1
    )
    row_delta = jnp.transpose(row_delta, (1, 2, 0))[..., None]
    grad_scores = (attn_probs * (grad_probs - row_delta)).astype(jnp.bfloat16)
    grad_query = jnp.einsum(
        "ngbs,snd->bngd", grad_scores, key_head, preferred_element_type=jnp.float32
    )
    grad_query = (grad_query * inv_scale).astype(jnp.bfloat16)
    gradient_of_key = (
        jnp.einsum("ngbs,bngd->snd", grad_scores, query_block, preferred_element_type=jnp.float32)
        * inv_scale
    )
    gradient_of_value = jnp.einsum(
        "ngbs,bngd->snd", probs_low, context_gradient, preferred_element_type=jnp.float32
    )
    return (context_rows, grad_query, gradient_of_key, gradient_of_value)


def per_device(
    handoff_gradient,
    output_weight,
    adapter_down,
    adapter_up,
    stored_queries,
    stored_keys,
    stored_values,
    segments,
):
    pipe_count = lax.axis_size("pipe")
    member = lax.axis_index("fsdp")
    query_width = stored_queries.shape[2]
    kv_width = stored_keys.shape[2]
    packed = jnp.concatenate([stored_queries[0], stored_keys[0], stored_values[0]], axis=1)
    depth_levels = pipe_count.bit_length() - 1
    bit_order = list(range(depth_levels))
    for bit_index in bit_order:
        packed = swapped(packed, "pipe", bit_index)
    query = packed[:, :query_width]
    key_local = packed[:, query_width : query_width + kv_width]
    value_local = packed[:, query_width + kv_width :]
    sender_whole = lax.all_gather(handoff_gradient[0], "fsdp", axis=0, tiled=True)
    incoming_gradient = shifted(sender_whole, "pipe", -1)
    token_count = incoming_gradient.shape[0]
    local_width = adapter_up.shape[2]
    local_columns = lax.dynamic_slice_in_dim(
        incoming_gradient, member * local_width, local_width, 1
    )
    rank_portion = jnp.einsum(
        "yh,gh->yg", local_columns, adapter_up[0], preferred_element_type=jnp.float32
    )
    rank_gradient = lax.psum(rank_portion, "fsdp")
    frozen_portion = jnp.einsum(
        "td,qd->tq", incoming_gradient, output_weight[0], preferred_element_type=jnp.float32
    )
    rank_projected = jnp.dot(
        rank_gradient, adapter_down[0].astype(jnp.float32), precision=lax.Precision.HIGHEST
    )
    context_gradient = (frozen_portion + adapter_scale * rank_projected).astype(jnp.bfloat16)
    kv_heads = kv_width // HEAD_SIZE
    query_group_count = query_width // HEAD_SIZE // kv_heads
    query_shaped = query.reshape(token_count, kv_heads, query_group_count, HEAD_SIZE)
    grad_shaped = context_gradient.reshape(token_count, kv_heads, query_group_count, HEAD_SIZE)
    key_shaped = key_local.reshape(token_count, kv_heads, HEAD_SIZE)
    value_shaped = value_local.reshape(token_count, kv_heads, HEAD_SIZE)
    block_rows = math.gcd(token_count, 512)
    doc_ids = segments[0]
    positions = jnp.arange(token_count)

    def one_block(totals, block_index):
        row_start = block_index * block_rows
        query_block = lax.dynamic_slice_in_dim(query_shaped, row_start, block_rows, 0)
        grad_block = lax.dynamic_slice_in_dim(grad_shaped, row_start, block_rows, 0)
        row_ids = lax.dynamic_slice_in_dim(doc_ids, row_start, block_rows, 0)
        row_pos = row_start + jnp.arange(block_rows)
        allowed = (positions[None, :] <= row_pos[:, None]) & (row_ids[:, None] == doc_ids[None, :])
        context_rows, grad_query, gradient_of_key, gradient_of_value = attend(
            query_block, key_shaped, value_shaped, grad_block, allowed
        )
        return (
            (totals[0] + gradient_of_key, totals[1] + gradient_of_value),
            (context_rows, grad_query),
        )

    zero_kv = jnp.zeros((token_count, kv_heads, HEAD_SIZE), jnp.float32)
    (key_total, value_total), (contexts, grad_queries) = lax.scan(
        one_block, (zero_kv, zero_kv), jnp.arange(token_count // block_rows)
    )
    context_rows = contexts.reshape(token_count, query_width)
    query_gradient = grad_queries.reshape(token_count, query_width)
    key_gradient = key_total.reshape(token_count, kv_width).astype(jnp.bfloat16)
    value_gradient = value_total.reshape(token_count, kv_width).astype(jnp.bfloat16)
    context_portion = jnp.einsum(
        "yp,up->yu", context_rows, adapter_down[0], preferred_element_type=jnp.float32
    )
    rank_context = lax.psum(context_portion.astype(jnp.bfloat16), "fsdp").astype(jnp.float32)
    gradient_scale = adapter_scale / math.sqrt(token_count)
    down_map_gradient = gradient_scale * jnp.dot(
        rank_gradient.T, context_rows.astype(jnp.float32), precision=lax.Precision.HIGHEST
    )
    up_map_gradient = gradient_scale * jnp.dot(
        rank_context.T, local_columns.astype(jnp.float32), precision=lax.Precision.HIGHEST
    )
    return (
        query_gradient[None],
        key_gradient[None],
        value_gradient[None],
        down_map_gradient[None],
        up_map_gradient[None],
    )


def solution(mesh):
    placed = (
        P("pipe", "fsdp", None),
        P("pipe", "fsdp", None),
        P("pipe", None, "fsdp"),
        P("pipe", None, "fsdp"),
        P("pipe", None, "fsdp"),
        P("pipe", None, "fsdp"),
        P("pipe", None, "fsdp"),
        P("pipe", None),
    )
    return jax.shard_map(
        per_device,
        mesh=mesh,
        in_specs=placed,
        out_specs=(
            P("pipe", None, "fsdp"),
            P("pipe", None, "fsdp"),
            P("pipe", None, "fsdp"),
            P("pipe", None, "fsdp"),
            P("pipe", None, "fsdp"),
        ),
        check_vma=False,
    )
```

profile of v0, /device:TPU:0, one launch (start us, length us, event | category | flops | bytes accessed | tf_op | source)
XLA Modules:
  0.0 717.0 jit_solution(2849481746487005264)
XLA Ops:
  7.2 0.7 all-gather.3.cloned.1.call-update
  7.9 222.6 %all-gather.3.cloned.1.call-done = bf16[1,768,8192]{2,1,0:T(8,128)(2,1)} async-done(((bf16[1,192,8192]{2,1,0:T(8,128)(2,1)}), bf16[1,768,8192]{2,1,0:T(8,128)(2,1)}) %all-gather.3.cloned.1.call-update) | async-done | bytes 12582928 | tf_op jit(solution)/shard_map/all_gather | solution.py:89
  230.5 2.0 collective-permute-start.3
  232.6 1.9 copy.22
  234.5 1.9 copy.23
  236.4 3.2 copy.21
  239.6 4.2 pad_maximum_fusion
  243.9 11.4 %collective-permute-done = bf16[768,2560]{0,1:T(8,128)(2,1)S(1)} collective-permute-done((bf16[768,2560]{0,1:T(8,128)(2,1)S(1)}, bf16[768,2560]{0,1:T(8,128)(2,1)S(1)}, u32[]{:S(2)}, u32[]{:S(2)}) %collective-permute-start) | collective-permute-done | bytes 3932192 | tf_op jit(solution)/shard_map/ppermute | solution.py:21
  255.3 1.5 collective-permute-start.1
  256.8 196.4 %collective-permute-done.1 = bf16[768,2560]{0,1:T(8,128)(2,1)} collective-permute-done((bf16[768,2560]{0,1:T(8,128)(2,1)S(1)}, bf16[768,2560]{0,1:T(8,128)(2,1)}, u32[]{:S(2)}, u32[]{:S(2)}) %collective-permute-start.1) | collective-permute-done | bytes 3932192 | tf_op jit(solution)/shard_map/ppermute | solution.py:21
  453.2 1.5 collective-permute-start.2
  454.6 44.5 %collective-permute-done.2 = bf16[768,2560]{0,1:T(8,128)(2,1)} collective-permute-done((bf16[768,2560]{0,1:T(8,128)(2,1)}, bf16[768,2560]{0,1:T(8,128)(2,1)}, u32[]{:S(2)}, u32[]{:S(2)}) %collective-permute-start.2) | collective-permute-done | bytes 3932192 | tf_op jit(solution)/shard_map/ppermute | solution.py:21
  499.2 1.2 fusion.79
  500.8 3.8 slice.12
  504.6 2.8 fusion.52
  507.4 16.5 %psum.14 = f32[768,16]{0,1:T(8,128)S(1)} all-reduce(f32[768,16]{0,1:T(8,128)S(1)} %fusion.52), channel_id=1, replica_groups=mesh['pipe'=8,'fsdp'=4] {'fsdp'}, use_global_device_ids=true, to_apply=%region_0.0 | all-reduce | flops 12288 | bytes 98304 | tf_op jit(solution)/shard_map/psum | solution.py:99
  523.9 4.6 fusion.65
  528.4 35.1 %fusion.61 = bf16[96,8,16,128]{3,1,2,0:T(8,128)(2,1)} fusion(f32[768,2048]{1,0:T(8,128)} %fusion.65, bf16[768,8192]{1,0:T(8,128)(2,1)} %collective-permute-done.3, bf16[1,2048,8192]{2,1,0:T(8,128)(2,1)} %param.11), kind=kOutput, calls=%fused_computation.61 | convolution fusion | flops 25774522368 | bytes 55574528 | tf_op jit(solution)/shard_map/td,qd->tq/dot_general | solution.py:100
  563.5 4.6 copy.46
  568.2 98.8 %while.17 = (s32[]{:T(128)}, f32[768,2,128]{0,2,1:T(8,128)}, f32[768,2,128]{0,2,1:T(8,128)S(1)}, bf16[3,256,2,8,128]{4,3,2,1,0:T(8,128)(2,1)}, bf16[3,256,2,8,12...) while((s32[]{:T(128)}, f32[768,2,128]{0,2,1:T(8,128)}, ...), condition=%wide.region_5.6_spmd.clone, body=%wide.region_1.5_spmd.clone.sunk | while | flops 4868535296 | bytes 139426192 | solution.py:133
  568.2 0.6 dynamic_slice.52
  569.8 1.4 constant_dynamic-slice_fusion.2
  571.2 10.2 %fusion.123 = (f32[2,8,256]{2,1,0:T(8,128)S(1)}, f32[2,8,256,768]{3,2,1,0:T(8,128)}) fusion(pred[256,768]{1,0:T(8,128)(4,1)S(1)} %fusion.122, bf16[768,2,8,128]{0,3,2,1:T(8,128)(2,1)} %get-tuple-element.293, s32[]{:T(128)S(6)} %select_n.34, bf16[768,2,128]{2,0,1:T(8,128)(2,1)S(1)} %get-tuple-element.296), kind=kOutput, calls=%fused_computation.69.clone.1 | convolution fusion | flops 817890048 | bytes 14237700 | tf_op jit(solution)/shard_map/while/body/eval_jaxpr/sub | solution.py:38
  581.4 5.3 fusion.124
  586.7 1.4 fusion.128
  588.2 1.8 fusion.125
  590.0 0.7 multiply_reduce_fusion.2
  590.7 0.9 slice-done.2
  591.6 2.6 fusion.126
  594.2 2.4 fusion.127
  596.6 1.8 fusion.129
  598.4 2.7 copy_dynamic-update-slice_fusion.3
  601.1 0.6 dynamic_slice.52
  602.7 1.4 constant_dynamic-slice_fusion.2
  604.1 10.2 %fusion.123 = (f32[2,8,256]{2,1,0:T(8,128)S(1)}, f32[2,8,256,768]{3,2,1,0:T(8,128)}) fusion(pred[256,768]{1,0:T(8,128)(4,1)S(1)} %fusion.122, bf16[768,2,8,128]{0,3,2,1:T(8,128)(2,1)} %get-tuple-element.293, s32[]{:T(128)S(6)} %select_n.34, bf16[768,2,128]{2,0,1:T(8,128)(2,1)S(1)} %get-tuple-element.296), kind=kOutput, calls=%fused_computation.69.clone.1 | convolution fusion | flops 817890048 | bytes 14237700 | tf_op jit(solution)/shard_map/while/body/eval_jaxpr/sub | solution.py:38
  614.3 5.3 fusion.124
  619.6 1.4 fusion.128
  621.1 1.8 fusion.125
  622.9 0.7 multiply_reduce_fusion.2
  623.6 0.9 slice-done.2
  624.5 2.6 fusion.126
  627.1 2.4 fusion.127
  629.5 1.8 fusion.129
  631.3 2.7 copy_dynamic-update-slice_fusion.3
  634.0 0.6 dynamic_slice.52
  635.6 1.4 constant_dynamic-slice_fusion.2
  637.0 10.3 %fusion.123 = (f32[2,8,256]{2,1,0:T(8,128)S(1)}, f32[2,8,256,768]{3,2,1,0:T(8,128)}) fusion(pred[256,768]{1,0:T(8,128)(4,1)S(1)} %fusion.122, bf16[768,2,8,128]{0,3,2,1:T(8,128)(2,1)} %get-tuple-element.293, s32[]{:T(128)S(6)} %select_n.34, bf16[768,2,128]{2,0,1:T(8,128)(2,1)S(1)} %get-tuple-element.296), kind=kOutput, calls=%fused_computation.69.clone.1 | convolution fusion | flops 817890048 | bytes 14237700 | tf_op jit(solution)/shard_map/while/body/eval_jaxpr/sub | solution.py:38
  647.2 5.3 fusion.124
  652.6 1.5 fusion.128
  654.0 1.8 fusion.125
  655.8 0.7 multiply_reduce_fusion.2
  656.5 0.9 slice-done.2
  657.4 2.6 fusion.126
  660.0 2.4 fusion.127
  662.5 1.8 fusion.129
  664.3 2.7 copy_dynamic-update-slice_fusion.3
  667.0 5.8 reshape.119
  672.7 3.9 fusion.60
  676.6 2.9 convolution_convert_fusion.1
  679.6 5.8 broadcast_in_dim_reshape.3
  685.4 0.9 copy.38
  686.3 0.9 copy.39
  687.3 19.8 %psum.15 = bf16[768,16]{1,0:T(8,128)(2,1)S(1)} all-reduce(bf16[768,16]{1,0:T(8,128)(2,1)S(1)} %convolution_convert_fusion.1), channel_id=1, replica_groups=mesh['pipe'=8,'fsdp'=4] {'fsdp'}, use_global_device_ids=true, to_apply=%region_6.7 | all-reduce | flops 12288 | bytes 49152 | tf_op jit(solution)/shard_map/psum | solution.py:143
  707.1 3.1 fusion.57
  (67 shorter events, 1.7 us)
Async XLA Ops:
  7.2 516.7 %copy-start = (bf16[1,16,2048]{2,1,0:T(8,128)(2,1)S(1)}, bf16[1,16,2048]{2,1,0:T(8,128)(2,1)}, u32[]{:S(2)}) copy-start(bf16[1,16,2048]{2,1,0:T(8,128)(2,1)} %param.12) | copy-start | bytes 196612
  7.2 223.3 %all-gather.3.cloned.1.call-start = ((), (), s32[]{:S(2)}) async-start(), calls=%async_computation | async-start | bytes 15728640 | tf_op jit(solution)/shard_map/all_gather | solution.py:89
  230.5 274.1 %collective-permute-start.3 = (bf16[768,8192]{1,0:T(8,128)(2,1)}, bf16[768,8192]{1,0:T(8,128)(2,1)}, u32[]{:S(2)}, u32[]{:S(2)}) collective-permute-start(bf16[768,8192]{1,0:T(8,128)(2,1)} %bitcast.163), channel_id=1, source_target_pairs={{4,0},{8,4},{12,8},{16,12},{20,16},{24,20},{28,24},{0,28},{5,1},{9... | collective-permute-start | bytes 37748744 | tf_op jit(solution)/shard_map/ppermute | solution.py:27
  236.4 218.2 %copy-start.6 = (s32[1,768]{1,0:T(1,128)S(1)}, s32[1,768]{1,0:T(1,128)}, u32[]{:S(2)}) copy-start(s32[1,768]{1,0:T(1,128)} %param.17) | copy-start | bytes 9220
  243.8 260.8 %copy-start.7 = (bf16[1,16,2048]{2,1,0:T(8,128)(2,1)S(1)}, bf16[1,16,2048]{2,1,0:T(8,128)(2,1)}, u32[]{:S(2)}) copy-start(bf16[1,16,2048]{2,1,0:T(8,128)(2,1)} %param.13) | copy-start | bytes 196612
  243.8 11.5 %collective-permute-start = (bf16[768,2560]{0,1:T(8,128)(2,1)S(1)}, bf16[768,2560]{0,1:T(8,128)(2,1)S(1)}, u32[]{:S(2)}, u32[]{:S(2)}) collective-permute-start(bf16[768,2560]{0,1:T(8,128)(2,1)S(1)} %pad_maximum_fusion), channel_id=1, source_target_pairs={{0,4},{4,0},{8,12},{12,8},{16,20},{20,16},{24,28},{28,24},{1,5},{5... | collective-permute-start | bytes 11796488 | tf_op jit(solution)/shard_map/ppermute | solution.py:21
  255.3 197.8 %collective-permute-start.1 = (bf16[768,2560]{0,1:T(8,128)(2,1)S(1)}, bf16[768,2560]{0,1:T(8,128)(2,1)}, u32[]{:S(2)}, u32[]{:S(2)}) collective-permute-start(bf16[768,2560]{0,1:T(8,128)(2,1)S(1)} %collective-permute-done), channel_id=1, source_target_pairs={{0,8},{8,0},{4,12},{12,4},{16,24},{24,16},{20,28},{28,20},{1,9},{9... | collective-permute-start | bytes 11796488 | tf_op jit(solution)/shard_map/ppermute | solution.py:21
  453.2 46.0 %collective-permute-start.2 = (bf16[768,2560]{0,1:T(8,128)(2,1)}, bf16[768,2560]{0,1:T(8,128)(2,1)}, u32[]{:S(2)}, u32[]{:S(2)}) collective-permute-start(bf16[768,2560]{0,1:T(8,128)(2,1)} %collective-permute-done.1), channel_id=1, source_target_pairs={{0,16},{16,0},{4,20},{20,4},{8,24},{24,8},{12,28},{28,12},{1,17},{... | collective-permute-start | bytes 11796488 | tf_op jit(solution)/shard_map/ppermute | solution.py:21
  523.9 39.7 %copy-start.4 = (f32[768,16]{0,1:T(8,128)}, f32[768,16]{0,1:T(8,128)S(1)}, u32[]{:S(2)}) copy-start(f32[768,16]{0,1:T(8,128)S(1)} %psum.14) | copy-start | bytes 147460
  586.7 4.0 slice-start
  586.7 4.0 slice-start.1
  588.1 3.4 slice-start.2
  591.6 2.6 copy-start.1
  596.6 4.5 copy-start.2
  619.6 4.0 slice-start
  619.6 4.0 slice-start.1
  621.0 3.4 slice-start.2
  624.5 2.6 copy-start.1
  629.5 4.5 copy-start.2
  652.5 4.0 slice-start
  652.5 4.0 slice-start.1
  654.0 3.4 slice-start.2
  657.4 2.6 copy-start.1
  662.5 4.5 copy-start.2
  667.0 5.8 copy-start.5
  676.6 8.7 %copy-start.3 = (f32[768,2,128]{0,2,1:T(8,128)S(1)}, f32[768,2,128]{0,2,1:T(8,128)}, u32[]{:S(2)}) copy-start(f32[768,2,128]{0,2,1:T(8,128)} %get-tuple-element.76) | copy-start | bytes 2359300
Sparse Core Ops, SparseCore 0:
  9.6 220.8 all-gather.2
where the time goes:
time: 718 us; the launch traced here: 717 us
  waiting for transfers between devices  476 us (66%)
  matrix products  113 us (16%)
  local copies, waits for them, and re-layouts  47.5 us (7%)
  blocking collectives  36.3 us (5%)
  other arithmetic  23 us (3%)
  between operations  14.1 us (2%)
    ppermute x3, waiting for transfers between devices, swapped(): return lax.ppermute(block, axis, route)  252 us
    all_gather x1, waiting for transfers between devices, per_device(): lax.all_gather(handoff_gradient[0], 'fsdp', axis=0, tiled=True)  223 us
    dot_general x1, matrix products, per_device(): jnp.einsum('td,qd->tq', incoming_gradient, output_weight[0], preferred_el...  35.1 us
    sub x3, matrix products, attend(): expanded = jnp.exp(scores - row_max)  30.6 us
    psum x1, blocking collectives, per_device(): lax.psum(context_portion.astype(jnp.bfloat16), 'fsdp').astype(jnp.float32)  19.8 us
    psum x1, blocking collectives, per_device(): rank_gradient = lax.psum(rank_portion, 'fsdp')  16.5 us
    convert_element_type x3, other arithmetic, attend(): probs_low = attn_probs.astype(jnp.bfloat16)  15.9 us
  transfers between devices with their start and end apart: 5, of which 4 were waited for; matrix products, arithmetic and copies ran while one was open for 2% of the time, Pallas kernels for 0%

commit v1 on v0

v1 whole, which is shorter than its diff:
```python
import functools
import math

import jax
import jax.numpy as jnp
from jax import lax
from jax.experimental import pallas as pl
from jax.experimental.pallas import tpu as pltpu
from jax.sharding import PartitionSpec as P

HEAD_SIZE = 128
DOC_REACH = 384
MASKED = -1e30
LOG2E = math.log2(math.e)
VMEM_BYTES = 44 * 2**20

adapter_scale = 2.0


def dot_nt(a, b):
    return lax.dot_general(a, b, (((1,), (1,)), ((), ())), preferred_element_type=jnp.float32)


def dot_nn(a, b):
    return lax.dot_general(a, b, (((1,), (0,)), ((), ())), preferred_element_type=jnp.float32)


def dot_tn(a, b):
    return lax.dot_general(a, b, (((0,), (0,)), ((), ())), preferred_element_type=jnp.float32)


def three_parts(a):
    high = a.astype(jnp.bfloat16)
    rest = a - high.astype(jnp.float32)
    middle = rest.astype(jnp.bfloat16)
    low = (rest - middle.astype(jnp.float32)).astype(jnp.bfloat16)
    return jnp.concatenate([high, middle, low], axis=0)


def folded(a):
    rows = a.shape[0] // 3
    return a[:rows] + a[rows : 2 * rows] + a[2 * rows :]


def stacked_heads(a):
    count = a.shape[1] // HEAD_SIZE
    return jnp.concatenate(
        [a[:, h * HEAD_SIZE : (h + 1) * HEAD_SIZE] for h in range(count)], axis=0
    )


def mask_bias(key_start, key_ids, query_pos, query_ids, shape):
    key_pos = key_start + lax.broadcasted_iota(jnp.int32, shape, 0)
    allowed = (key_pos <= query_pos) & (key_ids == query_ids)
    return jnp.where(allowed, 0.0, MASKED)


def forward_kernel(
    first_block, heads, total, q_ref, k_ref, v_ref, ids_ref, row_info_ref, down_ref, *rest
):
    ctx_ref, lse_ref, rank_ref, q_out_ref, bias_ref = rest[-5:]
    block, step = pl.program_id(0), pl.program_id(1)
    rows = q_ref.shape[0]
    window = bias_ref.shape[0]
    row_start = (first_block + block) * rows
    start = jnp.clip(row_start - DOC_REACH, 0, total - window)
    start = pl.multiple_of(start, 16)

    @pl.when(step == 0)
    def _():
        bias_ref[...] = mask_bias(
            start,
            ids_ref[pl.ds(start, window), :],
            row_info_ref[0, 0:1, :],
            row_info_ref[0, 1:2, :],
            bias_ref.shape,
        )
        rank_ref[...] = jnp.zeros_like(rank_ref)

    queries = q_ref[...]
    q_out_ref[...] = queries
    stacked = stacked_heads(queries)
    keys = k_ref[pl.ds(start, window), :]
    values = v_ref[pl.ds(start, window), :]
    scores = dot_nt(keys, stacked) * (LOG2E / math.sqrt(HEAD_SIZE)) + bias_ref[...]
    top = jnp.max(scores, axis=0, keepdims=True)
    expanded = jnp.exp2(scores - top)
    total_weight = jnp.sum(expanded, axis=0, keepdims=True)
    probs = (expanded * (1.0 / total_weight)).astype(jnp.bfloat16)
    lse_ref[0, 0] = top + jnp.log(total_weight) * LOG2E
    context_t = dot_tn(values, probs)
    context = context_t.T.astype(jnp.bfloat16)
    for h in range(heads):
        part = context[h * rows : (h + 1) * rows]
        ctx_ref[:, h * HEAD_SIZE : (h + 1) * HEAD_SIZE] = part
        rank_ref[0] += dot_nt(down_ref[:, h * HEAD_SIZE : (h + 1) * HEAD_SIZE], part)


def backward_kernel(spec, scalars_ref, *refs):
    candidates, pieces, heads, group, total, first, final, with_up = spec
    refs = list(refs)

    def take(count):
        taken = refs[:count]
        del refs[:count]
        return taken

    sources = [take(pieces) for _ in range(candidates)]
    (w_ref, up_ref, down_ref, q_ref, ctx_ref, k_ref, v_ref, ids_ref, row_info_ref, lse_ref) = take(10)
    rank_ctx_ref = take(1)[0] if with_up else None
    if not first:
        _, dk_in, dv_in, dm_in = take(4)
    um_in = take(1)[0] if with_up else None
    dq_ref, dk_ref, dv_ref, dm_ref = take(4)
    um_ref = take(1)[0] if with_up else None
    x_ref, rank_ref, bias_ref, dk_sum, dv_sum, sems = take(6)
    if with_up:
        ctx_rank_ref = take(1)[0]

    step = pl.program_id(0)
    rows, width = x_ref.shape
    window = bias_ref.shape[0]
    tile = heads * HEAD_SIZE
    start = pl.multiple_of(scalars_ref[2], 16)
    gradient_scale = adapter_scale / math.sqrt(total)
    inv_scale = 1.0 / math.sqrt(HEAD_SIZE)

    @pl.when(step == 0)
    def _():
        for c, parts in enumerate(sources):

            @pl.when(scalars_ref[0] == c)
            def _(parts=parts):
                copies = []
                depth = rows // pieces
                for p, part in enumerate(parts):
                    copies.append(
                        pltpu.make_async_copy(
                            part, x_ref.at[pl.ds(p * depth, depth), :], sems.at[p]
                        )
                    )
                for copy in copies:
                    copy.start()
                for copy in copies:
                    copy.wait()

        bias_ref[...] = mask_bias(
            start,
            ids_ref[pl.ds(start, window), :],
            row_info_ref[0, 0:1, :],
            row_info_ref[0, 1:2, :],
            bias_ref.shape,
        )
        rank_ref[...] = three_parts(dot_nt(up_ref[...], x_ref[...]))
        if with_up:
            ctx_rank_ref[...] = three_parts(rank_ctx_ref[0])

    steps_per_kv = group // heads

    chunk = min(2048, width)

    def accumulate(i, acc):
        at = pl.multiple_of(i * chunk, chunk)
        return acc + dot_nt(x_ref[:, pl.ds(at, chunk)], w_ref[:, pl.ds(at, chunk)])

    down = down_ref[...]
    acc = adapter_scale * dot_tn(rank_ref[...], jnp.concatenate([down, down, down], axis=0))
    acc = lax.fori_loop(0, width // chunk, accumulate, acc)
    grad = acc.astype(jnp.bfloat16)

    queries = stacked_heads(q_ref[...])
    context = ctx_ref[...]
    grads = stacked_heads(grad)
    keys = k_ref[pl.ds(start, window), :]
    values = v_ref[pl.ds(start, window), :]
    delta = jnp.sum(
        (grads.astype(jnp.float32) * stacked_heads(context).astype(jnp.float32)).T,
        axis=0,
        keepdims=True,
    )
    scores = dot_nt(keys, queries) * (LOG2E * inv_scale) + bias_ref[...]
    probs = jnp.exp2(scores - lse_ref[0, 0])
    grad_probs = dot_nt(values, grads)
    grad_scores = (probs * (grad_probs - delta)).astype(jnp.bfloat16)
    probs_low = probs.astype(jnp.bfloat16)

    fresh = lax.rem(step, steps_per_kv) == 0

    @pl.when(fresh)
    def _():
        if first:
            dk_sum[...] = jnp.zeros_like(dk_sum)
            dv_sum[...] = jnp.zeros_like(dv_sum)
        else:
            dk_sum[...] = dk_in[...]
            dv_sum[...] = dv_in[...]

    dk_sum[pl.ds(start, window), :] += dot_nn(grad_scores, queries) * inv_scale
    dv_sum[pl.ds(start, window), :] += dot_nn(probs_low, grads)

    @pl.when(lax.rem(step, steps_per_kv) == steps_per_kv - 1)
    def _():
        dk_ref[...] = dk_sum[...].astype(dk_ref.dtype)
        dv_ref[...] = dv_sum[...].astype(dv_ref.dtype)

    grad_q = (dot_tn(keys, grad_scores) * inv_scale).T.astype(jnp.bfloat16)
    for h in range(heads):
        dq_ref[:, h * HEAD_SIZE : (h + 1) * HEAD_SIZE] = grad_q[h * rows : (h + 1) * rows]

    down_part = gradient_scale * folded(dot_nn(rank_ref[...], context))
    dm_ref[...] = down_part if first else dm_in[...] + down_part
    if with_up:
        at = pl.multiple_of(scalars_ref[3] + step * tile, tile)
        um_ref[...] = um_in[...] + gradient_scale * folded(
            dot_nn(ctx_rank_ref[...], x_ref[:, pl.ds(at, tile)])
        )


def per_device(
    handoff_gradient,
    output_weight,
    adapter_down,
    adapter_up,
    stored_queries,
    stored_keys,
    stored_values,
    segments,
):
    pipe_count = lax.axis_size("pipe")
    line = lax.axis_size("fsdp")
    member = lax.axis_index("fsdp")
    shard = handoff_gradient.shape[1]
    total = shard * line
    model_width = handoff_gradient.shape[2]
    query_width = stored_queries.shape[2]
    kv_width = stored_keys.shape[2]
    rank = adapter_down.shape[1]
    query_heads = query_width // HEAD_SIZE
    kv_heads = kv_width // HEAD_SIZE
    group = query_heads // kv_heads
    local_width = adapter_up.shape[2]
    bf16, f32 = jnp.bfloat16, jnp.float32

    split = 2
    depth = shard // split
    from_next = [((i + 1) % pipe_count, i) for i in range(pipe_count)]
    mirrored = [(i, pipe_count - 1 - i) for i in range(pipe_count)]
    own = [
        lax.ppermute(handoff_gradient[0, p * depth : (p + 1) * depth], "pipe", from_next)
        for p in range(split)
    ]
    rising, falling = [own], [own]
    for k in range(1, line):
        up_pairs = [(i, i + 1) for i in range(k - 1, line - 1)]
        down_pairs = [(i + 1, i) for i in range(line - k)]
        up_now, down_now = [], []
        for p in range(split):
            up_now.append(lax.ppermute(rising[-1][p], "fsdp", up_pairs))
            down_now.append(lax.ppermute(falling[-1][p], "fsdp", down_pairs))
        rising.append(up_now)
        falling.append(down_now)

    up_full = lax.all_gather(adapter_up[0], "fsdp", axis=1, tiled=True)
    key_local = lax.ppermute(stored_keys[0], "pipe", mirrored)
    value_local = lax.ppermute(stored_values[0], "pipe", mirrored)
    query_half = [
        lax.ppermute(stored_queries[0, i * (total // 2) : (i + 1) * (total // 2)], "pipe", mirrored)
        for i in range(2)
    ]

    ids_column = segments[0][:, None]
    rows_f = total // 4
    heads_f = 2
    steps_f = query_heads // heads_f
    lanes_f = heads_f * rows_f
    window_f = min(total, rows_f + DOC_REACH)
    down = adapter_down[0]

    def row_info(rows, heads):
        pos = jnp.arange(total, dtype=jnp.int32).reshape(total // rows, 1, rows)
        ids = segments[0].reshape(total // rows, 1, rows)
        both = jnp.concatenate([pos, ids], axis=1)
        return jnp.tile(both, (1, 1, heads))

    forward_out = None
    info_f = row_info(rows_f, heads_f)
    for i in range(2):
        base = 2 * i
        in_specs = [
            pl.BlockSpec((rows_f, heads_f * HEAD_SIZE), lambda b, n: (b, n)),
            pl.BlockSpec((total, HEAD_SIZE), lambda b, n: (0, n * heads_f // group)),
            pl.BlockSpec((total, HEAD_SIZE), lambda b, n: (0, n * heads_f // group)),
            pl.BlockSpec((total, 1), lambda b, n: (0, 0)),
            pl.BlockSpec((1, 2, lanes_f), lambda b, n, base=base: (base + b, 0, 0)),
            pl.BlockSpec((rank, heads_f * HEAD_SIZE), lambda b, n: (0, n)),
        ]
        operands = [query_half[i], key_local, value_local, ids_column, info_f, down]
        aliases = {}
        if forward_out is not None:
            for j, a in enumerate(forward_out):
                aliases[len(operands)] = j
                operands.append(a)
                in_specs.append(pl.BlockSpec(memory_space=pl.ANY))
        forward_out = pl.pallas_call(
            functools.partial(forward_kernel, base, heads_f, total),
            grid=(2, steps_f),
            in_specs=in_specs,
            out_specs=[
                pl.BlockSpec((rows_f, heads_f * HEAD_SIZE), lambda b, n, base=base: (base + b, n)),
                pl.BlockSpec((1, 1, 1, lanes_f), lambda b, n, base=base: (base + b, n, 0, 0)),
                pl.BlockSpec((1, rank, rows_f), lambda b, n, base=base: (base + b, 0, 0)),
                pl.BlockSpec((rows_f, heads_f * HEAD_SIZE), lambda b, n, base=base: (base + b, n)),
            ],
            out_shape=[
                jax.ShapeDtypeStruct((total, query_width), bf16),
                jax.ShapeDtypeStruct((4, steps_f, 1, lanes_f), f32),
                jax.ShapeDtypeStruct((4, rank, rows_f), f32),
                jax.ShapeDtypeStruct((total, query_width), bf16),
            ],
            scratch_shapes=[pltpu.VMEM((window_f, lanes_f), f32)],
            input_output_aliases=aliases,
            compiler_params=pltpu.CompilerParams(
                dimension_semantics=("arbitrary", "arbitrary"), vmem_limit_bytes=VMEM_BYTES
            ),
            cost_estimate=pl.CostEstimate(
                flops=2 * 2 * total // 2 * window_f * query_width,
                bytes_accessed=4 * total * query_width,
                transcendentals=total // 2 * window_f * query_heads,
            ),
            name=f"forward_{i}",
        )(*operands)
    context, lse, rank_portion, query = forward_out
    rank_context = jnp.sum(lax.all_gather(rank_portion, "fsdp", axis=0), axis=0)

    def by_rows(rows, heads):
        normal = (
            lse.reshape(4, query_heads, rows_f // rows, rows)
            .transpose(0, 2, 1, 3)
            .reshape(total // rows, query_heads // heads, 1, heads * rows)
        )
        ranks = (
            rank_context.reshape(4, rank, rows_f // rows, rows)
            .transpose(0, 2, 1, 3)
            .reshape(total // rows, rank, rows)
        )
        return normal, ranks, row_info(rows, heads)

    tables = {}

    def backward(sources, choice, row_block, rows, state, up_map, final, name):
        first = state is None
        with_up = up_map is not None
        heads = max(1, min(group, 4, 384 // rows))
        if (rows, heads) not in tables:
            tables[rows, heads] = by_rows(rows, heads)
        normal, ranks, info = tables[rows, heads]
        tile = heads * HEAD_SIZE
        steps = query_heads // heads
        lanes = heads * rows
        window = min(total, rows + DOC_REACH)
        pieces = len(sources[0])
        start = jnp.clip(row_block * rows - DOC_REACH, 0, total - window)
        scalars = jnp.stack([choice, row_block, start, member * local_width]).astype(jnp.int32)
        anywhere = pl.BlockSpec(memory_space=pl.ANY)
        per_kv = group // heads
        kv_spec = pl.BlockSpec((total, HEAD_SIZE), lambda n, s: (0, n // per_kv))
        row_spec = pl.BlockSpec((rows, tile), lambda n, s: (s[1], n))
        rank_spec = pl.BlockSpec((rank, tile), lambda n, s: (0, n))
        operands = [part for parts in sources for part in parts]
        in_specs = [anywhere] * len(operands)
        operands += [
            output_weight[0],
            up_full,
            down,
            query,
            context,
            key_local,
            value_local,
            ids_column,
            info,
            normal,
        ]
        in_specs += [
            pl.BlockSpec((tile, model_width), lambda n, s: (n, 0)),
            pl.BlockSpec((rank, model_width), lambda n, s: (0, 0)),
            rank_spec,
            row_spec,
            row_spec,
            kv_spec,
            kv_spec,
            pl.BlockSpec((total, 1), lambda n, s: (0, 0)),
            pl.BlockSpec((1, 2, lanes), lambda n, s: (s[1], 0, 0)),
            pl.BlockSpec((1, 1, 1, lanes), lambda n, s: (s[1], n, 0, 0)),
        ]
        if with_up:
            operands.append(ranks)
            in_specs.append(pl.BlockSpec((1, rank, rows), lambda n, s: (s[1], 0, 0)))
        aliases = {}
        if not first:
            aliases[1 + len(operands)] = 0
            if not final:
                aliases[2 + len(operands)] = 1
                aliases[3 + len(operands)] = 2
            operands += list(state)
            in_specs += [anywhere, kv_spec, kv_spec, rank_spec]
        if with_up:
            operands.append(up_map)
            in_specs.append(rank_spec)
        kv_type = bf16 if final else f32
        out_shape = [
            jax.ShapeDtypeStruct((total, query_width), bf16),
            jax.ShapeDtypeStruct((total, kv_width), kv_type),
            jax.ShapeDtypeStruct((total, kv_width), kv_type),
            jax.ShapeDtypeStruct((rank, query_width), f32),
        ]
        out_specs = [row_spec, kv_spec, kv_spec, rank_spec]
        scratch = [
            pltpu.VMEM((rows, model_width), bf16),
            pltpu.VMEM((3 * rank, rows), bf16),
            pltpu.VMEM((window, lanes), f32),
            pltpu.VMEM((total, HEAD_SIZE), f32),
            pltpu.VMEM((total, HEAD_SIZE), f32),
            pltpu.SemaphoreType.DMA((pieces,)),
        ]
        if with_up:
            out_shape.append(jax.ShapeDtypeStruct((rank, query_width), f32))
            out_specs.append(rank_spec)
            scratch.append(pltpu.VMEM((3 * rank, rows), bf16))
        out = pl.pallas_call(
            functools.partial(
                backward_kernel, (len(sources), pieces, heads, group, total, first, final, with_up)
            ),
            grid_spec=pltpu.PrefetchScalarGridSpec(
                num_scalar_prefetch=1,
                grid=(steps,),
                in_specs=in_specs,
                out_specs=out_specs,
                scratch_shapes=scratch,
            ),
            out_shape=out_shape,
            input_output_aliases=aliases,
            compiler_params=pltpu.CompilerParams(
                dimension_semantics=("arbitrary",), vmem_limit_bytes=VMEM_BYTES
            ),
            cost_estimate=pl.CostEstimate(
                flops=2 * rows * model_width * query_width + 10 * rows * window * query_width,
                bytes_accessed=2 * model_width * query_width,
                transcendentals=rows * window * query_heads,
            ),
            name=name,
        )(scalars, *operands)
        return tuple(out[:4]), (out[4] if with_up else None)

    def arrival(device, order):
        found = []
        for k in range(1, line):
            if device >= k:
                found.append((k, True, device - k))
            if device + k < line:
                found.append((k, False, device + k))
        return found[order]

    def table_at(values):
        return jnp.asarray(values, jnp.int32)[member]

    zero = jnp.int32(0)
    state, _ = backward([own], zero, member, shard, None, None, False, "own")
    scale = adapter_scale / math.sqrt(total)

    def chosen(order):
        entries = [arrival(d, order) for d in range(line)]
        kinds = sorted({(k, rises) for k, rises, _ in entries})
        choice = table_at([kinds.index((k, rises)) for k, rises, _ in entries])
        owner = table_at([o for _, _, o in entries])
        sources = [(rising if rises else falling)[k] for k, rises in kinds]
        return sources, choice, owner

    ranks_whole = rank_context.reshape(4, rank, rows_f).transpose(1, 0, 2).reshape(rank, total)

    own_columns = jnp.concatenate(
        [lax.dynamic_slice_in_dim(part, member * local_width, local_width, 1) for part in own], axis=0
    )
    own_ranks = lax.dynamic_slice_in_dim(ranks_whole, member * shard, shard, 1)
    up_map = scale * jnp.dot(own_ranks, own_columns.astype(f32), precision=lax.Precision.HIGHEST)
    for order in range(line - 1):
        sources, choice, owner = chosen(order)
        if order < line - 2:
            state, up_map = backward(
                sources, choice, owner, shard, state, up_map, False, f"arrived_{order}"
            )
        else:
            for p in range(split):
                state, up_map = backward(
                    [[s[p]] for s in sources],
                    choice,
                    owner * split + p,
                    depth,
                    state,
                    up_map,
                    p == split - 1,
                    f"arrived_{order}_{p}",
                )
    query_gradient, key_gradient, value_gradient, down_map = state
    return (
        query_gradient[None],
        key_gradient[None],
        value_gradient[None],
        down_map[None],
        up_map[None],
    )


def solution(mesh):
    placed = (
        P("pipe", "fsdp", None),
        P("pipe", "fsdp", None),
        P("pipe", None, "fsdp"),
        P("pipe", None, "fsdp"),
        P("pipe", None, "fsdp"),
        P("pipe", None, "fsdp"),
        P("pipe", None, "fsdp"),
        P("pipe", None),
    )
    return jax.shard_map(
        per_device,
        mesh=mesh,
        in_specs=placed,
        out_specs=(
            P("pipe", None, "fsdp"),
            P("pipe", None, "fsdp"),
            P("pipe", None, "fsdp"),
            P("pipe", None, "fsdp"),
            P("pipe", None, "fsdp"),
        ),
        check_vma=False,
    )
```

time: 718 us -> 448 us (0.62)
  the two profiles are of different devices: /device:TPU:0 before, /device:TPU:16 now
where the time goes in v1:
time: 448 us; the launch traced here: 447 us
  Pallas kernels  194 us (43%)
  waiting for transfers between devices  87.5 us (20%)
  blocking collectives  78.9 us (18%)
  starting transfers between devices  39.4 us (9%)
  local copies, waits for them, and re-layouts  31.7 us (7%)
  other arithmetic  10.3 us (2%)
    pallas_call x5, Pallas kernels, backward(): pl.pallas_call(functools.partial(backward_kernel, (len(sources), pieces,...  158 us
    ppermute x1, waiting for transfers between devices, per_device(): key_local = lax.ppermute(stored_keys[0], 'pipe', mirrored)  76.1 us
    all_gather x1, blocking collectives, per_device(): up_full = lax.all_gather(adapter_up[0], 'fsdp', axis=1, tiled=True)  63.8 us
    pallas_call x2, Pallas kernels, per_device(): pl.pallas_call(functools.partial(forward_kernel, base, heads_f, total), g...  36 us
    ppermute x6, starting transfers between devices, per_device(): up_now.append(lax.ppermute(rising[-1][p], 'fsdp', up_pairs))  16.6 us
    all_gather x1, blocking collectives, per_device(): rank_context = jnp.sum(lax.all_gather(rank_portion, 'fsdp', axis=0), axis=0)  15 us
    ppermute x6, starting transfers between devices, per_device(): down_now.append(lax.ppermute(falling[-1][p], 'fsdp', down_pairs))  14.6 us
    unnamed x68, local copies, waits for them, and re-layouts  11.8 us
  transfers between devices with their start and end apart: 18, of which 2 were waited for; matrix products, arithmetic and copies ran while one was open for 7% of the time, Pallas kernels for 38%

profile of v1, /device:TPU:16, one launch (start us, length us, event | category | flops | bytes accessed | tf_op | source)
XLA Modules:
  0.0 447.0 jit_solution(4304383228130292280)
XLA Ops:
  0.6 2.3 slice_bitcast_fusion
  3.0 1.9 collective-permute-start
  5.0 0.7 collective-permute-start.11
  5.7 1.5 slice_bitcast_fusion.1
  7.3 2.6 collective-permute-start.8
  10.0 76.1 %collective-permute-done.8.k_ref.refs_7_.refs_9_.refs_11_ = bf16[768,256]{1,0:T(8,128)(2,1)S(1)} collective-permute-done((bf16[768,256]{1,0:T(8,128)(2,1)S(1)}, bf16[768,256]{1,0:T(8,128)(2,1)S(1)}, u32[]{:S(2)}, u32[]{:S(2)}) %collective-permute-start.8) | collective-permute-done | bytes 393248 | tf_op jit(solution)/shard_map/ppermute | solution.py:264
  86.0 0.7 copy-done.3
  86.8 2.8 collective-permute-start.7
  89.6 2.3 collective-permute-start.12
  92.0 2.4 collective-permute-start.1
  94.4 0.7 copy-done.6
  95.1 4.8 %collective-permute-start.14 = (bf16[96,8192]{1,0:T(8,128)(2,1)}, bf16[96,8192]{1,0:T(8,128)(2,1)}, u32[]{:S(2)}, u32[]{:S(2)}) collective-permute-start(bf16[96,8192]{1,0:T(8,128)(2,1)} %collective-permute-done.11.refs_0_), channel_id=1, source_target_pairs={{0,1},{1,2},{2,3},{4,5},{5,6},{6,7},{8,9},{9,10},{10,11},{12,13},{... | collective-permute-start | bytes 4718600 | tf_op jit(solution)/shard_map/ppermute | solution.py:258
  99.9 1.1 copy-done.21
  101.1 1.9 collective-permute-start.3
  103.5 0.6 dynamic_slice.32
  104.8 0.6 dynamic_slice.31
  105.3 0.6 dynamic_slice.30
  106.6 0.6 dynamic_slice.29
  107.2 0.6 dynamic_slice.28
  109.1 0.6 dynamic_slice.27
  109.8 0.7 tile.11.refs_12_
  110.5 63.8 %all-gather = bf16[1,16,8192]{2,1,0:T(8,128)(2,1)} all-gather(bf16[1,16,2048]{2,1,0:T(8,128)(2,1)S(1)} %copy-done.24), channel_id=2, replica_groups=mesh['pipe'=8,'fsdp'=4] {'fsdp'}, dimensions={2}, use_global_device_ids=true | all-gather | bytes 327680 | tf_op jit(solution)/shard_map/all_gather | solution.py:263
  174.3 1.2 add_add_fusion.1.scalars_ref
  175.5 0.7 add_add_fusion.scalars_ref
  176.2 0.7 add_add_fusion.4.scalars_ref
  176.9 1.8 add_add_fusion.3.scalars_ref
  178.7 1.9 add_add_fusion.2.scalars_ref
  180.6 1.0 copy-done.4
  181.6 1.0 copy-done.7
  182.6 0.8 copy-done.10
  183.4 1.4 copy-done.22
  184.8 17.6 %forward_0.1 = (bf16[768,2048]{1,0:T(8,128)(2,1)S(1)}, f32[4,8,1,384]{3,2,1,0:T(1,128)S(1)}, f32[4,16,192]{2,1,0:T(8,128)S(1)}, bf16[768,2048]{1,0:T(8,128)(2,1)S(1)}) custom-call(bf16[384,2048]{1,0:T(8,128)(2,1)S(1)} %copy-done.22, bf16[768,256]{1,0:T(8,128)(2,1)S(1)} %copy-done.4, bf16[768,256]{1,0:T(8,128)(2,1)S(1)} %copy-done.7, ...), custom_call_target="tpu_custom_call" | custom-call | flops 1811939328 | bytes 6291456 | tf_op jit(solution)/shard_map/forward_0/pallas_call | solution.py:304
  202.4 18.4 %forward_1.1 = (bf16[768,2048]{1,0:T(8,128)(2,1)S(1)}, f32[4,8,1,384]{3,2,1,0:T(1,128)S(1)}, f32[4,16,192]{2,1,0:T(8,128)S(1)}, bf16[768,2048]{1,0:T(8,128)(2,1)S(1)}) custom-call(bf16[384,2048]{1,0:T(8,128)(2,1)} %collective-permute-done.7.q_ref, ...), custom_call_target="tpu_custom_call", output_to_operand_aliasing={{0}: (6, {}), {1}: (7, {}), {2}: (8, {}), {3}: (9, {})} | custom-call | flops 1811939328 | bytes 6291456 | tf_op jit(solution)/shard_map/forward_1/pallas_call | solution.py:304
  220.9 1.6 copy-done.1
  222.5 0.6 copy-done.13
  223.1 15.0 %all-gather.1 = f32[16,16,192]{2,1,0:T(8,128)} all-gather(f32[4,16,192]{2,1,0:T(8,128)S(1)} %get-tuple-element.44), channel_id=3, replica_groups=mesh['pipe'=8,'fsdp'=4] {'fsdp'}, dimensions={0}, use_global_device_ids=true | all-gather | bytes 245760 | tf_op jit(solution)/shard_map/all_gather | solution.py:333
  238.1 1.6 reduce_sum.9.refs_14_.refs_16_
  239.7 5.9 %collective-permute-start.13 = (bf16[96,8192]{1,0:T(8,128)(2,1)}, bf16[96,8192]{1,0:T(8,128)(2,1)}, u32[]{:S(2)}, u32[]{:S(2)}) collective-permute-start(bf16[96,8192]{1,0:T(8,128)(2,1)} %collective-permute-done.12.refs_0_), channel_id=1, source_target_pairs={{1,0},{2,1},{5,4},{6,5},{9,8},{10,9},{13,12},{14,13},{17,16},{18,1... | collective-permute-start | bytes 4718600 | tf_op jit(solution)/shard_map/ppermute | solution.py:259
  245.7 2.4 collective-permute-start.2
  248.1 1.9 collective-permute-start.15
  250.0 1.9 collective-permute-start.4
  252.0 1.6 fusion.6
  253.6 1.5 copy.53
  255.1 1.5 reshape.130
  256.6 1.5 reduce.2
  258.2 1.6 reshape.127
  259.7 1.5 copy.59
  261.2 1.6 reshape.128.refs_13_
  262.8 0.9 pad_maximum_fusion
  263.7 1.0 constant_dynamic-slice_fusion
  264.7 1.0 constant_dynamic-slice_fusion.1
  265.7 1.2 convolution_multiply_fusion.refs_19_
  267.0 1.9 copy-done.2
  268.9 0.7 copy-done.20
  269.6 34.9 %own.1 = (bf16[768,2048]{1,0:T(8,128)(2,1)}, f32[768,256]{1,0:T(8,128)S(1)}, f32[768,256]{1,0:T(8,128)S(1)}, f32[16,2048]{1,0:T(8,128)S(1)}) custom-call(s32[4]{0:T(128)S(1)} %copy-done.20, bf16[96,8192]{1,0:T(8,128)(2,1)} %collective-permute-done.11.refs_0_, bf16[96,8192]{1,0:T(8,128)(2,1)} %collective-permute-done.refs_1_, bf16[2048,8192]{1,0:T(8,128)(2,1)} %bitcast.45, ...), custom_call_target="tpu_custom_call" | custom-call | flops 8707375104 | bytes 33554432 | tf_op jit(solution)/shard_map/own/pallas_call | solution.py:429
  304.5 0.8 collective-permute-start.16
  305.3 1.4 collective-permute-start.17
  306.7 0.8 collective-permute-start.5
  307.4 11.4 %collective-permute-done.4.refs_5_.refs_1_ = bf16[96,8192]{1,0:T(8,128)(2,1)} collective-permute-done((bf16[96,8192]{1,0:T(8,128)(2,1)}, bf16[96,8192]{1,0:T(8,128)(2,1)}, u32[]{:S(2)}, u32[]{:S(2)}) %collective-permute-start.4) | collective-permute-done | bytes 1572896 | tf_op jit(solution)/shard_map/ppermute | solution.py:258
  318.9 4.7 %collective-permute-start.6 = (bf16[96,8192]{1,0:T(8,128)(2,1)}, bf16[96,8192]{1,0:T(8,128)(2,1)S(1)}, u32[]{:S(2)}, u32[]{:S(2)}) collective-permute-start(bf16[96,8192]{1,0:T(8,128)(2,1)} %collective-permute-done.4.refs_5_.refs_1_), channel_id=1, source_target_pairs={{2,3},{6,7},{10,11},{14,15},{18,19},{22,23},{26,27},{30,31}} | collective-permute-start | bytes 4718600 | tf_op jit(solution)/shard_map/ppermute | solution.py:258
  323.6 35.2 %arrived_0.1 = (bf16[768,2048]{1,0:T(8,128)(2,1)}, f32[768,256]{1,0:T(8,128)S(1)}, f32[768,256]{1,0:T(8,128)S(1)}, f32[16,2048]{1,0:T(8,128)S(1)}, f32[16,2048]{1,0:T(8,128)S(1)}) custom-call(s32[4]{0:T(128)S(1)} %copy-done.18, bf16[96,8192]{1,0:T(8,128)(2,1)} %collective-permute-done.12.refs_0_, ...), custom_call_target="tpu_custom_call", output_to_operand_aliasing={{0}: (16, {}), {1}: (17, {}), {2}: (18, {})} | custom-call | flops 8707375104 | bytes 33554432 | tf_op jit(solution)/shard_map/arrived_0/pallas_call | solution.py:429
  358.8 35.2 %arrived_1.1 = (bf16[768,2048]{1,0:T(8,128)(2,1)}, f32[768,256]{1,0:T(8,128)S(1)}, f32[768,256]{1,0:T(8,128)S(1)}, f32[16,2048]{1,0:T(8,128)S(1)}, f32[16,2048]{1,0:T(8,128)S(1)}) custom-call(s32[4]{0:T(128)S(1)} %copy-done.19, bf16[96,8192]{1,0:T(8,128)(2,1)} %collective-permute-done.12.refs_0_, ...), custom_call_target="tpu_custom_call", output_to_operand_aliasing={{0}: (18, {}), {1}: (19, {}), {2}: (20, {})} | custom-call | flops 8707375104 | bytes 33554432 | tf_op jit(solution)/shard_map/arrived_1/pallas_call | solution.py:429
  394.1 26.4 %arrived_2_0.1 = (bf16[768,2048]{1,0:T(8,128)(2,1)}, f32[768,256]{1,0:T(8,128)S(1)}, f32[768,256]{1,0:T(8,128)S(1)}, f32[16,2048]{1,0:T(8,128)S(1)}, f32[16,2048]{1,0:T(8,128)S(1)}) custom-call(s32[4]{0:T(128)S(1)} %copy-done.17, ...), custom_call_target="tpu_custom_call", output_to_operand_aliasing={{0}: (16, {}), {1}: (17, {}), {2}: (18, {})} | custom-call | flops 4164943872 | bytes 33554432 | tf_op jit(solution)/shard_map/arrived_2_0/pallas_call | solution.py:429
  420.5 26.3 %arrived_2_1.1 = (bf16[768,2048]{1,0:T(8,128)(2,1)}, bf16[768,256]{1,0:T(8,128)(2,1)}, bf16[768,256]{1,0:T(8,128)(2,1)}, f32[16,2048]{1,0:T(8,128)}, f32[16,2048]{1,0:T(8,128)}) custom-call(s32[4]{0:T(128)S(1)} %add_add_fusion.scalars_ref, bf16[96,8192]{1,0:T(8,128)(2,1)} %collective-permute-done.2.refs_3_.refs_0_, ...), custom_call_target="tpu_custom_call", output_to_operand_aliasing={{0}: (16, {})} | custom-call | flops 4164943872 | bytes 33554432 | tf_op jit(solution)/shard_map/arrived_2_1/pallas_call | solution.py:429
  (88 shorter events, 0.8 us)
Async XLA Ops:
  0.6 5.1 %copy-start.23 = (bf16[1,768,2048]{2,1,0:T(8,128)(2,1)S(1)}, bf16[1,768,2048]{2,1,0:T(8,128)(2,1)}, u32[]{:S(2)}) copy-start(bf16[1,768,2048]{2,1,0:T(8,128)(2,1)} %param.18) | copy-start | bytes 9437188
  3.0 89.0 %collective-permute-start = (bf16[96,8192]{1,0:T(8,128)(2,1)S(1)}, bf16[96,8192]{1,0:T(8,128)(2,1)}, u32[]{:S(2)}, u32[]{:S(2)}) collective-permute-start(bf16[96,8192]{1,0:T(8,128)(2,1)S(1)} %get-tuple-element.70), channel_id=1, source_target_pairs={{4,0},{8,4},{12,8},{16,12},{20,16},{24,20},{28,24},{0,28},{5,1},{9... | collective-permute-start | bytes 4718600 | tf_op jit(solution)/shard_map/ppermute | solution.py:249
  4.9 2.4 copy-start.26
  4.9 5.0 %copy-start.27 = (bf16[1,768,256]{2,1,0:T(8,128)(2,1)S(1)}, bf16[1,768,256]{2,1,0:T(8,128)(2,1)}, u32[]{:S(2)}) copy-start(bf16[1,768,256]{2,1,0:T(8,128)(2,1)} %param.20) | copy-start | bytes 1179652
  4.9 98.1 %copy-start.25 = (s32[1,768]{1,0:T(1,128)S(1)}, s32[1,768]{1,0:T(1,128)}, u32[]{:S(2)}) copy-start(s32[1,768]{1,0:T(1,128)} %param.21) | copy-start | bytes 9220
  4.9 98.6 %copy-start.33 = (s32[4]{0:T(128)S(1)}, s32[4]{0:T(128)}, u32[]{:S(2)}) copy-start(s32[4]{0:T(128)} %constant.77.clone) | copy-start | bytes 52
  4.9 99.8 %copy-start.32 = (s32[4]{0:T(128)S(1)}, s32[4]{0:T(128)}, u32[]{:S(2)}) copy-start(s32[4]{0:T(128)} %constant.76.clone) | copy-start | bytes 52
  4.9 100.4 %copy-start.31 = (s32[4]{0:T(128)S(1)}, s32[4]{0:T(128)}, u32[]{:S(2)}) copy-start(s32[4]{0:T(128)} %constant.79.clone) | copy-start | bytes 52
  4.9 101.7 %copy-start.30 = (s32[4]{0:T(128)S(1)}, s32[4]{0:T(128)}, u32[]{:S(2)}) copy-start(s32[4]{0:T(128)} %constant.78.clone) | copy-start | bytes 52
  5.0 102.3 %copy-start.29 = (s32[4]{0:T(128)S(1)}, s32[4]{0:T(128)}, u32[]{:S(2)}) copy-start(s32[4]{0:T(128)} %constant.81.clone) | copy-start | bytes 52
  5.0 104.1 %copy-start.28 = (s32[4]{0:T(128)S(1)}, s32[4]{0:T(128)}, u32[]{:S(2)}) copy-start(s32[4]{0:T(128)} %constant.80.clone) | copy-start | bytes 52
  5.0 105.5 %copy-start.24 = (bf16[1,16,2048]{2,1,0:T(8,128)(2,1)S(1)}, bf16[1,16,2048]{2,1,0:T(8,128)(2,1)}, u32[]{:S(2)}) copy-start(bf16[1,16,2048]{2,1,0:T(8,128)(2,1)} %param.17) | copy-start | bytes 196612
  5.0 84.6 %collective-permute-start.11 = (bf16[96,8192]{1,0:T(8,128)(2,1)S(1)}, bf16[96,8192]{1,0:T(8,128)(2,1)}, u32[]{:S(2)}, u32[]{:S(2)}) collective-permute-start(bf16[96,8192]{1,0:T(8,128)(2,1)S(1)} %get-tuple-element.69), channel_id=1, source_target_pairs={{4,0},{8,4},{12,8},{16,12},{20,16},{24,20},{28,24},{0,28},{5,1},{9... | collective-permute-start | bytes 4718600 | tf_op jit(solution)/shard_map/ppermute | solution.py:249
  7.3 92.7 %collective-permute-start.10 = (bf16[384,2048]{1,0:T(8,128)(2,1)S(1)}, bf16[384,2048]{1,0:T(8,128)(2,1)S(1)}, u32[]{:S(2)}, u32[]{:S(2)}) collective-permute-start(bf16[384,2048]{1,0:T(8,128)(2,1)S(1)} %get-tuple-element.71), channel_id=1, source_target_pairs={{0,28},{4,24},{8,20},{12,16},{16,12},{20,8},{24,4},{28,0},{1,29},{... | collective-permute-start | bytes 4718600 | tf_op jit(solution)/shard_map/ppermute | solution.py:267
  7.3 78.7 %collective-permute-start.8 = (bf16[768,256]{1,0:T(8,128)(2,1)S(1)}, bf16[768,256]{1,0:T(8,128)(2,1)S(1)}, u32[]{:S(2)}, u32[]{:S(2)}) collective-permute-start(bf16[768,256]{1,0:T(8,128)(2,1)S(1)} %bitcast.54), channel_id=1, source_target_pairs={{0,28},{4,24},{8,20},{12,16},{16,12},{20,8},{24,4},{28,0},{1,29},{... | collective-permute-start | bytes 1179656 | tf_op jit(solution)/shard_map/ppermute | solution.py:264
  9.9 84.4 %collective-permute-start.9 = (bf16[768,256]{1,0:T(8,128)(2,1)S(1)}, bf16[768,256]{1,0:T(8,128)(2,1)S(1)}, u32[]{:S(2)}, u32[]{:S(2)}) collective-permute-start(bf16[768,256]{1,0:T(8,128)(2,1)S(1)} %bitcast.55), channel_id=1, source_target_pairs={{0,28},{4,24},{8,20},{12,16},{16,12},{20,8},{24,4},{28,0},{1,29},{... | collective-permute-start | bytes 1179656 | tf_op jit(solution)/shard_map/ppermute | solution.py:265
  86.0 0.7 copy-start.3
  86.8 115.6 %collective-permute-start.7 = (bf16[384,2048]{1,0:T(8,128)(2,1)}, bf16[384,2048]{1,0:T(8,128)(2,1)}, u32[]{:S(2)}, u32[]{:S(2)}) collective-permute-start(bf16[384,2048]{1,0:T(8,128)(2,1)} %get-tuple-element.72), channel_id=1, source_target_pairs={{0,28},{4,24},{8,20},{12,16},{16,12},{20,8},{24,4},{28,0},{1,29},{... | collective-permute-start | bytes 4718600 | tf_op jit(solution)/shard_map/ppermute | solution.py:267
  89.6 150.1 %collective-permute-start.12 = (bf16[96,8192]{1,0:T(8,128)(2,1)}, bf16[96,8192]{1,0:T(8,128)(2,1)}, u32[]{:S(2)}, u32[]{:S(2)}) collective-permute-start(bf16[96,8192]{1,0:T(8,128)(2,1)} %collective-permute-done.11.refs_0_), channel_id=1, source_target_pairs={{1,0},{2,1},{3,2},{5,4},{6,5},{7,6},{9,8},{10,9},{11,10},{13,12},{... | collective-permute-start | bytes 4718600 | tf_op jit(solution)/shard_map/ppermute | solution.py:259
  92.0 153.7 %collective-permute-start.1 = (bf16[96,8192]{1,0:T(8,128)(2,1)}, bf16[96,8192]{1,0:T(8,128)(2,1)}, u32[]{:S(2)}, u32[]{:S(2)}) collective-permute-start(bf16[96,8192]{1,0:T(8,128)(2,1)} %collective-permute-done.refs_1_), channel_id=1, source_target_pairs={{1,0},{2,1},{3,2},{5,4},{6,5},{7,6},{9,8},{10,9},{11,10},{13,12},{... | collective-permute-start | bytes 4718600 | tf_op jit(solution)/shard_map/ppermute | solution.py:259
  94.3 0.7 copy-start.6
  95.1 153.0 %collective-permute-start.14 = (bf16[96,8192]{1,0:T(8,128)(2,1)}, bf16[96,8192]{1,0:T(8,128)(2,1)}, u32[]{:S(2)}, u32[]{:S(2)}) collective-permute-start(bf16[96,8192]{1,0:T(8,128)(2,1)} %collective-permute-done.11.refs_0_), channel_id=1, source_target_pairs={{0,1},{1,2},{2,3},{4,5},{5,6},{6,7},{8,9},{9,10},{10,11},{12,13},{... | collective-permute-start | bytes 4718600 | tf_op jit(solution)/shard_map/ppermute | solution.py:258
  99.9 1.1 copy-start.21
  101.1 149.0 %collective-permute-start.3 = (bf16[96,8192]{1,0:T(8,128)(2,1)}, bf16[96,8192]{1,0:T(8,128)(2,1)}, u32[]{:S(2)}, u32[]{:S(2)}) collective-permute-start(bf16[96,8192]{1,0:T(8,128)(2,1)} %collective-permute-done.refs_1_), channel_id=1, source_target_pairs={{0,1},{1,2},{2,3},{4,5},{5,6},{6,7},{8,9},{9,10},{10,11},{12,13},{... | collective-permute-start | bytes 4718600 | tf_op jit(solution)/shard_map/ppermute | solution.py:258
  180.6 1.0 copy-start.4
  181.6 1.0 copy-start.7
  182.6 0.8 copy-start.10
  183.4 1.4 copy-start.22
  220.9 1.6 copy-start.1
  222.5 0.6 copy-start.13
  223.1 42.6 %copy-start = (bf16[768,2048]{1,0:T(8,128)(2,1)}, bf16[768,2048]{1,0:T(8,128)(2,1)S(1)}, u32[]{:S(2)}) copy-start(bf16[768,2048]{1,0:T(8,128)(2,1)S(1)} %get-tuple-element.42.refs_6_.refs_8_.refs_10_) | copy-start | bytes 9437188
  239.7 64.7 %collective-permute-start.13 = (bf16[96,8192]{1,0:T(8,128)(2,1)}, bf16[96,8192]{1,0:T(8,128)(2,1)}, u32[]{:S(2)}, u32[]{:S(2)}) collective-permute-start(bf16[96,8192]{1,0:T(8,128)(2,1)} %collective-permute-done.12.refs_0_), channel_id=1, source_target_pairs={{1,0},{2,1},{5,4},{6,5},{9,8},{10,9},{13,12},{14,13},{17,16},{18,1... | collective-permute-start | bytes 4718600 | tf_op jit(solution)/shard_map/ppermute | solution.py:259
  245.7 61.0 %collective-permute-start.2 = (bf16[96,8192]{1,0:T(8,128)(2,1)}, bf16[96,8192]{1,0:T(8,128)(2,1)}, u32[]{:S(2)}, u32[]{:S(2)}) collective-permute-start(bf16[96,8192]{1,0:T(8,128)(2,1)} %collective-permute-done.1.refs_1_), channel_id=1, source_target_pairs={{1,0},{2,1},{5,4},{6,5},{9,8},{10,9},{13,12},{14,13},{17,16},{18,1... | collective-permute-start | bytes 4718600 | tf_op jit(solution)/shard_map/ppermute | solution.py:259
  248.1 57.1 %collective-permute-start.15 = (bf16[96,8192]{1,0:T(8,128)(2,1)}, bf16[96,8192]{1,0:T(8,128)(2,1)}, u32[]{:S(2)}, u32[]{:S(2)}) collective-permute-start(bf16[96,8192]{1,0:T(8,128)(2,1)} %collective-permute-done.14.refs_2_), channel_id=1, source_target_pairs={{1,2},{2,3},{5,6},{6,7},{9,10},{10,11},{13,14},{14,15},{17,18},{18... | collective-permute-start | bytes 4718600 | tf_op jit(solution)/shard_map/ppermute | solution.py:258
  250.0 68.8 %collective-permute-start.4 = (bf16[96,8192]{1,0:T(8,128)(2,1)}, bf16[96,8192]{1,0:T(8,128)(2,1)}, u32[]{:S(2)}, u32[]{:S(2)}) collective-permute-start(bf16[96,8192]{1,0:T(8,128)(2,1)} %collective-permute-done.3.refs_3_), channel_id=1, source_target_pairs={{1,2},{2,3},{5,6},{6,7},{9,10},{10,11},{13,14},{14,15},{17,18},{18... | collective-permute-start | bytes 4718600 | tf_op jit(solution)/shard_map/ppermute | solution.py:258
  262.8 4.2 copy-start.5
  262.8 4.2 copy-start.8
  262.8 4.2 copy-start.9
  262.8 4.2 copy-start.11
  262.8 4.2 copy-start.14
  267.0 1.9 copy-start.2
  268.9 0.7 copy-start.20
  269.6 54.0 %copy-start.12 = (f32[4,16,192]{2,1,0:T(8,128)S(1)}, f32[4,16,192]{2,1,0:T(8,128)}, u32[]{:S(2)}) copy-start(f32[4,16,192]{2,1,0:T(8,128)} %reduce_sum.9.refs_14_.refs_16_) | copy-start | bytes 147460
  269.6 54.0 %copy-start.18 = (s32[4]{0:T(128)S(1)}, s32[4]{0:T(128)}, u32[]{:S(2)}) copy-start(s32[4]{0:T(128)} %add_add_fusion.3.scalars_ref) | copy-start | bytes 52
  304.5 89.6 %collective-permute-start.16 = (bf16[96,8192]{1,0:T(8,128)(2,1)}, bf16[96,8192]{1,0:T(8,128)(2,1)S(1)}, u32[]{:S(2)}, u32[]{:S(2)}) collective-permute-start(bf16[96,8192]{1,0:T(8,128)(2,1)} %collective-permute-done.13.refs_2_.refs_0_), channel_id=1, source_target_pairs={{1,0},{5,4},{9,8},{13,12},{17,16},{21,20},{25,24},{29,28}} | collective-permute-start | bytes 4718600 | tf_op jit(solution)/shard_map/ppermute | solution.py:259
  305.3 88.8 %collective-permute-start.17 = (bf16[96,8192]{1,0:T(8,128)(2,1)}, bf16[96,8192]{1,0:T(8,128)(2,1)S(1)}, u32[]{:S(2)}, u32[]{:S(2)}) collective-permute-start(bf16[96,8192]{1,0:T(8,128)(2,1)} %collective-permute-done.15.refs_4_.refs_1_), channel_id=1, source_target_pairs={{2,3},{6,7},{10,11},{14,15},{18,19},{22,23},{26,27},{30,31}} | collective-permute-start | bytes 4718600 | tf_op jit(solution)/shard_map/ppermute | solution.py:258
  306.7 113.8 %collective-permute-start.5 = (bf16[96,8192]{1,0:T(8,128)(2,1)}, bf16[96,8192]{1,0:T(8,128)(2,1)S(1)}, u32[]{:S(2)}, u32[]{:S(2)}) collective-permute-start(bf16[96,8192]{1,0:T(8,128)(2,1)} %collective-permute-done.2.refs_3_.refs_0_), channel_id=1, source_target_pairs={{1,0},{5,4},{9,8},{13,12},{17,16},{21,20},{25,24},{29,28}} | collective-permute-start | bytes 4718600 | tf_op jit(solution)/shard_map/ppermute | solution.py:259
  318.9 101.6 %collective-permute-start.6 = (bf16[96,8192]{1,0:T(8,128)(2,1)}, bf16[96,8192]{1,0:T(8,128)(2,1)S(1)}, u32[]{:S(2)}, u32[]{:S(2)}) collective-permute-start(bf16[96,8192]{1,0:T(8,128)(2,1)} %collective-permute-done.4.refs_5_.refs_1_), channel_id=1, source_target_pairs={{2,3},{6,7},{10,11},{14,15},{18,19},{22,23},{26,27},{30,31}} | collective-permute-start | bytes 4718600 | tf_op jit(solution)/shard_map/ppermute | solution.py:258
  323.6 35.2 %copy-start.19 = (s32[4]{0:T(128)S(1)}, s32[4]{0:T(128)}, u32[]{:S(2)}) copy-start(s32[4]{0:T(128)} %add_add_fusion.2.scalars_ref) | copy-start | bytes 52
  358.8 35.3 %copy-start.15 = (f32[8,4,1,384]{3,2,1,0:T(1,128)S(1)}, f32[8,4,1,384]{3,2,1,0:T(1,128)}, u32[]{:S(2)}) copy-start(f32[8,4,1,384]{3,2,1,0:T(1,128)} %reshape.128.refs_13_) | copy-start | bytes 147460
  358.8 35.3 %copy-start.16 = (s32[8,2,384]{2,1,0:T(2,128)S(1)}, s32[8,2,384]{2,1,0:T(2,128)}, u32[]{:S(2)}) copy-start(s32[8,2,384]{2,1,0:T(2,128)} %tile.11.refs_12_) | copy-start | bytes 73732
  358.8 35.3 %copy-start.17 = (s32[4]{0:T(128)S(1)}, s32[4]{0:T(128)}, u32[]{:S(2)}) copy-start(s32[4]{0:T(128)} %add_add_fusion.1.scalars_ref) | copy-start | bytes 52

commit v2 on v1

v2 whole, which is shorter than its diff:
```python
import functools
import math

import jax
import jax.numpy as jnp
import numpy as np
from jax import lax
from jax.experimental import pallas as pl
from jax.experimental.pallas import tpu as pltpu
from jax.sharding import PartitionSpec as P

HEAD_SIZE = 128
DOC_REACH = 384
MASKED = -1e30
LOG2E = math.log2(math.e)
VMEM_BYTES = 40 * 2**20
FLOPS_PER_MICRO = 1.0e9

adapter_scale = 2.0


def dot_nt(a, b):
    return lax.dot_general(a, b, (((1,), (1,)), ((), ())), preferred_element_type=jnp.float32)


def dot_nn(a, b):
    return lax.dot_general(a, b, (((1,), (0,)), ((), ())), preferred_element_type=jnp.float32)


def dot_tn(a, b):
    return lax.dot_general(a, b, (((0,), (0,)), ((), ())), preferred_element_type=jnp.float32)


def three_parts(a):
    high = a.astype(jnp.bfloat16)
    rest = a - high.astype(jnp.float32)
    middle = rest.astype(jnp.bfloat16)
    low = (rest - middle.astype(jnp.float32)).astype(jnp.bfloat16)
    return jnp.concatenate([high, middle, low], axis=0)


def folded(a):
    rows = a.shape[0] // 3
    return a[:rows] + a[rows : 2 * rows] + a[2 * rows :]


def stacked_heads(a):
    count = a.shape[1] // HEAD_SIZE
    return jnp.concatenate(
        [a[:, h * HEAD_SIZE : (h + 1) * HEAD_SIZE] for h in range(count)], axis=0
    )


def mask_bias(key_start, key_ids, query_pos, query_ids, shape):
    key_pos = key_start + lax.broadcasted_iota(jnp.int32, shape, 0)
    allowed = (key_pos <= query_pos) & (key_ids == query_ids)
    return jnp.where(allowed, 0.0, MASKED)


def forward_kernel(
    first_block, heads, total, q_ref, k_ref, v_ref, ids_ref, row_info_ref, down_ref, *rest
):
    ctx_ref, lse_ref, rank_ref, q_out_ref, bias_ref = rest[-5:]
    block, step = pl.program_id(0), pl.program_id(1)
    rows = q_ref.shape[0]
    window = bias_ref.shape[0]
    row_start = (first_block + block) * rows
    start = jnp.clip(row_start - DOC_REACH, 0, total - window)
    start = pl.multiple_of(start, 16)

    @pl.when(step == 0)
    def _():
        bias_ref[...] = mask_bias(
            start,
            ids_ref[pl.ds(start, window), :],
            row_info_ref[0, 0:1, :],
            row_info_ref[0, 1:2, :],
            bias_ref.shape,
        )
        rank_ref[...] = jnp.zeros_like(rank_ref)

    queries = q_ref[...]
    q_out_ref[...] = queries
    stacked = stacked_heads(queries)
    keys = k_ref[pl.ds(start, window), :]
    values = v_ref[pl.ds(start, window), :]
    scores = dot_nt(keys, stacked) * (LOG2E / math.sqrt(HEAD_SIZE)) + bias_ref[...]
    top = jnp.max(scores, axis=0, keepdims=True)
    expanded = jnp.exp2(scores - top)
    total_weight = jnp.sum(expanded, axis=0, keepdims=True)
    probs = (expanded * (1.0 / total_weight)).astype(jnp.bfloat16)
    lse_ref[0, 0] = top + jnp.log(total_weight) * LOG2E
    context_t = dot_tn(values, probs)
    context = context_t.T.astype(jnp.bfloat16)
    for h in range(heads):
        part = context[h * rows : (h + 1) * rows]
        ctx_ref[:, h * HEAD_SIZE : (h + 1) * HEAD_SIZE] = part
        rank_ref[0] += dot_nt(down_ref[:, h * HEAD_SIZE : (h + 1) * HEAD_SIZE], part)


def fetch(choice, groups, x_ref, sems):
    for c, parts in enumerate(groups):

        @pl.when(choice == c)
        def _(parts=parts):
            copies = []
            at = 0
            for p, part in enumerate(parts):
                width = part.shape[1]
                copies.append(
                    pltpu.make_async_copy(part, x_ref.at[:, pl.ds(at, width)], sems.at[p])
                )
                at += width
            for copy in copies:
                copy.start()
            for copy in copies:
                copy.wait()


def rank_product(up_ref, x_ref, first_column):
    local = up_ref.shape[2]
    width = x_ref.shape[1]
    total = None
    for j in range(width // local):
        part = dot_nt(up_ref[first_column // local + j], x_ref[:, j * local : (j + 1) * local])
        total = part if total is None else total + part
    return total


def project(x_ref, w_ref, acc):
    width = x_ref.shape[1]
    for at in range(0, width, 4096):
        to = min(at + 4096, width)
        acc = acc + dot_nt(x_ref[:, at:to], w_ref[:, at:to])
    return acc


def rank_term(rank, down):
    return adapter_scale * dot_tn(rank, jnp.concatenate([down, down, down], axis=0))


def projection_kernel(spec, scalars_ref, *refs):
    at_choice, candidates, pieces, before, ends, after = spec
    refs = list(refs)

    def take(count):
        taken = refs[:count]
        del refs[:count]
        return taken

    groups = [take(pieces) for _ in range(candidates)]
    first_column = sum(part.shape[1] for part in groups[0][:before])
    w_ref, up_ref, down_ref = take(3)
    if before:
        acc_in, rank_in = take(2)
    take(after)
    out_ref, rank_out = take(2)
    if ends:
        local_out = take(1)[0]
    x_ref, sems = take(2)
    if ends:
        parts_ref, local_ref = take(2)
    step = pl.program_id(0)

    @pl.when(step == 0)
    def _():
        fetch(scalars_ref[at_choice], [parts[before:] for parts in groups], x_ref, sems)
        rank = rank_product(up_ref, x_ref, first_column)
        rank_out[...] = rank + rank_in[...] if before else rank
        if ends:
            parts_ref[...] = three_parts(rank_out[...])
            for c, parts in enumerate(groups):
                at = 0
                for part in parts:
                    width = part.shape[1]
                    mine = scalars_ref[0] - at

                    @pl.when((scalars_ref[at_choice] == c) & (mine >= 0) & (mine < width))
                    def _(part=part, mine=mine):
                        copy = pltpu.make_async_copy(
                            part.at[:, pl.ds(pl.multiple_of(mine, 128), local_ref.shape[1])],
                            local_ref,
                            sems.at[0],
                        )
                        copy.start()
                        copy.wait()

                    at += width

    if ends:
        begin = rank_term(parts_ref[...], down_ref[...])
        if before:
            begin = begin + acc_in[...]
    else:
        begin = acc_in[...] if before else jnp.zeros(out_ref.shape, jnp.float32)
    out_ref[...] = project(x_ref, w_ref, begin).astype(out_ref.dtype)
    if ends:
        tile = local_out.shape[1]
        local_out[...] = local_ref[:, pl.ds(pl.multiple_of(step * tile, tile), tile)]


def up_map_kernel(count, scalars_ref, *refs):
    ranks = refs[:count]
    columns = refs[count : 2 * count]
    out_ref = refs[2 * count]
    rows_total = sum(c.shape[0] for c in columns)
    scale = adapter_scale / math.sqrt(rows_total * (count + 1) // count)
    total = None
    for rank, column in zip(ranks, columns):
        part = folded(dot_nn(three_parts(rank[0]), column[...]))
        total = part if total is None else total + part
    out_ref[...] = scale * total


def attention_backward(
    heads, steps_per_kv, step, start, inv_scale, grad, q_ref, ctx_ref, k_ref, v_ref, lse_ref,
    bias_ref, dk_sum, dv_sum, fresh_sums, dq_ref,
):
    window = bias_ref.shape[0]
    rows = grad.shape[0]
    queries = stacked_heads(q_ref[...])
    grads = stacked_heads(grad)
    keys = k_ref[pl.ds(start, window), :]
    values = v_ref[pl.ds(start, window), :]
    delta = jnp.sum(
        (grads.astype(jnp.float32) * stacked_heads(ctx_ref[...]).astype(jnp.float32)).T,
        axis=0,
        keepdims=True,
    )
    scores = dot_nt(keys, queries) * (LOG2E * inv_scale) + bias_ref[...]
    probs = jnp.exp2(scores - lse_ref[0, 0])
    grad_probs = dot_nt(values, grads)
    grad_scores = (probs * (grad_probs - delta)).astype(jnp.bfloat16)
    probs_low = probs.astype(jnp.bfloat16)

    @pl.when(lax.rem(step, steps_per_kv) == 0)
    def _():
        fresh_sums()

    dk_sum[pl.ds(start, window), :] += dot_nn(grad_scores, queries) * inv_scale
    dv_sum[pl.ds(start, window), :] += dot_nn(probs_low, grads)
    grad_q = (dot_tn(keys, grad_scores) * inv_scale).T.astype(jnp.bfloat16)
    for h in range(heads):
        dq_ref[:, h * HEAD_SIZE : (h + 1) * HEAD_SIZE] = grad_q[h * rows : (h + 1) * rows]


def backward_kernel(spec, scalars_ref, *refs):
    here, heads, group, total, first, last, after = spec
    refs = list(refs)

    def take(count):
        taken = refs[:count]
        del refs[:count]
        return taken

    if last:
        local_ref, rank_ctx_ref, um_in = take(3)
    grad_ref, rank_in, q_ref, ctx_ref, k_ref, v_ref, ids_ref, row_info_ref, lse_ref = take(9)
    if not first:
        _, dk_in, dv_in, dm_in = take(4)
    take(after)
    dq_ref, dk_ref, dv_ref, dm_ref = take(4)
    if last:
        um_ref = take(1)[0]
    bias_ref, parts_ref, dk_sum, dv_sum = take(4)

    step = pl.program_id(0)
    window = bias_ref.shape[0]
    start = pl.multiple_of(scalars_ref[here + 1], 16)
    gradient_scale = adapter_scale / math.sqrt(total)
    inv_scale = 1.0 / math.sqrt(HEAD_SIZE)
    steps_per_kv = group // heads

    @pl.when(step == 0)
    def _():
        parts_ref[...] = three_parts(rank_in[...])
        bias_ref[...] = mask_bias(
            start,
            ids_ref[pl.ds(start, window), :],
            row_info_ref[0, 0:1, :],
            row_info_ref[0, 1:2, :],
            bias_ref.shape,
        )

    def fresh_sums():
        if first:
            dk_sum[...] = jnp.zeros_like(dk_sum)
            dv_sum[...] = jnp.zeros_like(dv_sum)
        else:
            dk_sum[...] = dk_in[...]
            dv_sum[...] = dv_in[...]

    attention_backward(
        heads, steps_per_kv, step, start, inv_scale, grad_ref[...], q_ref, ctx_ref, k_ref, v_ref,
        lse_ref, bias_ref, dk_sum, dv_sum, fresh_sums, dq_ref,
    )

    @pl.when(lax.rem(step, steps_per_kv) == steps_per_kv - 1)
    def _():
        dk_ref[...] = dk_sum[...].astype(dk_ref.dtype)
        dv_ref[...] = dv_sum[...].astype(dv_ref.dtype)

    down_part = gradient_scale * folded(dot_nn(parts_ref[...], ctx_ref[...]))
    dm_ref[...] = down_part if first else dm_in[...] + down_part
    if last:
        um_ref[...] = um_in[...] + gradient_scale * folded(
            dot_nn(three_parts(rank_ctx_ref[0]), local_ref[...])
        )


def options(name, micros):
    return dict(
        compiler_params=pltpu.CompilerParams(
            dimension_semantics=("arbitrary",), vmem_limit_bytes=VMEM_BYTES
        ),
        cost_estimate=pl.CostEstimate(
            flops=int(micros * FLOPS_PER_MICRO), bytes_accessed=1, transcendentals=0
        ),
        name=name,
    )


ANYWHERE = pl.BlockSpec(memory_space=pl.ANY)


def per_device(
    handoff_gradient,
    output_weight,
    adapter_down,
    adapter_up,
    stored_queries,
    stored_keys,
    stored_values,
    segments,
):
    pipe_count = lax.axis_size("pipe")
    line = lax.axis_size("fsdp")
    member = lax.axis_index("fsdp")
    shard = handoff_gradient.shape[1]
    total = shard * line
    model_width = handoff_gradient.shape[2]
    query_width = stored_queries.shape[2]
    kv_width = stored_keys.shape[2]
    rank = adapter_down.shape[1]
    query_heads = query_width // HEAD_SIZE
    kv_heads = kv_width // HEAD_SIZE
    group = query_heads // kv_heads
    local_width = adapter_up.shape[2]
    bf16, f32 = jnp.bfloat16, jnp.float32
    weight = output_weight[0]
    down = adapter_down[0]

    def spread(block):
        blocks = [block]
        for d in range(1, line):
            route = [(i, (i + d) % line) for i in range(line)]
            blocks.append(lax.ppermute(block, "fsdp", route))
        turned = jnp.stack(blocks[::-1] + blocks[::-1])
        return lax.dynamic_slice_in_dim(turned, line - 1 - member, line, 0)

    from_next = [((i + 1) % pipe_count, i) for i in range(pipe_count)]
    mirrored = [(i, pipe_count - 1 - i) for i in range(pipe_count)]
    widths = [model_width // 4, model_width // 2, model_width // 4]
    pieces = len(widths)
    own, at = [], 0
    for width in widths:
        part = handoff_gradient[0, :, at : at + width]
        if own:
            part, _ = lax.optimization_barrier((part, own[-1]))
        own.append(lax.ppermute(part, "pipe", from_next))
        at += width
    up_all = spread(lax.optimization_barrier((adapter_up[0], own[0]))[0])
    rising, falling = [own], [own]

    def pass_on(tokens):
        k = len(rising)
        if k >= line:
            return
        up_pairs = [(i, i + 1) for i in range(k - 1, line - 1)]
        down_pairs = [(i + 1, i) for i in range(line - k)]
        up_now, down_now = [], []
        for p in range(pieces):
            up_part, down_part = rising[-1][p], falling[-1][p]
            if tokens is not None:
                up_part, down_part, _ = lax.optimization_barrier((up_part, down_part, tokens[p]))
            up_now.append(lax.ppermute(up_part, "fsdp", up_pairs))
            down_now.append(lax.ppermute(down_part, "fsdp", down_pairs))
        rising.append(up_now)
        falling.append(down_now)

    pass_on(None)
    saved_k, saved_v, saved_q, _ = lax.optimization_barrier(
        (stored_keys[0], stored_values[0], stored_queries[0], own[1])
    )
    key_local = lax.ppermute(saved_k, "pipe", mirrored)
    value_local = lax.ppermute(saved_v, "pipe", mirrored)
    half = total // 2
    query_half = [
        lax.ppermute(saved_q[i * half : (i + 1) * half], "pipe", mirrored) for i in range(2)
    ]

    def arrival(device, order):
        found = []
        for k in range(1, line):
            if device >= k:
                found.append((k, True, device - k))
            if device + k < line:
                found.append((k, False, device + k))
        return found[order]

    def groups_of(order):
        if order < 0:
            return [(0, True)]
        return sorted({arrival(d, order)[:2] for d in range(line)})

    def choices(order):
        return [(rising if rises else falling)[k] for k, rises in groups_of(order)]

    window = min(total, shard + DOC_REACH)
    table = np.zeros((line, 1 + 3 * line), np.int32)
    for d in range(line):
        table[d, 0] = d * local_width
        for order in range(-1, line - 1):
            found = (0, True, d) if order < 0 else arrival(d, order)
            first_key = min(max(found[2] * shard - DOC_REACH, 0), total - window)
            at = 4 + 3 * order
            table[d, at : at + 3] = groups_of(order).index(found[:2]), found[2], first_key
    scalars = lax.dynamic_index_in_dim(jnp.asarray(table), member, 0, keepdims=False)

    tile_p = min(512, query_width)

    def projection(order, after, low=0, high=pieces, sums=()):
        groups = choices(order)
        ends = high == pieces
        groups = [parts[:high] for parts in groups]
        width = sum(widths[low:high])
        block, odd = divmod(sum(widths[:low]), width)
        assert odd == 0
        operands = [part for parts in groups for part in parts]
        in_specs = [ANYWHERE] * len(operands)
        rank_spec = pl.BlockSpec((rank, shard), lambda n, s: (0, 0))
        tile_spec = pl.BlockSpec((shard, tile_p), lambda n, s: (0, n))
        operands += [weight, up_all, down, *sums, *after]
        in_specs += [
            pl.BlockSpec((tile_p, width), lambda n, s: (n, block)),
            pl.BlockSpec((line, rank, local_width), lambda n, s: (0, 0, 0)),
            pl.BlockSpec((rank, tile_p), lambda n, s: (0, n)),
        ]
        in_specs += [tile_spec, rank_spec][: len(sums)] + [ANYWHERE] * len(after)
        out_shape = [
            jax.ShapeDtypeStruct((shard, query_width), bf16 if ends else f32),
            jax.ShapeDtypeStruct((rank, shard), f32),
        ]
        out_specs = [tile_spec, rank_spec]
        scratch = [
            pltpu.VMEM((shard, width), bf16),
            pltpu.SemaphoreType.DMA((high - low,)),
        ]
        if ends:
            out_shape.append(jax.ShapeDtypeStruct((shard, local_width), bf16))
            out_specs.append(
                pl.BlockSpec((shard, local_width * tile_p // query_width), lambda n, s: (0, n))
            )
            scratch.append(pltpu.VMEM((3 * rank, shard), bf16))
            scratch.append(pltpu.VMEM((shard, local_width), bf16))
        return pl.pallas_call(
            functools.partial(
                projection_kernel, (4 + 3 * order, len(groups), high, low, ends, len(after))
            ),
            grid_spec=pltpu.PrefetchScalarGridSpec(
                num_scalar_prefetch=1,
                grid=(query_width // tile_p,),
                in_specs=in_specs,
                out_specs=out_specs,
                scratch_shapes=scratch,
            ),
            out_shape=out_shape,
            **options(f"projection_{order + 1}_{high}", 20 * (high - low) / pieces),
        )(scalars, *operands)

    projected = [projection(-1, [])]
    done_before = projected[0][1]
    if line > 2:
        pass_on([done_before] * pieces)
        projected.append(projection(0, [done_before, key_local, value_local, query_half[0]]))
        done_before = projected[1][1]

    ids_column = segments[0][:, None]
    rows_f = total // 4
    heads_f = 2
    steps_f = query_heads // heads_f
    lanes_f = heads_f * rows_f
    window_f = min(total, rows_f + DOC_REACH)

    def row_info(rows, heads):
        pos = jnp.arange(total, dtype=jnp.int32).reshape(total // rows, 1, rows)
        ids = segments[0].reshape(total // rows, 1, rows)
        both = jnp.concatenate([pos, ids], axis=1)
        return jnp.tile(both, (1, 1, heads))

    def waits(piece):
        return [rising[2][piece], falling[2][piece]] if line > 2 else []

    forward_out = None
    normalisers = []
    info_f = row_info(rows_f, heads_f)
    for i in range(2):
        base = 2 * i
        in_specs = [
            pl.BlockSpec((rows_f, heads_f * HEAD_SIZE), lambda b, n: (b, n)),
            pl.BlockSpec((total, HEAD_SIZE), lambda b, n: (0, n * heads_f // group)),
            pl.BlockSpec((total, HEAD_SIZE), lambda b, n: (0, n * heads_f // group)),
            pl.BlockSpec((total, 1), lambda b, n: (0, 0)),
            pl.BlockSpec((1, 2, lanes_f), lambda b, n, base=base: (base + b, 0, 0)),
            pl.BlockSpec((rank, heads_f * HEAD_SIZE), lambda b, n: (0, n)),
        ]
        operands = [query_half[i], key_local, value_local, ids_column, info_f, down]
        aliases = {}
        if forward_out is None:
            pins = [done_before] + waits(0)
            operands += pins
            in_specs += [ANYWHERE] * len(pins)
        else:
            for j, a in enumerate(forward_out):
                aliases[len(operands)] = j
                operands.append(a)
                in_specs.append(ANYWHERE)
            operands += waits(1)
            in_specs += [ANYWHERE] * len(waits(1))
        settings = options(f"forward_{i}", 18)
        settings["compiler_params"] = pltpu.CompilerParams(
            dimension_semantics=("arbitrary", "arbitrary"), vmem_limit_bytes=VMEM_BYTES
        )
        forward_out = pl.pallas_call(
            functools.partial(forward_kernel, base, heads_f, total),
            grid=(2, steps_f),
            in_specs=in_specs,
            out_specs=[
                pl.BlockSpec((rows_f, heads_f * HEAD_SIZE), lambda b, n, base=base: (base + b, n)),
                pl.BlockSpec((1, 1, 1, lanes_f), lambda b, n, base=base: (base + b, n, 0, 0)),
                pl.BlockSpec((1, rank, rows_f), lambda b, n, base=base: (base + b, 0, 0)),
                pl.BlockSpec((rows_f, heads_f * HEAD_SIZE), lambda b, n, base=base: (base + b, n)),
            ],
            out_shape=[
                jax.ShapeDtypeStruct((total, query_width), bf16),
                jax.ShapeDtypeStruct((4, steps_f, 1, lanes_f), f32),
                jax.ShapeDtypeStruct((4, rank, rows_f), f32),
                jax.ShapeDtypeStruct((total, query_width), bf16),
            ],
            scratch_shapes=[pltpu.VMEM((window_f, lanes_f), f32)],
            input_output_aliases=aliases,
            **settings,
        )(*operands)
        normalisers.append(forward_out[1])
    context, lse, rank_portion, query = forward_out

    rank_context = rank_portion
    for d in range(1, line):
        route = [(i, (i + d) % line) for i in range(line)]
        rank_context = rank_context + lax.ppermute(rank_portion, "fsdp", route)

    rows = shard
    heads = max(1, min(group, 384 // rows))
    normal = (
        lse.reshape(4, query_heads, rows_f // rows, rows)
        .transpose(0, 2, 1, 3)
        .reshape(total // rows, query_heads // heads, 1, heads * rows)
    )
    ranks = (
        rank_context.reshape(4, rank, rows_f // rows, rows)
        .transpose(0, 2, 1, 3)
        .reshape(total // rows, rank, rows)
    )
    info = row_info(rows, heads)
    tile = heads * HEAD_SIZE
    lanes = heads * rows
    per_kv = group // heads
    kv_spec = pl.BlockSpec((total, HEAD_SIZE), lambda n, s: (0, n // per_kv))
    tile_spec = pl.BlockSpec((rows, tile), lambda n, s: (0, n))
    map_spec = pl.BlockSpec((rank, tile), lambda n, s: (0, n))
    rank_spec = pl.BlockSpec((rank, rows), lambda n, s: (0, 0))

    def backward(order, state, source, up_map=None, after=()):
        first = state is None
        last = up_map is not None
        here = 5 + 3 * order
        row_spec = pl.BlockSpec((rows, tile), lambda n, s: (s[here], n))
        ctx_rank_spec = pl.BlockSpec((1, rank, rows), lambda n, s: (s[here], 0, 0))
        operands, in_specs = [], []
        grad, rank_grad, local_columns = source
        if last:
            operands += [local_columns, ranks, up_map]
            in_specs += [tile_spec, ctx_rank_spec, map_spec]
        operands += [
            grad,
            rank_grad,
            query,
            context,
            key_local,
            value_local,
            ids_column,
            info,
            normal,
        ]
        in_specs += [
            tile_spec,
            rank_spec,
            row_spec,
            row_spec,
            kv_spec,
            kv_spec,
            pl.BlockSpec((total, 1), lambda n, s: (0, 0)),
            pl.BlockSpec((1, 2, lanes), lambda n, s: (s[here], 0, 0)),
            pl.BlockSpec((1, 1, 1, lanes), lambda n, s: (s[here], n, 0, 0)),
        ]
        aliases = {}
        if not first:
            aliases[1 + len(operands)] = 0
            operands += list(state)
            in_specs += [ANYWHERE, kv_spec, kv_spec, map_spec]
        operands += list(after)
        in_specs += [ANYWHERE] * len(after)
        kv_type = bf16 if last else f32
        out_shape = [
            jax.ShapeDtypeStruct((total, query_width), bf16),
            jax.ShapeDtypeStruct((total, kv_width), kv_type),
            jax.ShapeDtypeStruct((total, kv_width), kv_type),
            jax.ShapeDtypeStruct((rank, query_width), f32),
        ]
        out_specs = [row_spec, kv_spec, kv_spec, map_spec]
        scratch = [
            pltpu.VMEM((window, lanes), f32),
            pltpu.VMEM((3 * rank, rows), bf16),
            pltpu.VMEM((total, HEAD_SIZE), f32),
            pltpu.VMEM((total, HEAD_SIZE), f32),
        ]
        if last:
            out_shape.append(jax.ShapeDtypeStruct((rank, local_width), f32))
            out_specs.append(map_spec)
        return pl.pallas_call(
            functools.partial(
                backward_kernel, (here, heads, group, total, first, last, len(after))
            ),
            grid_spec=pltpu.PrefetchScalarGridSpec(
                num_scalar_prefetch=1,
                grid=(query_heads // heads,),
                in_specs=in_specs,
                out_specs=out_specs,
                scratch_shapes=scratch,
            ),
            out_shape=out_shape,
            input_output_aliases=aliases,
            **options(f"backward_{order + 1}", 12),
        )(scalars, *operands)

    pass_on([normalisers[0]] + [lse] * (pieces - 1))
    state = backward(-1, None, projected[0], after=waits(pieces - 1))
    for order in range(line - 2):
        if order:
            projected.append(projection(order, [state[3], rising[-1][0], falling[-1][0]]))
        state = backward(order, state, projected[order + 1])
        pass_on([state[3]] * pieces)

    count = line - 1
    up_map = pl.pallas_call(
        functools.partial(up_map_kernel, count),
        grid_spec=pltpu.PrefetchScalarGridSpec(
            num_scalar_prefetch=1,
            grid=(local_width // tile,),
            in_specs=[
                pl.BlockSpec((1, rank, rows), lambda n, s, j=j: (s[2 + 3 * j], 0, 0)) for j in range(count)
            ]
            + [tile_spec] * count,
            out_specs=map_spec,
        ),
        out_shape=jax.ShapeDtypeStruct((rank, local_width), f32),
        **options("up_map", 3),
    )(scalars, *([ranks] * count), *[p[2] for p in projected])
    sums = projection(line - 2, [state[3], up_map], 0, pieces - 1)
    end = projection(line - 2, [], pieces - 1, pieces, sums)
    query_gradient, key_gradient, value_gradient, down_map, up_map = backward(
        line - 2, state, end, up_map
    )
    return (
        query_gradient[None],
        key_gradient[None],
        value_gradient[None],
        down_map[None],
        up_map[None],
    )


def solution(mesh):
    placed = (
        P("pipe", "fsdp", None),
        P("pipe", "fsdp", None),
        P("pipe", None, "fsdp"),
        P("pipe", None, "fsdp"),
        P("pipe", None, "fsdp"),
        P("pipe", None, "fsdp"),
        P("pipe", None, "fsdp"),
        P("pipe", None),
    )
    return jax.shard_map(
        per_device,
        mesh=mesh,
        in_specs=placed,
        out_specs=(
            P("pipe", None, "fsdp"),
            P("pipe", None, "fsdp"),
            P("pipe", None, "fsdp"),
            P("pipe", None, "fsdp"),
            P("pipe", None, "fsdp"),
        ),
        check_vma=False,
    )
```

time: 448 us -> 321 us (0.72)
  the two profiles are of different devices: /device:TPU:16 before, /device:TPU:0 now
where the time goes in v2:
time: 321 us; the launch traced here: 317 us
  Pallas kernels  162 us (50%)
  starting transfers between devices  62.7 us (20%)
  waiting for transfers between devices  50 us (16%)
  local copies, waits for them, and re-layouts  39.7 us (12%)
    pallas_call x5, Pallas kernels, projection(): pl.pallas_call(functools.partial(projection_kernel, (4 + 3 * order, len(g...  77.4 us
    pallas_call x4, Pallas kernels, backward(): pl.pallas_call(functools.partial(backward_kernel, (here, heads, group, to...  46.7 us
    pallas_call x2, Pallas kernels, per_device(): pl.pallas_call(functools.partial(forward_kernel, base, heads_f, total), g...  35.4 us
    unnamed x125, local copies, waits for them, and re-layouts  35.2 us
    ppermute x3, waiting for transfers between devices, per_device(): own.append(lax.ppermute(part, 'pipe', from_next))  33 us
    ppermute x9, starting transfers between devices, pass_on(): up_now.append(lax.ppermute(up_part, 'fsdp', up_pairs))  20.2 us
    ppermute x3, starting transfers between devices, per_device(): rank_context = rank_context + lax.ppermute(rank_portion, 'fsdp', route)  12.2 us
    ppermute x9, starting transfers between devices, pass_on(): down_now.append(lax.ppermute(down_part, 'fsdp', down_pairs))  11.6 us
  transfers between devices with their start and end apart: 31, of which 5 were waited for; matrix products, arithmetic and copies ran while one was open for 1% of the time, Pallas kernels for 45%

profile of v2, /device:TPU:0, one launch (start us, length us, event | category | flops | bytes accessed | tf_op | source)
XLA Modules:
  0.0 316.7 jit_solution(5626744003135978114)
XLA Ops:
  0.6 1.5 slice_bitcast_fusion.1
  2.2 3.4 %collective-permute-start = (bf16[192,2048]{1,0:T(8,128)(2,1)S(1)}, bf16[192,2048]{1,0:T(8,128)(2,1)S(1)}, u32[]{:S(2)}, u32[]{:S(2)}) collective-permute-start(bf16[192,2048]{1,0:T(8,128)(2,1)S(1)} %get-tuple-element.122), channel_id=1, source_target_pairs={{4,0},{8,4},{12,8},{16,12},{20,16},{24,20},{28,24},{0,28},{5,1},{9... | collective-permute-start | bytes 2359304 | tf_op jit(solution)/shard_map/ppermute | solution.py:370
  6.0 1.7 slice_bitcast_fusion
  7.7 7.4 %collective-permute-done.refs_0_ = bf16[192,2048]{1,0:T(8,128)(2,1)S(1)} collective-permute-done((bf16[192,2048]{1,0:T(8,128)(2,1)S(1)}, bf16[192,2048]{1,0:T(8,128)(2,1)S(1)}, u32[]{:S(2)}, u32[]{:S(2)}) %collective-permute-start) | collective-permute-done | bytes 786464 | tf_op jit(solution)/shard_map/ppermute | solution.py:370
  15.1 3.6 %collective-permute-start.5 = (bf16[16,2048]{1,0:T(8,128)(2,1)S(1)}, bf16[16,2048]{1,0:T(8,128)(2,1)S(1)}, u32[]{:S(2)}, u32[]{:S(2)}) collective-permute-start(bf16[16,2048]{1,0:T(8,128)(2,1)S(1)} %bitcast.45), channel_id=1, source_target_pairs={{0,3},{1,0},{2,1},{3,2},{4,7},{5,4},{6,5},{7,6},{8,11},{9,8},{10,9... | collective-permute-start | bytes 196616 | tf_op jit(solution)/shard_map/ppermute | solution.py:357
  19.4 1.0 collective-permute-start.7
  20.4 2.0 collective-permute-start.3
  22.4 1.3 collective-permute-start.2
  23.7 5.1 %collective-permute-start.1 = (bf16[192,2048]{1,0:T(8,128)(2,1)S(1)}, bf16[192,2048]{1,0:T(8,128)(2,1)S(1)}, u32[]{:S(2)}, u32[]{:S(2)}) collective-permute-start(bf16[192,2048]{1,0:T(8,128)(2,1)S(1)} %collective-permute-done.refs_0_), channel_id=1, source_target_pairs={{0,1},{1,2},{2,3},{4,5},{5,6},{6,7},{8,9},{9,10},{10,11},{12,13},{... | collective-permute-start | bytes 2359304 | tf_op jit(solution)/shard_map/ppermute | solution.py:386
  28.8 11.5 %collective-permute-done.3.refs_1_ = bf16[192,4096]{1,0:T(8,128)(2,1)S(1)} collective-permute-done((bf16[192,4096]{1,0:T(8,128)(2,1)S(1)}, bf16[192,4096]{1,0:T(8,128)(2,1)S(1)}, u32[]{:S(2)}, u32[]{:S(2)}) %collective-permute-start.3) | collective-permute-done | bytes 1572896 | tf_op jit(solution)/shard_map/ppermute | solution.py:370
  40.3 1.3 collective-permute-start.10
  41.6 5.1 %collective-permute-start.9 = (bf16[192,4096]{1,0:T(8,128)(2,1)S(1)}, bf16[192,4096]{1,0:T(8,128)(2,1)S(1)}, u32[]{:S(2)}, u32[]{:S(2)}) collective-permute-start(bf16[192,4096]{1,0:T(8,128)(2,1)S(1)} %collective-permute-done.3.refs_1_), channel_id=1, source_target_pairs={{0,1},{1,2},{2,3},{4,5},{5,6},{6,7},{8,9},{9,10},{10,11},{12,13},{... | collective-permute-start | bytes 4718600 | tf_op jit(solution)/shard_map/ppermute | solution.py:386
  46.7 2.6 collective-permute-start.4
  50.5 2.5 collective-permute-start.20
  53.0 14.2 %collective-permute-done.4.refs_2_ = bf16[192,2048]{1,0:T(8,128)(2,1)S(1)} collective-permute-done((bf16[192,2048]{1,0:T(8,128)(2,1)S(1)}, bf16[192,2048]{1,0:T(8,128)(2,1)S(1)}, u32[]{:S(2)}, u32[]{:S(2)}) %collective-permute-start.4) | collective-permute-done | bytes 786464 | tf_op jit(solution)/shard_map/ppermute | solution.py:370
  67.2 3.1 collective-permute-start.18
  70.3 8.2 %collective-permute-done.10.refs_1_ = bf16[192,4096]{1,0:T(8,128)(2,1)S(1)} collective-permute-done((bf16[192,4096]{1,0:T(8,128)(2,1)S(1)}, bf16[192,4096]{1,0:T(8,128)(2,1)S(1)}, u32[]{:S(2)}, u32[]{:S(2)}) %collective-permute-start.10) | collective-permute-done | bytes 1572896 | tf_op jit(solution)/shard_map/ppermute | solution.py:387
  78.5 1.3 collective-permute-start.13
  79.8 5.4 %collective-permute-start.12 = (bf16[192,2048]{1,0:T(8,128)(2,1)S(1)}, bf16[192,2048]{1,0:T(8,128)(2,1)}, u32[]{:S(2)}, u32[]{:S(2)}) collective-permute-start(bf16[192,2048]{1,0:T(8,128)(2,1)S(1)} %collective-permute-done.4.refs_2_), channel_id=1, source_target_pairs={{0,1},{1,2},{2,3},{4,5},{5,6},{6,7},{8,9},{9,10},{10,11},{12,13},{... | collective-permute-start | bytes 2359304 | tf_op jit(solution)/shard_map/ppermute | solution.py:386
  85.2 17.6 %projection_0_3.1 = (bf16[192,2048]{1,0:T(8,128)(2,1)S(1)}, f32[16,192]{1,0:T(8,128)S(1)}, bf16[192,2048]{1,0:T(8,128)(2,1)S(1)}) custom-call(s32[13]{0:T(128)S(1)} %dynamic-slice_bitcast_fusion.scalars_ref, bf16[192,2048]{1,0:T(8,128)(2,1)S(1)} %collective-permute-done.refs_0_, bf16[192,4096]{1,0:T(8,128)(2,1)S(1)} %collective-permute-done.3.refs_1_, ...), custom_call_target="tpu_custom_call" | custom-call | flops 20000000000 | bytes 1 | tf_op jit(solution)/shard_map/projection_0_3/pallas_call | solution.py:466
  105.0 1.3 collective-permute-start.8
  106.3 8.7 %collective-permute-done.18.refs_12_.q_ref = bf16[384,2048]{1,0:T(8,128)(2,1)S(1)} collective-permute-done((bf16[384,2048]{1,0:T(8,128)(2,1)S(1)}, bf16[384,2048]{1,0:T(8,128)(2,1)S(1)}, u32[]{:S(2)}, u32[]{:S(2)}) %collective-permute-start.18) | collective-permute-done | bytes 1572896 | tf_op jit(solution)/shard_map/ppermute | solution.py:399
  115.0 1.3 collective-permute-start.11
  117.1 20.2 %projection_1_3.1 = (bf16[192,2048]{1,0:T(8,128)(2,1)S(1)}, f32[16,192]{1,0:T(8,128)S(1)}, bf16[192,2048]{1,0:T(8,128)(2,1)S(1)}) custom-call(s32[13]{0:T(128)S(1)} %dynamic-slice_bitcast_fusion.scalars_ref, bf16[192,2048]{1,0:T(8,128)(2,1)S(1)} %collective-permute-done.2.refs_0_, bf16[192,4096]{1,0:T(8,128)(2,1)S(1)} %collective-permute-done.10.refs_1_, ...), custom_call_target="tpu_custom_call" | custom-call | flops 20000000000 | bytes 1 | tf_op jit(solution)/shard_map/projection_1_3/pallas_call | solution.py:466
  138.2 17.6 %forward_0.1 = (bf16[768,2048]{1,0:T(8,128)(2,1)S(1)}, f32[4,8,1,384]{3,2,1,0:T(1,128)S(1)}, f32[4,16,192]{2,1,0:T(8,128)S(1)}, bf16[768,2048]{1,0:T(8,128)(2,1)S(1)}) custom-call(bf16[384,2048]{1,0:T(8,128)(2,1)S(1)} %collective-permute-done.18.refs_12_.q_ref, bf16[768,256]{1,0:T(8,128)(2,1)S(1)} %collective-permute-done.19.refs_10_.k_ref.refs_4_.refs_7_, ...), custom_call_target="tpu_custom_call" | custom-call | flops 17999998976 | bytes 1 | tf_op jit(solution)/shard_map/forward_0/pallas_call | solution.py:534
  155.9 1.7 copy-done.28
  157.5 1.3 collective-permute-start.14
  159.5 1.3 collective-permute-start.21
  161.6 1.0 copy-done.4
  162.6 1.0 copy-done.16
  163.6 1.9 copy-done.29
  165.5 17.7 %forward_1.1 = (bf16[768,2048]{1,0:T(8,128)(2,1)S(1)}, f32[4,8,1,384]{3,2,1,0:T(1,128)S(1)}, f32[4,16,192]{2,1,0:T(8,128)S(1)}, bf16[768,2048]{1,0:T(8,128)(2,1)S(1)}) custom-call(bf16[384,2048]{1,0:T(8,128)(2,1)S(1)} %collective-permute-done.22.q_ref, ...), custom_call_target="tpu_custom_call", output_to_operand_aliasing={{0}: (6, {}), {1}: (7, {}), {2}: (8, {}), {3}: (9, {})} | custom-call | flops 17999998976 | bytes 1 | tf_op jit(solution)/shard_map/forward_1/pallas_call | solution.py:534
  183.2 1.6 copy-done.34
  184.9 9.8 %collective-permute-start.28 = (f32[4,16,192]{2,1,0:T(8,128)S(1)}, f32[4,16,192]{2,1,0:T(8,128)}, u32[]{:S(2)}, u32[]{:S(2)}) collective-permute-start(f32[4,16,192]{2,1,0:T(8,128)S(1)} %get-tuple-element.102), channel_id=1, source_target_pairs={{0,1},{1,2},{2,3},{3,0},{4,5},{5,6},{6,7},{7,4},{8,9},{9,10},{10,1... | collective-permute-start | bytes 147464 | tf_op jit(solution)/shard_map/ppermute | solution.py:560
  194.7 2.4 collective-permute-start.30
  197.1 1.9 copy-done.35
  199.0 1.1 copy-done.51
  200.2 11.4 %backward_0.1 = (bf16[768,2048]{1,0:T(8,128)(2,1)}, f32[768,256]{1,0:T(8,128)S(1)}, f32[768,256]{1,0:T(8,128)S(1)}, f32[16,2048]{1,0:T(8,128)S(1)}) custom-call(s32[13]{0:T(128)S(1)} %dynamic-slice_bitcast_fusion.scalars_ref, bf16[192,2048]{1,0:T(8,128)(2,1)S(1)} %copy-done.51, f32[16,192]{1,0:T(8,128)S(1)} %get-tuple-element.65.refs_9_.refs_1_, ...), custom_call_target="tpu_custom_call" | custom-call | flops 12000000000 | bytes 1 | tf_op jit(solution)/shard_map/backward_0/pallas_call | solution.py:640
  211.6 1.9 copy-done.31
  213.5 1.1 copy-done.45
  214.6 11.7 %backward_1.1 = (bf16[768,2048]{1,0:T(8,128)(2,1)}, f32[768,256]{1,0:T(8,128)S(1)}, f32[768,256]{1,0:T(8,128)S(1)}, f32[16,2048]{1,0:T(8,128)S(1)}) custom-call(s32[13]{0:T(128)S(1)} %dynamic-slice_bitcast_fusion.scalars_ref, bf16[192,2048]{1,0:T(8,128)(2,1)S(1)} %copy-done.45, ...), custom_call_target="tpu_custom_call", output_to_operand_aliasing={{0}: (10, {})} | custom-call | flops 12000000000 | bytes 1 | tf_op jit(solution)/shard_map/backward_1/pallas_call | solution.py:640
  226.3 1.3 collective-permute-start.23
  228.4 1.4 copy-done.9
  229.8 1.1 copy-done.11
  230.9 18.0 %projection_2_3.1 = (bf16[192,2048]{1,0:T(8,128)(2,1)S(1)}, f32[16,192]{1,0:T(8,128)S(1)}, bf16[192,2048]{1,0:T(8,128)(2,1)S(1)}) custom-call(s32[13]{0:T(128)S(1)} %dynamic-slice_bitcast_fusion.scalars_ref, bf16[192,2048]{1,0:T(8,128)(2,1)S(1)} %copy-done.11, bf16[192,4096]{1,0:T(8,128)(2,1)S(1)} %copy-done.9, ...), custom_call_target="tpu_custom_call" | custom-call | flops 20000000000 | bytes 1 | tf_op jit(solution)/shard_map/projection_2_3/pallas_call | solution.py:466
  249.9 1.0 copy-done.38
  250.8 1.0 copy-done.13
  251.8 1.0 copy-done.18
  252.8 1.9 copy-done.32
  254.7 1.1 copy-done.39
  255.9 1.1 copy-done.47
  257.0 1.1 copy-done.49
  258.1 11.7 %backward_2.1 = (bf16[768,2048]{1,0:T(8,128)(2,1)}, f32[768,256]{1,0:T(8,128)S(1)}, f32[768,256]{1,0:T(8,128)S(1)}, f32[16,2048]{1,0:T(8,128)S(1)}) custom-call(s32[13]{0:T(128)S(1)} %dynamic-slice_bitcast_fusion.scalars_ref, bf16[192,2048]{1,0:T(8,128)(2,1)S(1)} %copy-done.39, ...), custom_call_target="tpu_custom_call", output_to_operand_aliasing={{0}: (10, {})} | custom-call | flops 12000000000 | bytes 1 | tf_op jit(solution)/shard_map/backward_2/pallas_call | solution.py:640
  269.8 1.0 copy-done.42
  270.8 1.3 collective-permute-start.24
  274.0 1.1 copy-done.23
  275.1 1.1 copy-done.25
  276.2 2.4 up_map.1.refs_12_.refs_2_
  278.7 14.0 %projection_3_2.1 = (f32[192,2048]{1,0:T(8,128)S(1)}, f32[16,192]{1,0:T(8,128)S(1)}) custom-call(s32[13]{0:T(128)S(1)} %dynamic-slice_bitcast_fusion.scalars_ref, bf16[192,2048]{1,0:T(8,128)(2,1)S(1)} %collective-permute-done.8.rest_2_.refs_3_.refs_0_, bf16[192,4096]{1,0:T(8,128)(2,1)S(1)} %collective-permute-done.11.rest_5_.refs_4_.refs_1_, ...), custom_call_target="tpu_custom_call" | custom-call | flops 13333332992 | bytes 1 | tf_op jit(solution)/shard_map/projection_3_2/pallas_call | solution.py:466
  292.7 1.2 copy-done
  293.9 1.1 copy-done.2
  295.0 7.7 %projection_3_3.1 = (bf16[192,2048]{1,0:T(8,128)(2,1)S(1)}, f32[16,192]{1,0:T(8,128)S(1)}, bf16[192,2048]{1,0:T(8,128)(2,1)S(1)}) custom-call(s32[13]{0:T(128)S(1)} %dynamic-slice_bitcast_fusion.scalars_ref, bf16[192,2048]{1,0:T(8,128)(2,1)S(1)} %collective-permute-done.8.rest_2_.refs_3_.refs_0_, ...), custom_call_target="tpu_custom_call" | custom-call | flops 6666666496 | bytes 1 | tf_op jit(solution)/shard_map/projection_3_3/pallas_call | solution.py:466
  302.9 1.9 copy-done.33
  304.7 12.0 %backward_3.1 = (bf16[768,2048]{1,0:T(8,128)(2,1)}, bf16[768,256]{1,0:T(8,128)(2,1)}, bf16[768,256]{1,0:T(8,128)(2,1)}, f32[16,2048]{1,0:T(8,128)}, f32[16,2048]{1,0:T(8,128)}) custom-call(s32[13]{0:T(128)S(1)} %dynamic-slice_bitcast_fusion.scalars_ref, bf16[192,2048]{1,0:T(8,128)(2,1)S(1)} %get-tuple-element.108.refs_0_, ...), custom_call_target="tpu_custom_call", output_to_operand_aliasing={{0}: (13, {})} | custom-call | flops 12000000000 | bytes 1 | tf_op jit(solution)/shard_map/backward_3/pallas_call | solution.py:640
  (150 shorter events, 11.2 us)
Async XLA Ops:
  0.6 5.0 %copy-start.56 = (s32[1,768]{1,0:T(1,128)S(1)}, s32[1,768]{1,0:T(1,128)}, u32[]{:S(2)}) copy-start(s32[1,768]{1,0:T(1,128)} %param.16) | copy-start | bytes 9220
  2.2 12.9 %collective-permute-start = (bf16[192,2048]{1,0:T(8,128)(2,1)S(1)}, bf16[192,2048]{1,0:T(8,128)(2,1)S(1)}, u32[]{:S(2)}, u32[]{:S(2)}) collective-permute-start(bf16[192,2048]{1,0:T(8,128)(2,1)S(1)} %get-tuple-element.122), channel_id=1, source_target_pairs={{4,0},{8,4},{12,8},{16,12},{20,16},{24,20},{28,24},{0,28},{5,1},{9... | collective-permute-start | bytes 2359304 | tf_op jit(solution)/shard_map/ppermute | solution.py:370
  5.8 132.4 %copy-start.3 = (s32[768,1]{1,0:T(8,128)}, s32[768,1]{1,0:T(8,128)S(1)}, u32[]{:S(2)}) copy-start(s32[768,1]{1,0:T(8,128)S(1)} %copy.23.ids_ref.refs_6_.refs_9_) | copy-start | bytes 9220
  5.9 9.2 %copy-start.55 = (bf16[1,16,2048]{2,1,0:T(8,128)(2,1)S(1)}, bf16[1,16,2048]{2,1,0:T(8,128)(2,1)}, u32[]{:S(2)}) copy-start(bf16[1,16,2048]{2,1,0:T(8,128)(2,1)} %param.12) | copy-start | bytes 196612
  6.0 43.3 %copy-start.54 = (bf16[1,768,2048]{2,1,0:T(8,128)(2,1)S(1)}, bf16[1,768,2048]{2,1,0:T(8,128)(2,1)}, u32[]{:S(2)}) copy-start(bf16[1,768,2048]{2,1,0:T(8,128)(2,1)} %param.13) | copy-start | bytes 9437188
  15.1 8.6 %collective-permute-start.5 = (bf16[16,2048]{1,0:T(8,128)(2,1)S(1)}, bf16[16,2048]{1,0:T(8,128)(2,1)S(1)}, u32[]{:S(2)}, u32[]{:S(2)}) collective-permute-start(bf16[16,2048]{1,0:T(8,128)(2,1)S(1)} %bitcast.45), channel_id=1, source_target_pairs={{0,3},{1,0},{2,1},{3,2},{4,7},{5,4},{6,5},{7,6},{8,11},{9,8},{10,9... | collective-permute-start | bytes 196616 | tf_op jit(solution)/shard_map/ppermute | solution.py:357
  19.4 9.4 %collective-permute-start.6 = (bf16[16,2048]{1,0:T(8,128)(2,1)S(1)}, bf16[16,2048]{1,0:T(8,128)(2,1)S(1)}, u32[]{:S(2)}, u32[]{:S(2)}) collective-permute-start(bf16[16,2048]{1,0:T(8,128)(2,1)S(1)} %bitcast.46), channel_id=1, source_target_pairs={{0,2},{1,3},{2,0},{3,1},{4,6},{5,7},{6,4},{7,5},{8,10},{9,11},{10,... | collective-permute-start | bytes 196616 | tf_op jit(solution)/shard_map/ppermute | solution.py:357
  19.4 9.4 %collective-permute-start.7 = (bf16[16,2048]{1,0:T(8,128)(2,1)S(1)}, bf16[16,2048]{1,0:T(8,128)(2,1)S(1)}, u32[]{:S(2)}, u32[]{:S(2)}) collective-permute-start(bf16[16,2048]{1,0:T(8,128)(2,1)S(1)} %bitcast.47), channel_id=1, source_target_pairs={{0,1},{1,2},{2,3},{3,0},{4,5},{5,6},{6,7},{7,4},{8,9},{9,10},{10,1... | collective-permute-start | bytes 196616 | tf_op jit(solution)/shard_map/ppermute | solution.py:357
  20.4 19.9 %collective-permute-start.3 = (bf16[192,4096]{1,0:T(8,128)(2,1)S(1)}, bf16[192,4096]{1,0:T(8,128)(2,1)S(1)}, u32[]{:S(2)}, u32[]{:S(2)}) collective-permute-start(bf16[192,4096]{1,0:T(8,128)(2,1)S(1)} %slice_bitcast_fusion), channel_id=1, source_target_pairs={{4,0},{8,4},{12,8},{16,12},{20,16},{24,20},{28,24},{0,28},{5,1},{9... | collective-permute-start | bytes 4718600 | tf_op jit(solution)/shard_map/ppermute | solution.py:370
  22.4 27.2 %collective-permute-start.2 = (bf16[192,2048]{1,0:T(8,128)(2,1)S(1)}, bf16[192,2048]{1,0:T(8,128)(2,1)S(1)}, u32[]{:S(2)}, u32[]{:S(2)}) collective-permute-start(bf16[192,2048]{1,0:T(8,128)(2,1)S(1)} %collective-permute-done.refs_0_), channel_id=1, source_target_pairs={{1,0},{2,1},{3,2},{5,4},{6,5},{7,6},{9,8},{10,9},{11,10},{13,12},{... | collective-permute-start | bytes 2359304 | tf_op jit(solution)/shard_map/ppermute | solution.py:387
  23.7 26.7 %collective-permute-start.1 = (bf16[192,2048]{1,0:T(8,128)(2,1)S(1)}, bf16[192,2048]{1,0:T(8,128)(2,1)S(1)}, u32[]{:S(2)}, u32[]{:S(2)}) collective-permute-start(bf16[192,2048]{1,0:T(8,128)(2,1)S(1)} %collective-permute-done.refs_0_), channel_id=1, source_target_pairs={{0,1},{1,2},{2,3},{4,5},{5,6},{6,7},{8,9},{9,10},{10,11},{12,13},{... | collective-permute-start | bytes 2359304 | tf_op jit(solution)/shard_map/ppermute | solution.py:386
  40.3 38.2 %collective-permute-start.10 = (bf16[192,4096]{1,0:T(8,128)(2,1)S(1)}, bf16[192,4096]{1,0:T(8,128)(2,1)S(1)}, u32[]{:S(2)}, u32[]{:S(2)}) collective-permute-start(bf16[192,4096]{1,0:T(8,128)(2,1)S(1)} %collective-permute-done.3.refs_1_), channel_id=1, source_target_pairs={{1,0},{2,1},{3,2},{5,4},{6,5},{7,6},{9,8},{10,9},{11,10},{13,12},{... | collective-permute-start | bytes 4718600 | tf_op jit(solution)/shard_map/ppermute | solution.py:387
  41.6 38.2 %collective-permute-start.9 = (bf16[192,4096]{1,0:T(8,128)(2,1)S(1)}, bf16[192,4096]{1,0:T(8,128)(2,1)S(1)}, u32[]{:S(2)}, u32[]{:S(2)}) collective-permute-start(bf16[192,4096]{1,0:T(8,128)(2,1)S(1)} %collective-permute-done.3.refs_1_), channel_id=1, source_target_pairs={{0,1},{1,2},{2,3},{4,5},{5,6},{6,7},{8,9},{9,10},{10,11},{12,13},{... | collective-permute-start | bytes 4718600 | tf_op jit(solution)/shard_map/ppermute | solution.py:386
  46.7 20.4 %collective-permute-start.4 = (bf16[192,2048]{1,0:T(8,128)(2,1)S(1)}, bf16[192,2048]{1,0:T(8,128)(2,1)S(1)}, u32[]{:S(2)}, u32[]{:S(2)}) collective-permute-start(bf16[192,2048]{1,0:T(8,128)(2,1)S(1)} %get-tuple-element.63), channel_id=1, source_target_pairs={{4,0},{8,4},{12,8},{16,12},{20,16},{24,20},{28,24},{0,28},{5,1},{9... | collective-permute-start | bytes 2359304 | tf_op jit(solution)/shard_map/ppermute | solution.py:370
  49.4 35.9 %copy-start.7 = (bf16[1,16,2048]{2,1,0:T(8,128)(2,1)S(1)}, bf16[1,16,2048]{2,1,0:T(8,128)(2,1)}, u32[]{:S(2)}) copy-start(bf16[1,16,2048]{2,1,0:T(8,128)(2,1)} %param.11) | copy-start | bytes 196612
  50.3 66.7 %copy-start.10 = (bf16[192,2048]{1,0:T(8,128)(2,1)}, bf16[192,2048]{1,0:T(8,128)(2,1)S(1)}, u32[]{:S(2)}) copy-start(bf16[192,2048]{1,0:T(8,128)(2,1)S(1)} %collective-permute-done.2.refs_0_) | copy-start | bytes 2359300
  50.3 53.5 %collective-permute-start.19 = (bf16[768,256]{1,0:T(8,128)(2,1)S(1)}, bf16[768,256]{1,0:T(8,128)(2,1)S(1)}, u32[]{:S(2)}, u32[]{:S(2)}) collective-permute-start(bf16[768,256]{1,0:T(8,128)(2,1)S(1)} %bitcast.51), channel_id=1, source_target_pairs={{0,28},{4,24},{8,20},{12,16},{16,12},{20,8},{24,4},{28,0},{1,29},{... | collective-permute-start | bytes 1179656 | tf_op jit(solution)/shard_map/ppermute | solution.py:395
  50.5 53.9 %collective-permute-start.20 = (bf16[768,256]{1,0:T(8,128)(2,1)S(1)}, bf16[768,256]{1,0:T(8,128)(2,1)S(1)}, u32[]{:S(2)}, u32[]{:S(2)}) collective-permute-start(bf16[768,256]{1,0:T(8,128)(2,1)S(1)} %bitcast.52), channel_id=1, source_target_pairs={{0,28},{4,24},{8,20},{12,16},{16,12},{20,8},{24,4},{28,0},{1,29},{... | collective-permute-start | bytes 1179656 | tf_op jit(solution)/shard_map/ppermute | solution.py:396
  67.2 47.8 %collective-permute-start.18 = (bf16[384,2048]{1,0:T(8,128)(2,1)S(1)}, bf16[384,2048]{1,0:T(8,128)(2,1)S(1)}, u32[]{:S(2)}, u32[]{:S(2)}) collective-permute-start(bf16[384,2048]{1,0:T(8,128)(2,1)S(1)} %get-tuple-element.120), channel_id=1, source_target_pairs={{0,28},{4,24},{8,20},{12,16},{16,12},{20,8},{24,4},{28,0},{1,29},{... | collective-permute-start | bytes 4718600 | tf_op jit(solution)/shard_map/ppermute | solution.py:399
  78.5 38.6 %copy-start.8 = (bf16[192,4096]{1,0:T(8,128)(2,1)}, bf16[192,4096]{1,0:T(8,128)(2,1)S(1)}, u32[]{:S(2)}) copy-start(bf16[192,4096]{1,0:T(8,128)(2,1)S(1)} %collective-permute-done.10.refs_1_) | copy-start | bytes 4718596
  78.5 26.5 %collective-permute-start.13 = (bf16[192,2048]{1,0:T(8,128)(2,1)S(1)}, bf16[192,2048]{1,0:T(8,128)(2,1)}, u32[]{:S(2)}, u32[]{:S(2)}) collective-permute-start(bf16[192,2048]{1,0:T(8,128)(2,1)S(1)} %collective-permute-done.4.refs_2_), channel_id=1, source_target_pairs={{1,0},{2,1},{3,2},{5,4},{6,5},{7,6},{9,8},{10,9},{11,10},{13,12},{... | collective-permute-start | bytes 2359304 | tf_op jit(solution)/shard_map/ppermute | solution.py:387
  79.8 36.5 %collective-permute-start.12 = (bf16[192,2048]{1,0:T(8,128)(2,1)S(1)}, bf16[192,2048]{1,0:T(8,128)(2,1)}, u32[]{:S(2)}, u32[]{:S(2)}) collective-permute-start(bf16[192,2048]{1,0:T(8,128)(2,1)S(1)} %collective-permute-done.4.refs_2_), channel_id=1, source_target_pairs={{0,1},{1,2},{2,3},{4,5},{5,6},{6,7},{8,9},{9,10},{10,11},{12,13},{... | collective-permute-start | bytes 2359304 | tf_op jit(solution)/shard_map/ppermute | solution.py:386
  103.8 33.4 %copy-start.20 = (bf16[192,2048]{1,0:T(8,128)(2,1)}, bf16[192,2048]{1,0:T(8,128)(2,1)S(1)}, u32[]{:S(2)}) copy-start(bf16[192,2048]{1,0:T(8,128)(2,1)S(1)} %get-tuple-element.103.refs_3_) | copy-start | bytes 2359300
  103.8 107.8 %copy-start.12 = (bf16[768,256]{1,0:T(8,128)(2,1)}, bf16[768,256]{1,0:T(8,128)(2,1)S(1)}, u32[]{:S(2)}) copy-start(bf16[768,256]{1,0:T(8,128)(2,1)S(1)} %collective-permute-done.19.refs_10_.k_ref.refs_4_.refs_7_) | copy-start | bytes 1179652
  103.8 55.7 %collective-permute-start.22 = (bf16[384,2048]{1,0:T(8,128)(2,1)S(1)}, bf16[384,2048]{1,0:T(8,128)(2,1)S(1)}, u32[]{:S(2)}, u32[]{:S(2)}) collective-permute-start(bf16[384,2048]{1,0:T(8,128)(2,1)S(1)} %get-tuple-element.119), channel_id=1, source_target_pairs={{0,28},{4,24},{8,20},{12,16},{16,12},{20,8},{24,4},{28,0},{1,29},{... | collective-permute-start | bytes 4718600 | tf_op jit(solution)/shard_map/ppermute | solution.py:399
  104.3 33.9 %copy-start.15 = (bf16[768,256]{1,0:T(8,128)(2,1)}, bf16[768,256]{1,0:T(8,128)(2,1)S(1)}, u32[]{:S(2)}) copy-start(bf16[768,256]{1,0:T(8,128)(2,1)S(1)} %collective-permute-done.20.refs_11_.v_ref.refs_5_.refs_8_) | copy-start | bytes 1179652
  104.3 33.8 %collective-permute-start.15 = (bf16[192,2048]{1,0:T(8,128)(2,1)S(1)}, bf16[192,2048]{1,0:T(8,128)(2,1)S(1)}, u32[]{:S(2)}, u32[]{:S(2)}) collective-permute-start(bf16[192,2048]{1,0:T(8,128)(2,1)S(1)} %collective-permute-done.1.refs_3_), channel_id=1, source_target_pairs={{1,2},{2,3},{5,6},{6,7},{9,10},{10,11},{13,14},{14,15},{17,18},{18... | collective-permute-start | bytes 2359304 | tf_op jit(solution)/shard_map/ppermute | solution.py:386
  105.0 33.1 %collective-permute-start.8 = (bf16[192,2048]{1,0:T(8,128)(2,1)S(1)}, bf16[192,2048]{1,0:T(8,128)(2,1)S(1)}, u32[]{:S(2)}, u32[]{:S(2)}) collective-permute-start(bf16[192,2048]{1,0:T(8,128)(2,1)S(1)} %collective-permute-done.2.refs_0_), channel_id=1, source_target_pairs={{1,0},{2,1},{5,4},{6,5},{9,8},{10,9},{13,12},{14,13},{17,16},{18,1... | collective-permute-start | bytes 2359304 | tf_op jit(solution)/shard_map/ppermute | solution.py:387
  115.0 45.9 %collective-permute-start.11 = (bf16[192,4096]{1,0:T(8,128)(2,1)S(1)}, bf16[192,4096]{1,0:T(8,128)(2,1)S(1)}, u32[]{:S(2)}, u32[]{:S(2)}) collective-permute-start(bf16[192,4096]{1,0:T(8,128)(2,1)S(1)} %collective-permute-done.10.refs_1_), channel_id=1, source_target_pairs={{1,0},{2,1},{5,4},{6,5},{9,8},{10,9},{13,12},{14,13},{17,16},{18,1... | collective-permute-start | bytes 4718600 | tf_op jit(solution)/shard_map/ppermute | solution.py:387
  116.3 45.3 %collective-permute-start.16 = (bf16[192,4096]{1,0:T(8,128)(2,1)S(1)}, bf16[192,4096]{1,0:T(8,128)(2,1)S(1)}, u32[]{:S(2)}, u32[]{:S(2)}) collective-permute-start(bf16[192,4096]{1,0:T(8,128)(2,1)S(1)} %collective-permute-done.9.refs_4_), channel_id=1, source_target_pairs={{1,2},{2,3},{5,6},{6,7},{9,10},{10,11},{13,14},{14,15},{17,18},{18... | collective-permute-start | bytes 4718600 | tf_op jit(solution)/shard_map/ppermute | solution.py:386
  138.2 17.7 %copy-start.22 = (bf16[192,2048]{1,0:T(8,128)(2,1)}, bf16[192,2048]{1,0:T(8,128)(2,1)S(1)}, u32[]{:S(2)}) copy-start(bf16[192,2048]{1,0:T(8,128)(2,1)S(1)} %get-tuple-element.104.refs_4_) | copy-start | bytes 2359300
  157.5 37.2 %collective-permute-start.14 = (bf16[192,2048]{1,0:T(8,128)(2,1)}, bf16[192,2048]{1,0:T(8,128)(2,1)S(1)}, u32[]{:S(2)}, u32[]{:S(2)}) collective-permute-start(bf16[192,2048]{1,0:T(8,128)(2,1)} %collective-permute-done.13.refs_2_), channel_id=1, source_target_pairs={{1,0},{2,1},{5,4},{6,5},{9,8},{10,9},{13,12},{14,13},{17,16},{18,1... | collective-permute-start | bytes 2359304 | tf_op jit(solution)/shard_map/ppermute | solution.py:387
  158.8 35.9 %collective-permute-start.17 = (bf16[192,2048]{1,0:T(8,128)(2,1)}, bf16[192,2048]{1,0:T(8,128)(2,1)S(1)}, u32[]{:S(2)}, u32[]{:S(2)}) collective-permute-start(bf16[192,2048]{1,0:T(8,128)(2,1)} %collective-permute-done.12.refs_5_), channel_id=1, source_target_pairs={{1,2},{2,3},{5,6},{6,7},{9,10},{10,11},{13,14},{14,15},{17,18},{18... | collective-permute-start | bytes 2359304 | tf_op jit(solution)/shard_map/ppermute | solution.py:386
  159.5 66.8 %collective-permute-start.21 = (bf16[192,2048]{1,0:T(8,128)(2,1)S(1)}, bf16[192,2048]{1,0:T(8,128)(2,1)S(1)}, u32[]{:S(2)}, u32[]{:S(2)}) collective-permute-start(bf16[192,2048]{1,0:T(8,128)(2,1)S(1)} %collective-permute-done.8.rest_2_.refs_3_.refs_0_), channel_id=1, source_target_pairs={{1,0},{5,4},{9,8},{13,12},{17,16},{21,20},{25,24},{29,28}} | collective-permute-start | bytes 2359304 | tf_op jit(solution)/shard_map/ppermute | solution.py:387
  160.8 66.7 %collective-permute-start.25 = (bf16[192,2048]{1,0:T(8,128)(2,1)S(1)}, bf16[192,2048]{1,0:T(8,128)(2,1)S(1)}, u32[]{:S(2)}, u32[]{:S(2)}) collective-permute-start(bf16[192,2048]{1,0:T(8,128)(2,1)S(1)} %collective-permute-done.15.rest_1_.refs_6_.refs_2_.refs_3_), channel_id=1, source_target_pairs={{2,3},{6,7},{10,11},{14,15},{18,19},{22,23},{26,27},{30,31}} | collective-permute-start | bytes 2359304 | tf_op jit(solution)/shard_map/ppermute | solution.py:386
  165.5 31.7 %copy-start.5 = (s32[768,1]{1,0:T(8,128)S(1)}, s32[768,1]{1,0:T(8,128)}, u32[]{:S(2)}) copy-start(s32[768,1]{1,0:T(8,128)} %copy-done.3) | copy-start | bytes 9220
  165.5 31.7 %copy-start.17 = (bf16[768,256]{1,0:T(8,128)(2,1)S(1)}, bf16[768,256]{1,0:T(8,128)(2,1)}, u32[]{:S(2)}) copy-start(bf16[768,256]{1,0:T(8,128)(2,1)} %copy-done.15) | copy-start | bytes 1179652
  184.9 26.7 %copy-start.30 = (bf16[768,2048]{1,0:T(8,128)(2,1)}, bf16[768,2048]{1,0:T(8,128)(2,1)S(1)}, u32[]{:S(2)}) copy-start(bf16[768,2048]{1,0:T(8,128)(2,1)S(1)} %get-tuple-element.89.refs_3_.refs_6_) | copy-start | bytes 9437188
  184.9 66.0 %copy-start.52 = (f32[4,8,1,384]{3,2,1,0:T(1,128)}, f32[4,8,1,384]{3,2,1,0:T(1,128)S(1)}, u32[]{:S(2)}) copy-start(f32[4,8,1,384]{3,2,1,0:T(1,128)S(1)} %get-tuple-element.81.refs_8_.refs_11_) | copy-start | bytes 147460
  184.9 85.9 %collective-permute-start.28 = (f32[4,16,192]{2,1,0:T(8,128)S(1)}, f32[4,16,192]{2,1,0:T(8,128)}, u32[]{:S(2)}, u32[]{:S(2)}) collective-permute-start(f32[4,16,192]{2,1,0:T(8,128)S(1)} %get-tuple-element.102), channel_id=1, source_target_pairs={{0,1},{1,2},{2,3},{3,0},{4,5},{5,6},{6,7},{7,4},{8,9},{9,10},{10,1... | collective-permute-start | bytes 147464 | tf_op jit(solution)/shard_map/ppermute | solution.py:560
  194.7 77.4 %collective-permute-start.29 = (f32[4,16,192]{2,1,0:T(8,128)S(1)}, f32[4,16,192]{2,1,0:T(8,128)}, u32[]{:S(2)}, u32[]{:S(2)}) collective-permute-start(f32[4,16,192]{2,1,0:T(8,128)S(1)} %get-tuple-element.102), channel_id=1, source_target_pairs={{0,2},{1,3},{2,0},{3,1},{4,6},{5,7},{6,4},{7,5},{8,10},{9,11},{10,... | collective-permute-start | bytes 147464 | tf_op jit(solution)/shard_map/ppermute | solution.py:560
  194.7 78.3 %collective-permute-start.30 = (f32[4,16,192]{2,1,0:T(8,128)S(1)}, f32[4,16,192]{2,1,0:T(8,128)}, u32[]{:S(2)}, u32[]{:S(2)}) collective-permute-start(f32[4,16,192]{2,1,0:T(8,128)S(1)} %get-tuple-element.102), channel_id=1, source_target_pairs={{0,3},{1,0},{2,1},{3,2},{4,7},{5,4},{6,5},{7,6},{8,11},{9,8},{10,9... | collective-permute-start | bytes 147464 | tf_op jit(solution)/shard_map/ppermute | solution.py:560
  197.1 1.9 copy-start.35
  200.1 11.4 %copy-start.36 = (bf16[768,2048]{1,0:T(8,128)(2,1)S(1)}, bf16[768,2048]{1,0:T(8,128)(2,1)}, u32[]{:S(2)}) copy-start(bf16[768,2048]{1,0:T(8,128)(2,1)} %copy-done.34) | copy-start | bytes 9437188
  211.6 1.9 copy-start.31
  226.3 22.6 %copy-start.46 = (f32[768,256]{1,0:T(8,128)}, f32[768,256]{1,0:T(8,128)S(1)}, u32[]{:S(2)}) copy-start(f32[768,256]{1,0:T(8,128)S(1)} %get-tuple-element.99.refs_10_) | copy-start | bytes 2359300
  226.3 22.6 %copy-start.48 = (f32[768,256]{1,0:T(8,128)}, f32[768,256]{1,0:T(8,128)S(1)}, u32[]{:S(2)}) copy-start(f32[768,256]{1,0:T(8,128)S(1)} %get-tuple-element.100.refs_11_) | copy-start | bytes 2359300
  226.3 52.4 %collective-permute-start.23 = (bf16[192,4096]{1,0:T(8,128)(2,1)S(1)}, bf16[192,4096]{1,0:T(8,128)(2,1)S(1)}, u32[]{:S(2)}, u32[]{:S(2)}) collective-permute-start(bf16[192,4096]{1,0:T(8,128)(2,1)S(1)} %collective-permute-done.11.rest_5_.refs_4_.refs_1_), channel_id=1, source_target_pairs={{1,0},{5,4},{9,8},{13,12},{17,16},{21,20},{25,24},{29,28}} | collective-permute-start | bytes 4718600 | tf_op jit(solution)/shard_map/ppermute | solution.py:387
  227.6 51.1 %copy-start.1 = (bf16[192,2048]{1,0:T(8,128)(2,1)}, bf16[192,2048]{1,0:T(8,128)(2,1)S(1)}, u32[]{:S(2)}) copy-start(bf16[192,2048]{1,0:T(8,128)(2,1)S(1)} %collective-permute-done.25.refs_13_.refs_6_.refs_9_) | copy-start | bytes 2359300
  227.6 51.1 %collective-permute-start.26 = (bf16[192,4096]{1,0:T(8,128)(2,1)S(1)}, bf16[192,4096]{1,0:T(8,128)(2,1)S(1)}, u32[]{:S(2)}, u32[]{:S(2)}) collective-permute-start(bf16[192,4096]{1,0:T(8,128)(2,1)S(1)} %collective-permute-done.16.rest_4_.refs_7_.refs_3_.refs_4_), channel_id=1, source_target_pairs={{2,3},{6,7},{10,11},{14,15},{18,19},{22,23},{26,27},{30,31}} | collective-permute-start | bytes 4718600 | tf_op jit(solution)/shard_map/ppermute | solution.py:386
  230.9 19.9 %copy-start.37 = (bf16[768,2048]{1,0:T(8,128)(2,1)S(1)}, bf16[768,2048]{1,0:T(8,128)(2,1)}, u32[]{:S(2)}) copy-start(bf16[768,2048]{1,0:T(8,128)(2,1)} %copy-done.34) | copy-start | bytes 9437188
  258.1 15.8 %copy-start.21 = (bf16[192,2048]{1,0:T(8,128)(2,1)S(1)}, bf16[192,2048]{1,0:T(8,128)(2,1)}, u32[]{:S(2)}) copy-start(bf16[192,2048]{1,0:T(8,128)(2,1)} %copy-done.20) | copy-start | bytes 2359300
  270.8 7.9 %copy-start.40 = (f32[768,256]{1,0:T(8,128)}, f32[768,256]{1,0:T(8,128)S(1)}, u32[]{:S(2)}) copy-start(f32[768,256]{1,0:T(8,128)S(1)} %get-tuple-element.112.refs_13_) | copy-start | bytes 2359300
  270.8 7.9 %copy-start.26 = (f32[16,2048]{1,0:T(8,128)}, f32[16,2048]{1,0:T(8,128)S(1)}, u32[]{:S(2)}) copy-start(f32[16,2048]{1,0:T(8,128)S(1)} %get-tuple-element.101.refs_11_.refs_15_) | copy-start | bytes 393220
  270.8 23.1 %collective-permute-start.24 = (bf16[192,2048]{1,0:T(8,128)(2,1)S(1)}, bf16[192,2048]{1,0:T(8,128)(2,1)S(1)}, u32[]{:S(2)}, u32[]{:S(2)}) collective-permute-start(bf16[192,2048]{1,0:T(8,128)(2,1)S(1)} %collective-permute-done.14.refs_10_.refs_5_.refs_2_), channel_id=1, source_target_pairs={{1,0},{5,4},{9,8},{13,12},{17,16},{21,20},{25,24},{29,28}} | collective-permute-start | bytes 2359304 | tf_op jit(solution)/shard_map/ppermute | solution.py:387
  272.1 21.8 %collective-permute-start.27 = (bf16[192,2048]{1,0:T(8,128)(2,1)S(1)}, bf16[192,2048]{1,0:T(8,128)(2,1)S(1)}, u32[]{:S(2)}, u32[]{:S(2)}) collective-permute-start(bf16[192,2048]{1,0:T(8,128)(2,1)S(1)} %collective-permute-done.17.refs_9_.refs_8_.refs_5_), channel_id=1, source_target_pairs={{2,3},{6,7},{10,11},{14,15},{18,19},{22,23},{26,27},{30,31}} | collective-permute-start | bytes 2359304 | tf_op jit(solution)/shard_map/ppermute | solution.py:386
  295.0 7.8 %copy-start.6 = (s32[768,1]{1,0:T(8,128)S(1)}, s32[768,1]{1,0:T(8,128)}, u32[]{:S(2)}) copy-start(s32[768,1]{1,0:T(8,128)} %copy-done.3) | copy-start | bytes 9220
  295.0 7.8 %copy-start.14 = (bf16[768,256]{1,0:T(8,128)(2,1)S(1)}, bf16[768,256]{1,0:T(8,128)(2,1)}, u32[]{:S(2)}) copy-start(bf16[768,256]{1,0:T(8,128)(2,1)} %copy-done.12) | copy-start | bytes 1179652
  295.0 7.8 %copy-start.19 = (bf16[768,256]{1,0:T(8,128)(2,1)S(1)}, bf16[768,256]{1,0:T(8,128)(2,1)}, u32[]{:S(2)}) copy-start(bf16[768,256]{1,0:T(8,128)(2,1)} %copy-done.15) | copy-start | bytes 1179652
  295.0 7.8 %copy-start.27 = (f32[16,2048]{1,0:T(8,128)S(1)}, f32[16,2048]{1,0:T(8,128)}, u32[]{:S(2)}) copy-start(f32[16,2048]{1,0:T(8,128)} %copy-done.26) | copy-start | bytes 393220
  295.0 7.8 %copy-start.41 = (f32[768,256]{1,0:T(8,128)S(1)}, f32[768,256]{1,0:T(8,128)}, u32[]{:S(2)}) copy-start(f32[768,256]{1,0:T(8,128)} %copy-done.40) | copy-start | bytes 2359300
  295.0 7.8 %copy-start.43 = (f32[768,256]{1,0:T(8,128)S(1)}, f32[768,256]{1,0:T(8,128)}, u32[]{:S(2)}) copy-start(f32[768,256]{1,0:T(8,128)} %copy-done.42) | copy-start | bytes 2359300
  295.0 7.8 %copy-start.53 = (f32[4,8,1,384]{3,2,1,0:T(1,128)S(1)}, f32[4,8,1,384]{3,2,1,0:T(1,128)}, u32[]{:S(2)}) copy-start(f32[4,8,1,384]{3,2,1,0:T(1,128)} %copy-done.52) | copy-start | bytes 147460
  302.9 1.9 copy-start.33
  (26 other events, 30.7 us)

commit v3 on v2

v3 whole, which is shorter than its diff:
```python
import functools
import math

import jax
import jax.numpy as jnp
import numpy as np
from jax import lax
from jax.experimental import pallas as pl
from jax.experimental.pallas import tpu as pltpu
from jax.sharding import PartitionSpec as P

HEAD_SIZE = 128
MASKED = -1e30
LOG2E = math.log2(math.e)
VMEM_BYTES = 40 * 2**20
KEY_BLOCK = 192
QKV_AFTER = 1
FLOPS_PER_MICRO = 1.0e9

adapter_scale = 2.0


def dot_nt(a, b):
    return lax.dot_general(a, b, (((1,), (1,)), ((), ())), preferred_element_type=jnp.float32)


def dot_nn(a, b):
    return lax.dot_general(a, b, (((1,), (0,)), ((), ())), preferred_element_type=jnp.float32)


def dot_tn(a, b):
    return lax.dot_general(a, b, (((0,), (0,)), ((), ())), preferred_element_type=jnp.float32)


def three_parts(a):
    high = a.astype(jnp.bfloat16)
    rest = a - high.astype(jnp.float32)
    middle = rest.astype(jnp.bfloat16)
    low = (rest - middle.astype(jnp.float32)).astype(jnp.bfloat16)
    return jnp.concatenate([high, middle, low], axis=0)


def folded(a):
    rows = a.shape[0] // 3
    return a[:rows] + a[rows : 2 * rows] + a[2 * rows :]


def stacked_heads(a):
    count = a.shape[1] // HEAD_SIZE
    return jnp.concatenate(
        [a[:, h * HEAD_SIZE : (h + 1) * HEAD_SIZE] for h in range(count)], axis=0
    )


def key_blocks(first_key, row_start, rows):
    return first_key // KEY_BLOCK, (row_start + rows + KEY_BLOCK - 1) // KEY_BLOCK


def fill_bias(bias_ref, ids_ref, row_info_ref, low, high):
    lanes = bias_ref.shape[1]

    def one(i, _):
        at = pl.multiple_of(i * KEY_BLOCK, KEY_BLOCK)
        key_pos = at + lax.broadcasted_iota(jnp.int32, (KEY_BLOCK, lanes), 0)
        allowed = (key_pos <= row_info_ref[0, 0:1, :]) & (
            ids_ref[pl.ds(at, KEY_BLOCK), :] == row_info_ref[0, 1:2, :]
        )
        bias_ref[pl.ds(at, KEY_BLOCK), :] = jnp.where(allowed, 0.0, MASKED)
        return 0

    lax.fori_loop(low, high, one, 0)


def forward_kernel(
    grain, scalars_ref, q_ref, k_ref, v_ref, ids_ref, row_info_ref, down_ref, *rest
):
    ctx_ref, lse_ref, rank_ref, bias_ref, scores_ref, context_ref = rest[-6:]
    step = pl.program_id(1)
    rows = q_ref.shape[0]
    heads = q_ref.shape[1] // HEAD_SIZE
    row_start = pl.program_id(0) * rows
    first_key = scalars_ref[scalars_ref.shape[0] - k_ref.shape[0] // grain + row_start // grain]
    low, high = key_blocks(first_key, row_start, rows)
    lanes = heads * rows
    chunk = bias_ref.shape[1]

    @pl.when(step == 0)
    def _():
        fill_bias(bias_ref, ids_ref, row_info_ref, low, high)
        rank_ref[...] = jnp.zeros_like(rank_ref)

    stacked = stacked_heads(q_ref[...])

    def weigh(i, carry):
        top, weight = carry
        at = pl.multiple_of(i * KEY_BLOCK, KEY_BLOCK)
        keys = k_ref[pl.ds(at, KEY_BLOCK), :]
        bias = bias_ref[pl.ds(at, KEY_BLOCK), :]
        tops, weights = [], []
        for c in range(0, lanes, chunk):
            scores = dot_nt(keys, stacked[c : c + chunk]) * (LOG2E / math.sqrt(HEAD_SIZE)) + bias
            scores_ref[pl.ds(at, KEY_BLOCK), c : c + chunk] = scores
            old = top[:, c : c + chunk]
            new = jnp.maximum(old, jnp.max(scores, axis=0, keepdims=True))
            tops.append(new)
            weights.append(
                weight[:, c : c + chunk] * jnp.exp2(old - new)
                + jnp.sum(jnp.exp2(scores - new), axis=0, keepdims=True)
            )
        return jnp.concatenate(tops, axis=1), jnp.concatenate(weights, axis=1)

    top, weight = lax.fori_loop(
        low,
        high,
        weigh,
        (jnp.full((1, lanes), 2 * MASKED, jnp.float32), jnp.zeros((1, lanes), jnp.float32)),
    )
    lse = top + jnp.log(weight) * LOG2E
    lse_ref[0, 0] = lse
    context_ref[...] = jnp.zeros_like(context_ref)

    def add_values(i, _):
        at = pl.multiple_of(i * KEY_BLOCK, KEY_BLOCK)
        values = v_ref[pl.ds(at, KEY_BLOCK), :]
        for c in range(0, lanes, chunk):
            scores = scores_ref[pl.ds(at, KEY_BLOCK), c : c + chunk]
            probs = jnp.exp2(scores - lse[:, c : c + chunk]).astype(jnp.bfloat16)
            context_ref[:, c : c + chunk] += dot_tn(values, probs)
        return 0

    lax.fori_loop(low, high, add_values, 0)
    context = context_ref[...].T.astype(jnp.bfloat16)
    for h in range(heads):
        part = context[h * rows : (h + 1) * rows]
        ctx_ref[:, h * HEAD_SIZE : (h + 1) * HEAD_SIZE] = part
        rank_ref[0] += dot_nt(down_ref[:, h * HEAD_SIZE : (h + 1) * HEAD_SIZE], part)


def fetch(choice, groups, x_ref, sems):
    for c, parts in enumerate(groups):

        @pl.when(choice == c)
        def _(parts=parts):
            copies = []
            at = 0
            for p, (part, first, width) in enumerate(parts):
                copies.append(
                    pltpu.make_async_copy(
                        part.at[:, pl.ds(first, width)], x_ref.at[:, pl.ds(at, width)], sems.at[p]
                    )
                )
                at += width
            for copy in copies:
                copy.start()
            for copy in copies:
                copy.wait()


def rank_product(up_ref, x_ref, first_column):
    local = up_ref.shape[2]
    width = x_ref.shape[1]
    total = None
    for j in range(width // local):
        part = dot_nt(up_ref[first_column // local + j], x_ref[:, j * local : (j + 1) * local])
        total = part if total is None else total + part
    return total


def project(x_ref, w_ref, acc):
    width = x_ref.shape[1]
    for at in range(0, width, 4096):
        to = min(at + 4096, width)
        acc = acc + dot_nt(x_ref[:, at:to], w_ref[:, at:to])
    return acc


def rank_term(rank, down):
    return adapter_scale * dot_tn(rank, jnp.concatenate([down, down, down], axis=0))


def projection_kernel(spec, scalars_ref, *refs):
    at_choice, places, before, ends, after = spec
    refs = list(refs)

    def take(count):
        taken = refs[:count]
        del refs[:count]
        return taken

    groups = [
        [(ref, *place) for ref, place in zip(take(len(group)), group)] for group in places
    ]
    first_column = sum(columns for _, columns in places[0][:before])
    w_ref, up_ref, down_ref = take(3)
    if before:
        acc_in, rank_in = take(2)
    take(after)
    out_ref, rank_out = take(2)
    if ends:
        local_out = take(1)[0]
    x_ref, sems = take(2)
    if ends:
        parts_ref, local_ref = take(2)
    step = pl.program_id(0)

    @pl.when(step == 0)
    def _():
        fetch(scalars_ref[at_choice], [parts[before:] for parts in groups], x_ref, sems)
        rank = rank_product(up_ref, x_ref, first_column)
        rank_out[...] = rank + rank_in[...] if before else rank
        if ends:
            parts_ref[...] = three_parts(rank_out[...])
            for c, parts in enumerate(groups):
                at = 0
                for part, first, width in parts:
                    mine = scalars_ref[0] - at

                    @pl.when((scalars_ref[at_choice] == c) & (mine >= 0) & (mine < width))
                    def _(part=part, mine=mine, first=first):
                        copy = pltpu.make_async_copy(
                            part.at[:, pl.ds(pl.multiple_of(mine + first, 128), local_ref.shape[1])],
                            local_ref,
                            sems.at[0],
                        )
                        copy.start()
                        copy.wait()

                    at += width

    if ends:
        begin = rank_term(parts_ref[...], down_ref[...])
        if before:
            begin = begin + acc_in[...]
    else:
        begin = acc_in[...] if before else jnp.zeros(out_ref.shape, jnp.float32)
    out_ref[...] = project(x_ref, w_ref, begin).astype(out_ref.dtype)
    if ends:
        tile = local_out.shape[1]
        local_out[...] = local_ref[:, pl.ds(pl.multiple_of(step * tile, tile), tile)]


def up_map_kernel(count, scalars_ref, *refs):
    ranks = refs[:count]
    columns = refs[count : 2 * count]
    out_ref = refs[2 * count + 1]
    rows_total = sum(c.shape[0] for c in columns)
    scale = adapter_scale / math.sqrt(rows_total * (count + 1) // count)
    total = None
    for rank, column in zip(ranks, columns):
        part = folded(dot_nn(three_parts(rank[0]), column[...]))
        total = part if total is None else total + part
    out_ref[...] = scale * total


def backward_kernel(spec, scalars_ref, *refs):
    here, grain, first, last, after = spec
    refs = list(refs)

    def take(count):
        taken = refs[:count]
        del refs[:count]
        return taken

    if last:
        local_ref, rank_ctx_ref, um_in = take(3)
    grad_ref, rank_in, q_ref, ctx_ref, k_ref, v_ref, ids_ref, row_info_ref, lse_ref = take(9)
    if not first:
        _, dk_in, dv_in, dm_in = take(4)
    take(after)
    dq_ref, dk_ref, dv_ref, dm_ref = take(4)
    if last:
        um_ref = take(1)[0]
    bias_ref, parts_ref, dk_sum, dv_sum, probs_ref, grad_scores_ref, grad_q_ref = take(7)

    step = pl.program_id(0)
    total = k_ref.shape[0]
    rows = q_ref.shape[0]
    heads = q_ref.shape[1] // HEAD_SIZE
    lanes = heads * rows
    chunk = bias_ref.shape[1]
    row_start = scalars_ref[here] * rows
    first_key = scalars_ref[scalars_ref.shape[0] - total // grain + row_start // grain]
    low, high = key_blocks(first_key, row_start, rows)
    gradient_scale = adapter_scale / math.sqrt(total)
    inv_scale = 1.0 / math.sqrt(HEAD_SIZE)

    @pl.when(step == 0)
    def _():
        parts_ref[...] = three_parts(rank_in[...])
        fill_bias(bias_ref, ids_ref, row_info_ref, low, high)

    if first:
        dk_sum[...] = jnp.zeros_like(dk_sum)
        dv_sum[...] = jnp.zeros_like(dv_sum)
    else:
        dk_sum[...] = dk_in[...]
        dv_sum[...] = dv_in[...]
    grad_q_ref[...] = jnp.zeros_like(grad_q_ref)
    queries = stacked_heads(q_ref[...])
    grads = stacked_heads(grad_ref[...])
    delta = jnp.sum(
        (grads.astype(jnp.float32) * stacked_heads(ctx_ref[...]).astype(jnp.float32)).T,
        axis=0,
        keepdims=True,
    )

    def one(i, _):
        at = pl.multiple_of(i * KEY_BLOCK, KEY_BLOCK)
        keys = k_ref[pl.ds(at, KEY_BLOCK), :]
        values = v_ref[pl.ds(at, KEY_BLOCK), :]
        bias = bias_ref[pl.ds(at, KEY_BLOCK), :]
        for c in range(0, lanes, chunk):
            here = slice(c, c + chunk)
            scores = dot_nt(keys, queries[here]) * (LOG2E * inv_scale) + bias
            probs = jnp.exp2(scores - lse_ref[0, 0, :, here])
            grad_probs = dot_nt(values, grads[here])
            probs_ref[:, here] = probs.astype(jnp.bfloat16)
            grad_scores_ref[:, here] = (probs * (grad_probs - delta[:, here])).astype(jnp.bfloat16)
        grad_scores = grad_scores_ref[...]
        dk_sum[pl.ds(at, KEY_BLOCK), :] += dot_nn(grad_scores, queries) * inv_scale
        dv_sum[pl.ds(at, KEY_BLOCK), :] += dot_nn(probs_ref[...], grads)
        grad_q_ref[...] += dot_tn(keys, grad_scores)
        return 0

    lax.fori_loop(low, high, one, 0)
    dk_ref[...] = dk_sum[...].astype(dk_ref.dtype)
    dv_ref[...] = dv_sum[...].astype(dv_ref.dtype)
    grad_q = (grad_q_ref[...] * inv_scale).T.astype(jnp.bfloat16)
    for h in range(heads):
        dq_ref[:, h * HEAD_SIZE : (h + 1) * HEAD_SIZE] = grad_q[h * rows : (h + 1) * rows]

    down_part = gradient_scale * folded(dot_nn(parts_ref[...], ctx_ref[...]))
    dm_ref[...] = down_part if first else dm_in[...] + down_part
    if last:
        um_ref[...] = um_in[...] + gradient_scale * folded(
            dot_nn(three_parts(rank_ctx_ref[0]), local_ref[...])
        )


def options(name, micros, axes=1):
    return dict(
        compiler_params=pltpu.CompilerParams(
            dimension_semantics=("arbitrary",) * axes, vmem_limit_bytes=VMEM_BYTES
        ),
        cost_estimate=pl.CostEstimate(
            flops=int(micros * FLOPS_PER_MICRO), bytes_accessed=1, transcendentals=0
        ),
        name=name,
    )


ANYWHERE = pl.BlockSpec(memory_space=pl.ANY)


def per_device(
    handoff_gradient,
    output_weight,
    adapter_down,
    adapter_up,
    stored_queries,
    stored_keys,
    stored_values,
    segments,
):
    pipe_count = lax.axis_size("pipe")
    line = lax.axis_size("fsdp")
    member = lax.axis_index("fsdp")
    shard = handoff_gradient.shape[1]
    total = shard * line
    model_width = handoff_gradient.shape[2]
    query_width = stored_queries.shape[2]
    kv_width = stored_keys.shape[2]
    rank = adapter_down.shape[1]
    query_heads = query_width // HEAD_SIZE
    kv_heads = kv_width // HEAD_SIZE
    group = query_heads // kv_heads
    local_width = adapter_up.shape[2]
    bf16, f32 = jnp.bfloat16, jnp.float32
    weight = output_weight[0]
    down = adapter_down[0]

    def spread(block):
        blocks = [block]
        for d in range(1, line):
            route = [(i, (i + d) % line) for i in range(line)]
            blocks.append(lax.ppermute(block, "fsdp", route))
        turned = jnp.stack(blocks[::-1] + blocks[::-1])
        return lax.dynamic_slice_in_dim(turned, line - 1 - member, line, 0)

    from_next = [((i + 1) % pipe_count, i) for i in range(pipe_count)]
    mirrored = [(i, pipe_count - 1 - i) for i in range(pipe_count)]
    widths = [model_width // 2, model_width // 2]
    own, at = [], 0
    for width in widths:
        part = handoff_gradient[0, :, at : at + width]
        if own:
            part, _ = lax.optimization_barrier((part, own[-1]))
        else:
            first_part = part
        own.append(lax.ppermute(part, "pipe", from_next))
        at += width
    saved = lax.optimization_barrier(
        (stored_queries[0], stored_keys[0], stored_values[0], first_part)
    )[:3]
    packed = jnp.concatenate(saved, axis=1)
    up_all = spread(lax.optimization_barrier((adapter_up[0], packed))[0])
    rising, falling = [own], [own]
    crossing = {}

    def after(part, token):
        return part if token is None else lax.optimization_barrier((part, token))[0]

    def pass_on(token):
        k = len(rising)
        if k >= line:
            return
        up_pairs = [(i, i + 1) for i in range(k - 1, line - 1)]
        down_pairs = [(i + 1, i) for i in range(line - k)]
        rising.append([lax.ppermute(after(p, token), "fsdp", up_pairs) for p in rising[-1]])
        falling.append([lax.ppermute(after(p, token), "fsdp", down_pairs) for p in falling[-1]])

    def cross(piece, kind, token):
        routes = {
            "near": [(1, 0), (2, 3)],
            "middle": [(1, 2), (2, 1)],
            "far": [(1, 3), (2, 0)],
        }
        rose, fell = rising[1][piece], falling[1][piece]
        first = member == (2 if kind == "near" else 1)
        part = jnp.where(first, rose, fell)
        crossing.setdefault(kind, []).append(
            lax.ppermute(after(part, token), "fsdp", routes[kind])
        )

    pass_on(None)
    packed, _ = lax.optimization_barrier((packed, own[QKV_AFTER]))
    packed = lax.ppermute(packed, "pipe", mirrored)

    def arrival(device, order):
        found = []
        for k in range(1, line):
            if device >= k:
                found.append((k, True, device - k))
            if device + k < line:
                found.append((k, False, device + k))
        return found[order]

    def groups_of(order):
        if order < 0:
            return ["own"]
        return sorted({carrier(d, order) for d in range(line)})

    def carrier(device, order):
        if order < 0:
            return "own"
        k, rises, _ = arrival(device, order)
        if line == 4 and k > 1:
            return "far" if k == 3 else "near" if device in (0, 3) else "middle"
        return f"{'rising' if rises else 'falling'} {k}"

    def choices(order):
        groups = []
        for name in groups_of(order):
            if name == "own":
                parts = own
            elif name in crossing:
                parts = crossing[name]
            else:
                way, k = name.split()
                parts = (rising if way == "rising" else falling)[int(k)]
            groups.append([(part, 0, part.shape[1]) for part in parts])
        return groups

    rows_f = total // 4
    grain = math.gcd(rows_f, shard)
    table = np.zeros((line, 1 + 2 * line), np.int32)
    for d in range(line):
        table[d, 0] = d * local_width
        for order in range(-1, line - 1):
            owner = d if order < 0 else arrival(d, order)[2]
            at = 3 + 2 * order
            table[d, at : at + 2] = groups_of(order).index(carrier(d, order)), owner
    ids = segments[0]
    first_keys = jnp.sum(ids[None, :] < ids[::grain, None], axis=1, dtype=jnp.int32)
    scalars = jnp.concatenate(
        [lax.dynamic_index_in_dim(jnp.asarray(table), member, 0, keepdims=False), first_keys]
    )

    tile_p = min(512, query_width)

    def projection(order, after, low=0, high=None, sums=()):
        groups = choices(order)
        high = len(groups[0]) if high is None else high
        ends = high == len(groups[0])
        groups = [parts[:high] for parts in groups]
        offsets = [0]
        for _, _, columns in groups[0]:
            offsets.append(offsets[-1] + columns)
        places = [[(first, columns) for _, first, columns in parts] for parts in groups]
        width = offsets[high] - offsets[low]
        block, odd = divmod(offsets[low], width)
        assert odd == 0
        operands = [part for parts in groups for part, _, _ in parts]
        in_specs = [ANYWHERE] * len(operands)
        rank_spec = pl.BlockSpec((rank, shard), lambda n, s: (0, 0))
        tile_spec = pl.BlockSpec((shard, tile_p), lambda n, s: (0, n))
        operands += [weight, up_all, down, *sums, *after]
        in_specs += [
            pl.BlockSpec((tile_p, width), lambda n, s: (n, block)),
            pl.BlockSpec((line, rank, local_width), lambda n, s: (0, 0, 0)),
            pl.BlockSpec((rank, tile_p), lambda n, s: (0, n)),
        ]
        in_specs += [tile_spec, rank_spec][: len(sums)] + [ANYWHERE] * len(after)
        out_shape = [
            jax.ShapeDtypeStruct((shard, query_width), bf16 if ends else f32),
            jax.ShapeDtypeStruct((rank, shard), f32),
        ]
        out_specs = [tile_spec, rank_spec]
        scratch = [
            pltpu.VMEM((shard, width), bf16),
            pltpu.SemaphoreType.DMA((high - low,)),
        ]
        if ends:
            out_shape.append(jax.ShapeDtypeStruct((shard, local_width), bf16))
            out_specs.append(
                pl.BlockSpec((shard, local_width * tile_p // query_width), lambda n, s: (0, n))
            )
            scratch.append(pltpu.VMEM((3 * rank, shard), bf16))
            scratch.append(pltpu.VMEM((shard, local_width), bf16))
        return pl.pallas_call(
            functools.partial(
                projection_kernel, (3 + 2 * order, places, low, ends, len(after))
            ),
            grid_spec=pltpu.PrefetchScalarGridSpec(
                num_scalar_prefetch=1,
                grid=(query_width // tile_p,),
                in_specs=in_specs,
                out_specs=out_specs,
                scratch_shapes=scratch,
            ),
            out_shape=out_shape,
            **options(f"projection_{order + 1}_{high}", 18 * width / model_width),
        )(scalars, *operands)

    projected = [projection(-1, [])]
    done_before = projected[0][1]
    if line == 4:
        cross(0, "near", done_before)
        cross(0, "middle", done_before)
        cross(1, "near", done_before)
        cross(1, "middle", done_before)
    else:
        pass_on(done_before)
    if line > 2:
        projected.append(projection(0, [done_before]))
        done_before = projected[1][1]

    ids_column = ids[:, None]
    lanes_f = group * rows_f
    chunk_f = 2 * rows_f if group % 2 == 0 else rows_f

    def row_info(rows, heads):
        pos = jnp.arange(total, dtype=jnp.int32).reshape(total // rows, 1, rows)
        row_ids = ids.reshape(total // rows, 1, rows)
        both = jnp.concatenate([pos, row_ids], axis=1)
        return jnp.tile(both, (1, 1, heads))

    wide = group * HEAD_SIZE
    pins = [crossing["near"][0], crossing["middle"][0]] if line == 4 else []
    key_at, value_at = query_heads, query_heads + kv_heads
    context, lse, rank_portion = pl.pallas_call(
        functools.partial(forward_kernel, grain),
        grid_spec=pltpu.PrefetchScalarGridSpec(
            num_scalar_prefetch=1,
            grid=(4, kv_heads),
            in_specs=[
                pl.BlockSpec((rows_f, wide), lambda b, n, s: (b, n)),
                pl.BlockSpec((total, HEAD_SIZE), lambda b, n, s: (0, key_at + n)),
                pl.BlockSpec((total, HEAD_SIZE), lambda b, n, s: (0, value_at + n)),
                pl.BlockSpec((total, 1), lambda b, n, s: (0, 0)),
                pl.BlockSpec((1, 2, chunk_f), lambda b, n, s: (b, 0, 0)),
                pl.BlockSpec((rank, wide), lambda b, n, s: (0, n)),
                ANYWHERE,
            ]
            + [ANYWHERE] * len(pins),
            out_specs=[
                pl.BlockSpec((rows_f, wide), lambda b, n, s: (b, n)),
                pl.BlockSpec((1, 1, 1, lanes_f), lambda b, n, s: (b, n, 0, 0)),
                pl.BlockSpec((1, rank, rows_f), lambda b, n, s: (b, 0, 0)),
            ],
            scratch_shapes=[
                pltpu.VMEM((total, chunk_f), f32),
                pltpu.VMEM((total, lanes_f), f32),
                pltpu.VMEM((HEAD_SIZE, lanes_f), f32),
            ],
        ),
        out_shape=[
            jax.ShapeDtypeStruct((total, query_width), bf16),
            jax.ShapeDtypeStruct((4, kv_heads, 1, lanes_f), f32),
            jax.ShapeDtypeStruct((4, rank, rows_f), f32),
        ],
        **options("forward", 20, 2),
    )(scalars, packed, packed, packed, ids_column, row_info(rows_f, chunk_f // rows_f), down, done_before, *pins)

    rank_context = rank_portion
    for d in range(1, line):
        route = [(i, (i + d) % line) for i in range(line)]
        rank_context = rank_context + lax.ppermute(rank_portion, "fsdp", route)

    rows = shard
    heads = group
    chunk = rows * max(h for h in range(1, group + 1) if group % h == 0 and (h == 1 or h * rows <= 384))
    normal = (
        lse.reshape(4, query_heads, rows_f // rows, rows)
        .transpose(0, 2, 1, 3)
        .reshape(total // rows, query_heads // heads, 1, heads * rows)
    )
    ranks = (
        rank_context.reshape(4, rank, rows_f // rows, rows)
        .transpose(0, 2, 1, 3)
        .reshape(total // rows, rank, rows)
    )
    info = row_info(rows, chunk // rows)
    tile = heads * HEAD_SIZE
    lanes = heads * rows
    kv_spec = pl.BlockSpec((total, HEAD_SIZE), lambda n, s: (0, n))
    tile_spec = pl.BlockSpec((rows, tile), lambda n, s: (0, n))
    map_spec = pl.BlockSpec((rank, tile), lambda n, s: (0, n))
    rank_spec = pl.BlockSpec((rank, rows), lambda n, s: (0, 0))

    def backward(order, state, source, up_map=None, after=()):
        first = state is None
        last = up_map is not None
        here = 4 + 2 * order
        row_spec = pl.BlockSpec((rows, tile), lambda n, s: (s[here], n))
        ctx_rank_spec = pl.BlockSpec((1, rank, rows), lambda n, s: (s[here], 0, 0))
        operands, in_specs = [], []
        grad, rank_grad, local_columns = source
        if last:
            operands += [local_columns, ranks, up_map]
            in_specs += [tile_spec, ctx_rank_spec, map_spec]
        operands += [
            grad,
            rank_grad,
            packed,
            context,
            packed,
            packed,
            ids_column,
            info,
            normal,
        ]
        in_specs += [
            tile_spec,
            rank_spec,
            row_spec,
            row_spec,
            pl.BlockSpec((total, HEAD_SIZE), lambda n, s: (0, key_at + n)),
            pl.BlockSpec((total, HEAD_SIZE), lambda n, s: (0, value_at + n)),
            pl.BlockSpec((total, 1), lambda n, s: (0, 0)),
            pl.BlockSpec((1, 2, chunk), lambda n, s: (s[here], 0, 0)),
            pl.BlockSpec((1, 1, 1, lanes), lambda n, s: (s[here], n, 0, 0)),
        ]
        aliases = {}
        if not first:
            aliases[1 + len(operands)] = 0
            operands += list(state)
            in_specs += [ANYWHERE, kv_spec, kv_spec, map_spec]
        operands += list(after)
        in_specs += [ANYWHERE] * len(after)
        kv_type = bf16 if last else f32
        out_shape = [
            jax.ShapeDtypeStruct((total, query_width), bf16),
            jax.ShapeDtypeStruct((total, kv_width), kv_type),
            jax.ShapeDtypeStruct((total, kv_width), kv_type),
            jax.ShapeDtypeStruct((rank, query_width), f32),
        ]
        out_specs = [row_spec, kv_spec, kv_spec, map_spec]
        scratch = [
            pltpu.VMEM((total, chunk), f32),
            pltpu.VMEM((3 * rank, rows), bf16),
            pltpu.VMEM((total, HEAD_SIZE), f32),
            pltpu.VMEM((total, HEAD_SIZE), f32),
            pltpu.VMEM((KEY_BLOCK, lanes), bf16),
            pltpu.VMEM((KEY_BLOCK, lanes), bf16),
            pltpu.VMEM((HEAD_SIZE, lanes), f32),
        ]
        if last:
            out_shape.append(jax.ShapeDtypeStruct((rank, local_width), f32))
            out_specs.append(map_spec)
        return pl.pallas_call(
            functools.partial(
                backward_kernel, (here, grain, first, last, len(after))
            ),
            grid_spec=pltpu.PrefetchScalarGridSpec(
                num_scalar_prefetch=1,
                grid=(query_heads // heads,),
                in_specs=in_specs,
                out_specs=out_specs,
                scratch_shapes=scratch,
            ),
            out_shape=out_shape,
            input_output_aliases=aliases,
            **options(f"backward_{order + 1}", 8),
        )(scalars, *operands)

    if line == 4:
        cross(0, "far", lse)
    else:
        pass_on(lse)
    state = backward(-1, None, projected[0])
    for order in range(line - 2):
        if order:
            projected.append(projection(order, [state[3]]))
        pins = [crossing["near"][1]] if line == 4 and order == 0 else []
        state = backward(order, state, projected[order + 1], after=pins)
        if line != 4:
            pass_on(state[3])
        elif order == 0:
            cross(1, "far", state[3])

    sums = projection(line - 2, [state[3]], 0, 1)

    count = line - 1
    up_map = pl.pallas_call(
        functools.partial(up_map_kernel, count),
        grid_spec=pltpu.PrefetchScalarGridSpec(
            num_scalar_prefetch=1,
            grid=(local_width // tile,),
            in_specs=[
                pl.BlockSpec((1, rank, rows), lambda n, s, j=j: (s[2 + 2 * j], 0, 0)) for j in range(count)
            ]
            + [tile_spec] * count
            + [ANYWHERE],
            out_specs=map_spec,
        ),
        out_shape=jax.ShapeDtypeStruct((rank, local_width), f32),
        **options("up_map", 3),
    )(scalars, *([ranks] * count), *[p[2] for p in projected], sums[1])
    end = projection(line - 2, [], 1, 2, sums)
    query_gradient, key_gradient, value_gradient, down_map, up_map = backward(
        line - 2, state, end, up_map
    )
    return (
        query_gradient[None],
        key_gradient[None],
        value_gradient[None],
        down_map[None],
        up_map[None],
    )


def solution(mesh):
    placed = (
        P("pipe", "fsdp", None),
        P("pipe", "fsdp", None),
        P("pipe", None, "fsdp"),
        P("pipe", None, "fsdp"),
        P("pipe", None, "fsdp"),
        P("pipe", None, "fsdp"),
        P("pipe", None, "fsdp"),
        P("pipe", None),
    )
    return jax.shard_map(
        per_device,
        mesh=mesh,
        in_specs=placed,
        out_specs=(
            P("pipe", None, "fsdp"),
            P("pipe", None, "fsdp"),
            P("pipe", None, "fsdp"),
            P("pipe", None, "fsdp"),
            P("pipe", None, "fsdp"),
        ),
        check_vma=False,
    )
```

time: 321 us -> 269 us (0.84)
  Pallas kernels: 162 us -> 128 us
  waiting for transfers between devices: 50 us -> 80.7 us
  local copies, waits for them, and re-layouts: 39.7 us -> 14.8 us
  starting transfers between devices: 62.7 us -> 40.5 us
    ppermute x22 -> x11, waiting for transfers between devices: 16.9 us -> 52.2 us  [the longest x6 27.1 us: cross(): lax.ppermute(after(part, token), 'fsdp', routes[kind])]
    pallas_call x11 -> x10, Pallas kernels: 160 us -> 126 us  [the longest x5 74.2 us: projection(): pl.pallas_call(functools.partial(projection_kernel, (3 + 2 * order, place...]
    unnamed x125 -> x49, local copies, waits for them, and re-layouts: 35.2 us -> 9.54 us
    ppermute x22 -> x11, starting transfers between devices: 37.9 us -> 22.4 us  [the longest x2 10.2 us: pass_on(): lax.ppermute(after(p, token), 'fsdp', up_pairs)]
    ppermute x3 -> x2, waiting for transfers between devices: 33 us -> 25.6 us  [per_device(): own.append(lax.ppermute(part, 'pipe', from_next))]
    ppermute x3 -> x2, starting transfers between devices: 7.93 us -> 3.75 us  [per_device(): own.append(lax.ppermute(part, 'pipe', from_next))]
    ppermute x3, starting transfers between devices: 12.2 us -> 8.37 us  [per_device(): rank_context = rank_context + lax.ppermute(rank_portion, 'fsdp', route)]
  transfers between devices with their start and end apart: 31 -> 19, of which waited for: 5 -> 6; matrix products, arithmetic and copies ran while one was open for 1% -> 2% of each run, Pallas kernels for 45% -> 40%
where the time goes in v3:
time: 269 us; the launch traced here: 268 us
  Pallas kernels  128 us (48%)
  waiting for transfers between devices  80.7 us (30%)
  starting transfers between devices  40.5 us (15%)
  local copies, waits for them, and re-layouts  14.8 us (6%)
  other arithmetic  3.09 us (1%)
    pallas_call x5, Pallas kernels, projection(): pl.pallas_call(functools.partial(projection_kernel, (3 + 2 * order, place...  74.2 us
    pallas_call x4, Pallas kernels, backward(): pl.pallas_call(functools.partial(backward_kernel, (here, grain, first, la...  31.1 us
    ppermute x6, waiting for transfers between devices, cross(): lax.ppermute(after(part, token), 'fsdp', routes[kind])  27.1 us
    ppermute x2, waiting for transfers between devices, per_device(): own.append(lax.ppermute(part, 'pipe', from_next))  25.6 us
    ppermute x2, waiting for transfers between devices, pass_on(): lax.ppermute(after(p, token), 'fsdp', down_pairs)  25 us
    pallas_call x1, Pallas kernels, per_device(): pl.pallas_call(functools.partial(forward_kernel, grain), grid_spec=pltpu....  20.9 us
    ppermute x2, starting transfers between devices, pass_on(): lax.ppermute(after(p, token), 'fsdp', up_pairs)  10.2 us
    unnamed x49, local copies, waits for them, and re-layouts  9.54 us
  transfers between devices with their start and end apart: 19, of which 6 were waited for; matrix products, arithmetic and copies ran while one was open for 2% of the time, Pallas kernels for 40%

profile of v3, /device:TPU:0, one launch (start us, length us, event | category | flops | bytes accessed | tf_op | source)
XLA Modules:
  0.0 267.9 jit_solution(5128196302600815361)
XLA Ops:
  0.6 4.1 %slice_bitcast_fusion = (bf16[192,4096]{1,0:T(8,128)(2,1)}, bf16[192,4096]{1,0:T(8,128)(2,1)}) fusion(bf16[1,192,8192]{2,1,0:T(8,128)(2,1)} %param.9), kind=kLoop, calls=%fused_computation | loop fusion | bytes 6291456 | tf_op jit(solution)/shard_map/squeeze | solution.py:395
  4.7 0.3 constant_dynamic-update-slice_fusion.2
  5.0 0.7 copy-done.16
  5.8 0.1 copy-done.17
  5.9 0.7 copy-done.18
  6.6 5.0 %collective-permute-start.7 = (bf16[16,2048]{1,0:T(8,128)(2,1)S(1)}, bf16[16,2048]{1,0:T(8,128)(2,1)S(1)}, u32[]{:S(2)}, u32[]{:S(2)}) collective-permute-start(bf16[16,2048]{1,0:T(8,128)(2,1)S(1)} %bitcast.44), channel_id=1, source_target_pairs={{0,3},{1,0},{2,1},{3,2},{4,7},{5,4},{6,5},{7,6},{8,11},{9,8},{10,9... | collective-permute-start | bytes 196616 | tf_op jit(solution)/shard_map/ppermute | solution.py:386
  11.6 0.0 collective-permute-start.8
  11.7 1.0 collective-permute-start.9
  12.7 1.0 collective-permute-start
  13.7 0.1 slice.9
  13.8 0.1 reshape_squeeze.4
  13.9 0.2 convert_reduce_fusion
  14.1 0.1 tile.5.row_info_ref.refs_7_.refs_10_
  14.2 0.2 copy.25.ids_ref.refs_6_.refs_9_
  14.4 0.7 dynamic-slice_bitcast_fusion
  15.1 0.1 pad_add_fusion.1.scalars_ref
  15.2 0.0 collective-permute-done.7
  15.2 2.9 %collective-permute-done.8 = bf16[16,2048]{1,0:T(8,128)(2,1)S(1)} collective-permute-done((bf16[16,2048]{1,0:T(8,128)(2,1)S(1)}, bf16[16,2048]{1,0:T(8,128)(2,1)S(1)}, u32[]{:S(2)}, u32[]{:S(2)}) %collective-permute-start.8) | collective-permute-done | bytes 65568 | tf_op jit(solution)/shard_map/ppermute | solution.py:386
  18.1 0.0 collective-permute-done.9
  18.2 13.8 %collective-permute-done.refs_0_ = bf16[192,4096]{1,0:T(8,128)(2,1)S(1)} collective-permute-done((bf16[192,4096]{1,0:T(8,128)(2,1)}, bf16[192,4096]{1,0:T(8,128)(2,1)S(1)}, u32[]{:S(2)}, u32[]{:S(2)}) %collective-permute-start) | collective-permute-done | bytes 1572896 | tf_op jit(solution)/shard_map/ppermute | solution.py:400
  32.0 2.7 %collective-permute-start.3 = (bf16[192,4096]{1,0:T(8,128)(2,1)}, bf16[192,4096]{1,0:T(8,128)(2,1)S(1)}, u32[]{:S(2)}, u32[]{:S(2)}) collective-permute-start(bf16[192,4096]{1,0:T(8,128)(2,1)} %get-tuple-element.54), channel_id=1, source_target_pairs={{4,0},{8,4},{12,8},{16,12},{20,16},{24,20},{28,24},{0,28},{5,1},{9... | collective-permute-start | bytes 4718600 | tf_op jit(solution)/shard_map/ppermute | solution.py:400
  34.7 1.3 collective-permute-start.2
  36.0 5.1 %collective-permute-start.1 = (bf16[192,4096]{1,0:T(8,128)(2,1)S(1)}, bf16[192,4096]{1,0:T(8,128)(2,1)S(1)}, u32[]{:S(2)}, u32[]{:S(2)}) collective-permute-start(bf16[192,4096]{1,0:T(8,128)(2,1)S(1)} %collective-permute-done.refs_0_), channel_id=1, source_target_pairs={{0,1},{1,2},{2,3},{4,5},{5,6},{6,7},{8,9},{9,10},{10,11},{12,13},{... | collective-permute-start | bytes 4718600 | tf_op jit(solution)/shard_map/ppermute | solution.py:419
  41.1 11.8 %collective-permute-done.3.refs_1_ = bf16[192,4096]{1,0:T(8,128)(2,1)S(1)} collective-permute-done((bf16[192,4096]{1,0:T(8,128)(2,1)}, bf16[192,4096]{1,0:T(8,128)(2,1)S(1)}, u32[]{:S(2)}, u32[]{:S(2)}) %collective-permute-start.3) | collective-permute-done | bytes 1572896 | tf_op jit(solution)/shard_map/ppermute | solution.py:400
  52.9 2.7 %collective-permute-start.4 = (bf16[768,2560]{1,0:T(8,128)(2,1)}, bf16[768,2560]{1,0:T(8,128)(2,1)}, u32[]{:S(2)}, u32[]{:S(2)}) collective-permute-start(bf16[768,2560]{1,0:T(8,128)(2,1)} %copy-done.15), channel_id=1, source_target_pairs={{0,28},{4,24},{8,20},{12,16},{16,12},{20,8},{24,4},{28,0},{1,29},{... | collective-permute-start | bytes 11796488 | tf_op jit(solution)/shard_map/ppermute | solution.py:437
  55.6 1.3 collective-permute-start.5
  56.9 5.1 %collective-permute-start.6 = (bf16[192,4096]{1,0:T(8,128)(2,1)S(1)}, bf16[192,4096]{1,0:T(8,128)(2,1)S(1)}, u32[]{:S(2)}, u32[]{:S(2)}) collective-permute-start(bf16[192,4096]{1,0:T(8,128)(2,1)S(1)} %collective-permute-done.3.refs_1_), channel_id=1, source_target_pairs={{0,1},{1,2},{2,3},{4,5},{5,6},{6,7},{8,9},{9,10},{10,11},{12,13},{... | collective-permute-start | bytes 4718600 | tf_op jit(solution)/shard_map/ppermute | solution.py:419
  62.0 17.6 %projection_0_2.1 = (bf16[192,2048]{1,0:T(8,128)(2,1)S(1)}, f32[16,192]{1,0:T(8,128)S(1)}, bf16[192,2048]{1,0:T(8,128)(2,1)S(1)}) custom-call(s32[13]{0:T(128)S(1)} %pad_add_fusion.1.scalars_ref, bf16[192,4096]{1,0:T(8,128)(2,1)S(1)} %collective-permute-done.refs_0_, bf16[192,4096]{1,0:T(8,128)(2,1)S(1)} %collective-permute-done.3.refs_1_, ...), custom_call_target="tpu_custom_call" | custom-call | flops 17999998976 | bytes 1 | tf_op jit(solution)/shard_map/projection_0_2/pallas_call | solution.py:530
  79.7 0.0 collective-permute-done.1.refs_2_
  79.7 1.4 broadcast_select_fusion.1
  81.0 0.8 collective-permute-start.11
  81.8 1.3 collective-permute-start.10
  83.1 25.0 %collective-permute-done.5.refs_1_ = bf16[192,4096]{1,0:T(8,128)(2,1)S(1)} collective-permute-done((bf16[192,4096]{1,0:T(8,128)(2,1)S(1)}, bf16[192,4096]{1,0:T(8,128)(2,1)S(1)}, u32[]{:S(2)}, u32[]{:S(2)}) %collective-permute-start.5) | collective-permute-done | bytes 1572896 | tf_op jit(solution)/shard_map/ppermute | solution.py:420
  108.1 1.4 broadcast_select_fusion
  109.5 1.3 collective-permute-start.13
  110.8 0.8 collective-permute-start.15
  111.6 17.6 %projection_1_2.1 = (bf16[192,2048]{1,0:T(8,128)(2,1)S(1)}, f32[16,192]{1,0:T(8,128)S(1)}, bf16[192,2048]{1,0:T(8,128)(2,1)S(1)}) custom-call(s32[13]{0:T(128)S(1)} %pad_add_fusion.1.scalars_ref, bf16[192,4096]{1,0:T(8,128)(2,1)S(1)} %collective-permute-done.2.refs_0_, bf16[192,4096]{1,0:T(8,128)(2,1)S(1)} %collective-permute-done.5.refs_1_, ...), custom_call_target="tpu_custom_call" | custom-call | flops 17999998976 | bytes 1 | tf_op jit(solution)/shard_map/projection_1_2/pallas_call | solution.py:530
  129.2 0.9 copy-done.12
  130.1 11.7 %collective-permute-done.10.rest_1_.refs_2_ = bf16[192,4096]{1,0:T(8,128)(2,1)S(1)} collective-permute-done((bf16[192,4096]{1,0:T(8,128)(2,1)S(1)}, bf16[192,4096]{1,0:T(8,128)(2,1)S(1)}, u32[]{:S(2)}, u32[]{:S(2)}) %collective-permute-start.10) | collective-permute-done | bytes 1572896 | tf_op jit(solution)/shard_map/ppermute | solution.py:432
  141.8 0.0 collective-permute-done.4.q_ref.k_ref.v_ref.refs_2_.refs_4_.refs_5_.refs_7_.refs_8_
  141.8 20.9 %forward.1 = (bf16[768,2048]{1,0:T(8,128)(2,1)S(1)}, f32[4,2,1,1536]{3,2,1,0:T(1,128)S(1)}, f32[4,16,192]{2,1,0:T(8,128)S(1)}) custom-call(s32[13]{0:T(128)S(1)} %pad_add_fusion.1.scalars_ref, bf16[768,2560]{1,0:T(8,128)(2,1)} %collective-permute-done.4.q_ref.k_ref.v_ref.refs_2_.refs_4_.refs_5_.refs_7_.refs_8_, ...), custom_call_target="tpu_custom_call" | custom-call | flops 20000000000 | bytes 1 | tf_op jit(solution)/shard_map/forward/pallas_call | solution.py:571
  162.7 3.6 %collective-permute-start.16 = (f32[4,16,192]{2,1,0:T(8,128)S(1)}, f32[4,16,192]{2,1,0:T(8,128)S(1)}, u32[]{:S(2)}, u32[]{:S(2)}) collective-permute-start(f32[4,16,192]{2,1,0:T(8,128)S(1)} %get-tuple-element.83), channel_id=1, source_target_pairs={{0,1},{1,2},{2,3},{3,0},{4,5},{5,6},{6,7},{7,4},{8,9},{9,10},{10,1... | collective-permute-start | bytes 147464 | tf_op jit(solution)/shard_map/ppermute | solution.py:608
  166.4 2.2 collective-permute-start.17
  168.5 2.6 collective-permute-start.18
  171.1 5.8 %backward_0.1 = (bf16[768,2048]{1,0:T(8,128)(2,1)}, f32[768,256]{1,0:T(8,128)S(1)}, f32[768,256]{1,0:T(8,128)S(1)}, f32[16,2048]{1,0:T(8,128)S(1)}) custom-call(s32[13]{0:T(128)S(1)} %pad_add_fusion.1.scalars_ref, bf16[192,2048]{1,0:T(8,128)(2,1)S(1)} %get-tuple-element.65.refs_0_, f32[16,192]{1,0:T(8,128)S(1)} %get-tuple-element.57.refs_7_.refs_1_, ...), custom_call_target="tpu_custom_call" | custom-call | flops 8000000000 | bytes 1 | tf_op jit(solution)/shard_map/backward_0/pallas_call | solution.py:691
  176.9 0.0 collective-permute-done.13.refs_13_.refs_3_
  177.0 1.2 copy-done.1
  178.2 1.3 collective-permute-start.12
  179.5 1.4 copy-done.2
  180.9 7.7 %backward_1.1 = (bf16[768,2048]{1,0:T(8,128)(2,1)}, f32[768,256]{1,0:T(8,128)S(1)}, f32[768,256]{1,0:T(8,128)S(1)}, f32[16,2048]{1,0:T(8,128)S(1)}) custom-call(s32[13]{0:T(128)S(1)} %pad_add_fusion.1.scalars_ref, bf16[192,2048]{1,0:T(8,128)(2,1)S(1)} %get-tuple-element.63.refs_0_, ...), custom_call_target="tpu_custom_call", output_to_operand_aliasing={{0}: (10, {})} | custom-call | flops 8000000000 | bytes 1 | tf_op jit(solution)/shard_map/backward_1/pallas_call | solution.py:691
  188.6 17.6 %projection_2_2.1 = (bf16[192,2048]{1,0:T(8,128)(2,1)S(1)}, f32[16,192]{1,0:T(8,128)S(1)}, bf16[192,2048]{1,0:T(8,128)(2,1)S(1)}) custom-call(s32[13]{0:T(128)S(1)} %pad_add_fusion.1.scalars_ref, bf16[192,4096]{1,0:T(8,128)(2,1)S(1)} %collective-permute-done.2.refs_0_, bf16[192,4096]{1,0:T(8,128)(2,1)S(1)} %collective-permute-done.5.refs_1_, ...), custom_call_target="tpu_custom_call" | custom-call | flops 17999998976 | bytes 1 | tf_op jit(solution)/shard_map/projection_2_2/pallas_call | solution.py:530
  206.3 0.0 collective-permute-done.16
  206.3 1.5 collective-permute-start.14
  207.8 1.9 copy-done.4
  209.7 1.1 copy-done.7
  210.8 1.1 copy-done.9
  211.9 7.7 %backward_2.1 = (bf16[768,2048]{1,0:T(8,128)(2,1)}, f32[768,256]{1,0:T(8,128)S(1)}, f32[768,256]{1,0:T(8,128)S(1)}, f32[16,2048]{1,0:T(8,128)S(1)}) custom-call(s32[13]{0:T(128)S(1)} %pad_add_fusion.1.scalars_ref, bf16[192,2048]{1,0:T(8,128)(2,1)S(1)} %get-tuple-element.74.refs_0_, ...), custom_call_target="tpu_custom_call", output_to_operand_aliasing={{0}: (10, {})} | custom-call | flops 8000000000 | bytes 1 | tf_op jit(solution)/shard_map/backward_2/pallas_call | solution.py:691
  219.7 0.0 collective-permute-done.12.refs_0_
  219.7 10.4 %projection_3_1.1 = (f32[192,2048]{1,0:T(8,128)S(1)}, f32[16,192]{1,0:T(8,128)S(1)}) custom-call(s32[13]{0:T(128)S(1)} %pad_add_fusion.1.scalars_ref, bf16[192,4096]{1,0:T(8,128)(2,1)S(1)} %collective-permute-done.12.refs_0_, bf16[192,4096]{1,0:T(8,128)(2,1)S(1)} %collective-permute-done.11.rest_2_.refs_1_.refs_2_, bf16[2048,8192]{1,0:T(8,128)(2,1)} %bitcast.39, ...), custom_call_target="tpu_custom_call" | custom-call | flops 8999999488 | bytes 1 | tf_op jit(solution)/shard_map/projection_3_1/pallas_call | solution.py:530
  230.2 1.3 up_map.1.refs_2_
  231.5 0.0 collective-permute-done.15.refs_3_
  231.5 15.4 %collective-permute-done.14.refs_1_ = bf16[192,4096]{1,0:T(8,128)(2,1)S(1)} collective-permute-done((bf16[192,4096]{1,0:T(8,128)(2,1)}, bf16[192,4096]{1,0:T(8,128)(2,1)S(1)}, u32[]{:S(2)}, u32[]{:S(2)}) %collective-permute-start.14) | collective-permute-done | bytes 1572896 | tf_op jit(solution)/shard_map/ppermute | solution.py:432
  246.9 11.0 %projection_3_2.1 = (bf16[192,2048]{1,0:T(8,128)(2,1)S(1)}, f32[16,192]{1,0:T(8,128)S(1)}, bf16[192,2048]{1,0:T(8,128)(2,1)S(1)}) custom-call(s32[13]{0:T(128)S(1)} %pad_add_fusion.1.scalars_ref, bf16[192,4096]{1,0:T(8,128)(2,1)S(1)} %collective-permute-done.12.refs_0_, bf16[192,4096]{1,0:T(8,128)(2,1)S(1)} %collective-permute-done.14.refs_1_, ...), custom_call_target="tpu_custom_call" | custom-call | flops 8999999488 | bytes 1 | tf_op jit(solution)/shard_map/projection_3_2/pallas_call | solution.py:530
  257.9 9.8 %backward_3.1 = (bf16[768,2048]{1,0:T(8,128)(2,1)}, bf16[768,256]{1,0:T(8,128)(2,1)}, bf16[768,256]{1,0:T(8,128)(2,1)}, f32[16,2048]{1,0:T(8,128)}, f32[16,2048]{1,0:T(8,128)}) custom-call(s32[13]{0:T(128)S(1)} %pad_add_fusion.1.scalars_ref, bf16[192,2048]{1,0:T(8,128)(2,1)S(1)} %get-tuple-element.82.refs_0_, ...), custom_call_target="tpu_custom_call", output_to_operand_aliasing={{0}: (13, {})} | custom-call | flops 8000000000 | bytes 1 | tf_op jit(solution)/shard_map/backward_3/pallas_call | solution.py:691
  (53 shorter events, 0.3 us)
Async XLA Ops:
  0.6 4.1 %copy-start.14 = (bf16[1,768,2048]{2,1,0:T(8,128)(2,1)S(1)}, bf16[1,768,2048]{2,1,0:T(8,128)(2,1)}, u32[]{:S(2)}) copy-start(bf16[1,768,2048]{2,1,0:T(8,128)(2,1)} %param.13) | copy-start | bytes 9437188
  4.7 1.0 copy-start.16
  4.7 1.1 copy-start.17
  5.7 0.9 copy-start.18
  5.7 8.0 %copy-start.19 = (s32[1,768]{1,0:T(1,128)S(1)}, s32[1,768]{1,0:T(1,128)}, u32[]{:S(2)}) copy-start(s32[1,768]{1,0:T(1,128)} %param.16) | copy-start | bytes 9220
  5.8 56.2 %copy-start = (bf16[1,16,2048]{2,1,0:T(8,128)(2,1)S(1)}, bf16[1,16,2048]{2,1,0:T(8,128)(2,1)}, u32[]{:S(2)}) copy-start(bf16[1,16,2048]{2,1,0:T(8,128)(2,1)} %param.11) | copy-start | bytes 196612
  5.9 5.8 %copy-start.15 = (bf16[768,2560]{1,0:T(8,128)(2,1)}, bf16[768,2560]{1,0:T(8,128)(2,1)S(1)}, u32[]{:S(2)}) copy-start(bf16[768,2560]{1,0:T(8,128)(2,1)S(1)} %constant_dynamic-update-slice_fusion) | copy-start | bytes 11796484
  6.6 8.6 %collective-permute-start.7 = (bf16[16,2048]{1,0:T(8,128)(2,1)S(1)}, bf16[16,2048]{1,0:T(8,128)(2,1)S(1)}, u32[]{:S(2)}, u32[]{:S(2)}) collective-permute-start(bf16[16,2048]{1,0:T(8,128)(2,1)S(1)} %bitcast.44), channel_id=1, source_target_pairs={{0,3},{1,0},{2,1},{3,2},{4,7},{5,4},{6,5},{7,6},{8,11},{9,8},{10,9... | collective-permute-start | bytes 196616 | tf_op jit(solution)/shard_map/ppermute | solution.py:386
  11.6 6.5 %collective-permute-start.8 = (bf16[16,2048]{1,0:T(8,128)(2,1)S(1)}, bf16[16,2048]{1,0:T(8,128)(2,1)S(1)}, u32[]{:S(2)}, u32[]{:S(2)}) collective-permute-start(bf16[16,2048]{1,0:T(8,128)(2,1)S(1)} %bitcast.45), channel_id=1, source_target_pairs={{0,2},{1,3},{2,0},{3,1},{4,6},{5,7},{6,4},{7,5},{8,10},{9,11},{10,... | collective-permute-start | bytes 196616 | tf_op jit(solution)/shard_map/ppermute | solution.py:386
  11.7 6.5 %collective-permute-start.9 = (bf16[16,2048]{1,0:T(8,128)(2,1)S(1)}, bf16[16,2048]{1,0:T(8,128)(2,1)S(1)}, u32[]{:S(2)}, u32[]{:S(2)}) collective-permute-start(bf16[16,2048]{1,0:T(8,128)(2,1)S(1)} %bitcast.46), channel_id=1, source_target_pairs={{0,1},{1,2},{2,3},{3,0},{4,5},{5,6},{6,7},{7,4},{8,9},{9,10},{10,1... | collective-permute-start | bytes 196616 | tf_op jit(solution)/shard_map/ppermute | solution.py:386
  12.7 19.3 %collective-permute-start = (bf16[192,4096]{1,0:T(8,128)(2,1)}, bf16[192,4096]{1,0:T(8,128)(2,1)S(1)}, u32[]{:S(2)}, u32[]{:S(2)}) collective-permute-start(bf16[192,4096]{1,0:T(8,128)(2,1)} %get-tuple-element.102), channel_id=1, source_target_pairs={{4,0},{8,4},{12,8},{16,12},{20,16},{24,20},{28,24},{0,28},{5,1},{9... | collective-permute-start | bytes 4718600 | tf_op jit(solution)/shard_map/ppermute | solution.py:400
  32.0 21.0 %collective-permute-start.3 = (bf16[192,4096]{1,0:T(8,128)(2,1)}, bf16[192,4096]{1,0:T(8,128)(2,1)S(1)}, u32[]{:S(2)}, u32[]{:S(2)}) collective-permute-start(bf16[192,4096]{1,0:T(8,128)(2,1)} %get-tuple-element.54), channel_id=1, source_target_pairs={{4,0},{8,4},{12,8},{16,12},{20,16},{24,20},{28,24},{0,28},{5,1},{9... | collective-permute-start | bytes 4718600 | tf_op jit(solution)/shard_map/ppermute | solution.py:400
  34.7 44.9 %collective-permute-start.2 = (bf16[192,4096]{1,0:T(8,128)(2,1)S(1)}, bf16[192,4096]{1,0:T(8,128)(2,1)S(1)}, u32[]{:S(2)}, u32[]{:S(2)}) collective-permute-start(bf16[192,4096]{1,0:T(8,128)(2,1)S(1)} %collective-permute-done.refs_0_), channel_id=1, source_target_pairs={{1,0},{2,1},{3,2},{5,4},{6,5},{7,6},{9,8},{10,9},{11,10},{13,12},{... | collective-permute-start | bytes 4718600 | tf_op jit(solution)/shard_map/ppermute | solution.py:420
  36.0 43.6 %collective-permute-start.1 = (bf16[192,4096]{1,0:T(8,128)(2,1)S(1)}, bf16[192,4096]{1,0:T(8,128)(2,1)S(1)}, u32[]{:S(2)}, u32[]{:S(2)}) collective-permute-start(bf16[192,4096]{1,0:T(8,128)(2,1)S(1)} %collective-permute-done.refs_0_), channel_id=1, source_target_pairs={{0,1},{1,2},{2,3},{4,5},{5,6},{6,7},{8,9},{9,10},{10,11},{12,13},{... | collective-permute-start | bytes 4718600 | tf_op jit(solution)/shard_map/ppermute | solution.py:419
  52.9 88.9 %collective-permute-start.4 = (bf16[768,2560]{1,0:T(8,128)(2,1)}, bf16[768,2560]{1,0:T(8,128)(2,1)}, u32[]{:S(2)}, u32[]{:S(2)}) collective-permute-start(bf16[768,2560]{1,0:T(8,128)(2,1)} %copy-done.15), channel_id=1, source_target_pairs={{0,28},{4,24},{8,20},{12,16},{16,12},{20,8},{24,4},{28,0},{1,29},{... | collective-permute-start | bytes 11796488 | tf_op jit(solution)/shard_map/ppermute | solution.py:437
  55.6 52.5 %collective-permute-start.5 = (bf16[192,4096]{1,0:T(8,128)(2,1)S(1)}, bf16[192,4096]{1,0:T(8,128)(2,1)S(1)}, u32[]{:S(2)}, u32[]{:S(2)}) collective-permute-start(bf16[192,4096]{1,0:T(8,128)(2,1)S(1)} %collective-permute-done.3.refs_1_), channel_id=1, source_target_pairs={{1,0},{2,1},{3,2},{5,4},{6,5},{7,6},{9,8},{10,9},{11,10},{13,12},{... | collective-permute-start | bytes 4718600 | tf_op jit(solution)/shard_map/ppermute | solution.py:420
  56.9 51.2 %collective-permute-start.6 = (bf16[192,4096]{1,0:T(8,128)(2,1)S(1)}, bf16[192,4096]{1,0:T(8,128)(2,1)S(1)}, u32[]{:S(2)}, u32[]{:S(2)}) collective-permute-start(bf16[192,4096]{1,0:T(8,128)(2,1)S(1)} %collective-permute-done.3.refs_1_), channel_id=1, source_target_pairs={{0,1},{1,2},{2,3},{4,5},{5,6},{6,7},{8,9},{9,10},{10,11},{12,13},{... | collective-permute-start | bytes 4718600 | tf_op jit(solution)/shard_map/ppermute | solution.py:419
  79.6 1.4 copy-start.10
  81.0 49.1 %collective-permute-start.11 = (bf16[192,4096]{1,0:T(8,128)(2,1)}, bf16[192,4096]{1,0:T(8,128)(2,1)S(1)}, u32[]{:S(2)}, u32[]{:S(2)}) collective-permute-start(bf16[192,4096]{1,0:T(8,128)(2,1)} %get-tuple-element.62), channel_id=1, source_target_pairs={{1,2},{2,1},{5,6},{6,5},{9,10},{10,9},{13,14},{14,13},{17,18},{18,... | collective-permute-start | bytes 4718600 | tf_op jit(solution)/shard_map/ppermute | solution.py:432
  81.8 60.0 %collective-permute-start.10 = (bf16[192,4096]{1,0:T(8,128)(2,1)S(1)}, bf16[192,4096]{1,0:T(8,128)(2,1)S(1)}, u32[]{:S(2)}, u32[]{:S(2)}) collective-permute-start(bf16[192,4096]{1,0:T(8,128)(2,1)S(1)} %get-tuple-element.59), channel_id=1, source_target_pairs={{1,0},{2,3},{5,4},{6,7},{9,8},{10,11},{13,12},{14,15},{17,16},{18,... | collective-permute-start | bytes 4718600 | tf_op jit(solution)/shard_map/ppermute | solution.py:432
  109.5 67.4 %collective-permute-start.13 = (bf16[192,4096]{1,0:T(8,128)(2,1)S(1)}, bf16[192,4096]{1,0:T(8,128)(2,1)S(1)}, u32[]{:S(2)}, u32[]{:S(2)}) collective-permute-start(bf16[192,4096]{1,0:T(8,128)(2,1)S(1)} %get-tuple-element.70), channel_id=1, source_target_pairs={{1,0},{2,3},{5,4},{6,7},{9,8},{10,11},{13,12},{14,15},{17,16},{18,... | collective-permute-start | bytes 4718600 | tf_op jit(solution)/shard_map/ppermute | solution.py:432
  110.8 120.7 %collective-permute-start.15 = (bf16[192,4096]{1,0:T(8,128)(2,1)}, bf16[192,4096]{1,0:T(8,128)(2,1)S(1)}, u32[]{:S(2)}, u32[]{:S(2)}) collective-permute-start(bf16[192,4096]{1,0:T(8,128)(2,1)} %get-tuple-element.73), channel_id=1, source_target_pairs={{1,2},{2,1},{5,6},{6,5},{9,10},{10,9},{13,14},{14,13},{17,18},{18,... | collective-permute-start | bytes 4718600 | tf_op jit(solution)/shard_map/ppermute | solution.py:432
  129.2 0.9 copy-start.12
  162.7 16.8 %copy-start.3 = (bf16[768,2048]{1,0:T(8,128)(2,1)}, bf16[768,2048]{1,0:T(8,128)(2,1)S(1)}, u32[]{:S(2)}) copy-start(bf16[768,2048]{1,0:T(8,128)(2,1)S(1)} %get-tuple-element.64.refs_3_.refs_6_) | copy-start | bytes 9437188
  162.7 43.5 %collective-permute-start.16 = (f32[4,16,192]{2,1,0:T(8,128)S(1)}, f32[4,16,192]{2,1,0:T(8,128)S(1)}, u32[]{:S(2)}, u32[]{:S(2)}) collective-permute-start(f32[4,16,192]{2,1,0:T(8,128)S(1)} %get-tuple-element.83), channel_id=1, source_target_pairs={{0,1},{1,2},{2,3},{3,0},{4,5},{5,6},{6,7},{7,4},{8,9},{9,10},{10,1... | collective-permute-start | bytes 147464 | tf_op jit(solution)/shard_map/ppermute | solution.py:608
  166.4 53.3 %collective-permute-start.17 = (f32[4,16,192]{2,1,0:T(8,128)S(1)}, f32[4,16,192]{2,1,0:T(8,128)S(1)}, u32[]{:S(2)}, u32[]{:S(2)}) collective-permute-start(f32[4,16,192]{2,1,0:T(8,128)S(1)} %get-tuple-element.83), channel_id=1, source_target_pairs={{0,2},{1,3},{2,0},{3,1},{4,6},{5,7},{6,4},{7,5},{8,10},{9,11},{10,... | collective-permute-start | bytes 147464 | tf_op jit(solution)/shard_map/ppermute | solution.py:608
  168.5 51.1 %collective-permute-start.18 = (f32[4,16,192]{2,1,0:T(8,128)S(1)}, f32[4,16,192]{2,1,0:T(8,128)S(1)}, u32[]{:S(2)}, u32[]{:S(2)}) collective-permute-start(f32[4,16,192]{2,1,0:T(8,128)S(1)} %get-tuple-element.83), channel_id=1, source_target_pairs={{0,3},{1,0},{2,1},{3,2},{4,7},{5,4},{6,5},{7,6},{8,11},{9,8},{10,9... | collective-permute-start | bytes 147464 | tf_op jit(solution)/shard_map/ppermute | solution.py:608
  177.0 1.2 copy-start.1
  178.2 41.5 %collective-permute-start.12 = (bf16[192,4096]{1,0:T(8,128)(2,1)}, bf16[192,4096]{1,0:T(8,128)(2,1)S(1)}, u32[]{:S(2)}, u32[]{:S(2)}) collective-permute-start(bf16[192,4096]{1,0:T(8,128)(2,1)} %get-tuple-element.62), channel_id=1, source_target_pairs={{1,3},{2,0},{5,7},{6,4},{9,11},{10,8},{13,15},{14,12},{17,19},{18,... | collective-permute-start | bytes 4718600 | tf_op jit(solution)/shard_map/ppermute | solution.py:432
  179.5 1.4 copy-start.2
  188.6 17.6 %copy-start.6 = (f32[768,256]{1,0:T(8,128)}, f32[768,256]{1,0:T(8,128)S(1)}, u32[]{:S(2)}) copy-start(f32[768,256]{1,0:T(8,128)S(1)} %get-tuple-element.77.refs_10_) | copy-start | bytes 2359300
  188.6 17.6 %copy-start.8 = (f32[768,256]{1,0:T(8,128)}, f32[768,256]{1,0:T(8,128)S(1)}, u32[]{:S(2)}) copy-start(f32[768,256]{1,0:T(8,128)S(1)} %get-tuple-element.78.refs_11_) | copy-start | bytes 2359300
  206.3 40.6 %collective-permute-start.14 = (bf16[192,4096]{1,0:T(8,128)(2,1)}, bf16[192,4096]{1,0:T(8,128)(2,1)S(1)}, u32[]{:S(2)}, u32[]{:S(2)}) collective-permute-start(bf16[192,4096]{1,0:T(8,128)(2,1)} %get-tuple-element.73), channel_id=1, source_target_pairs={{1,3},{2,0},{5,7},{6,4},{9,11},{10,8},{13,15},{14,12},{17,19},{18,... | collective-permute-start | bytes 4718600 | tf_op jit(solution)/shard_map/ppermute | solution.py:432
  207.8 1.9 copy-start.4
  209.7 1.1 copy-start.7
  210.8 1.1 copy-start.9
  219.7 10.4 %copy-start.11 = (bf16[192,2048]{1,0:T(8,128)(2,1)S(1)}, bf16[192,2048]{1,0:T(8,128)(2,1)}, u32[]{:S(2)}) copy-start(bf16[192,2048]{1,0:T(8,128)(2,1)} %copy-done.10) | copy-start | bytes 2359300
  219.7 10.4 %copy-start.13 = (bf16[192,2048]{1,0:T(8,128)(2,1)S(1)}, bf16[192,2048]{1,0:T(8,128)(2,1)}, u32[]{:S(2)}) copy-start(bf16[192,2048]{1,0:T(8,128)(2,1)} %copy-done.12) | copy-start | bytes 2359300
  246.9 11.0 %copy-start.5 = (bf16[768,2048]{1,0:T(8,128)(2,1)S(1)}, bf16[768,2048]{1,0:T(8,128)(2,1)}, u32[]{:S(2)}) copy-start(bf16[768,2048]{1,0:T(8,128)(2,1)} %copy-done.3) | copy-start | bytes 9437188

commit v4 on v3

--- a/solution.py
+++ b/solution.py
@@ -395,15 +395,10 @@
         part = handoff_gradient[0, :, at : at + width]
         if own:
             part, _ = lax.optimization_barrier((part, own[-1]))
-        else:
-            first_part = part
         own.append(lax.ppermute(part, "pipe", from_next))
         at += width
-    saved = lax.optimization_barrier(
-        (stored_queries[0], stored_keys[0], stored_values[0], first_part)
-    )[:3]
-    packed = jnp.concatenate(saved, axis=1)
-    up_all = spread(lax.optimization_barrier((adapter_up[0], packed))[0])
+    packed = jnp.concatenate([stored_queries[0], stored_keys[0], stored_values[0]], axis=1)
+    up_all = spread(lax.optimization_barrier((adapter_up[0], own[0]))[0])
     rising, falling = [own], [own]
     crossing = {}
 

time: 269 us -> 267 us (level)
    ppermute x3, waiting for transfers between devices: 2.92 us -> 0.01 us  [spread(): blocks.append(lax.ppermute(block, 'fsdp', route))]
    unnamed x49 -> x47, local copies, waits for them, and re-layouts: 9.54 us -> 7.69 us
  transfers between devices with their start and end apart: 19 -> 19, of which waited for: 6 -> 5; matrix products, arithmetic and copies ran while one was open for 2% -> 3% of each run, Pallas kernels for 40% -> 40%
where the time goes in v4:
time: 267 us
  Pallas kernels  128 us (48%)
  waiting for transfers between devices  78.6 us (29%)
  starting transfers between devices  40.7 us (15%)
  local copies, waits for them, and re-layouts  12.9 us (5%)
  other arithmetic  5.77 us (2%)
    pallas_call x5, Pallas kernels, projection(): pl.pallas_call(functools.partial(projection_kernel, (3 + 2 * order, place...  74.2 us
    pallas_call x4, Pallas kernels, backward(): pl.pallas_call(functools.partial(backward_kernel, (here, grain, first, la...  31.1 us
    ppermute x6, waiting for transfers between devices, cross(): lax.ppermute(after(part, token), 'fsdp', routes[kind])  27.4 us
    ppermute x2, waiting for transfers between devices, per_device(): own.append(lax.ppermute(part, 'pipe', from_next))  26 us
    ppermute x2, waiting for transfers between devices, pass_on(): lax.ppermute(after(p, token), 'fsdp', down_pairs)  25.2 us
    pallas_call x1, Pallas kernels, per_device(): pl.pallas_call(functools.partial(forward_kernel, grain), grid_spec=pltpu....  20.9 us
    ppermute x2, starting transfers between devices, pass_on(): lax.ppermute(after(p, token), 'fsdp', up_pairs)  10.2 us
    ppermute x3, starting transfers between devices, per_device(): rank_context = rank_context + lax.ppermute(rank_portion, 'fsdp', route)  8.39 us
  transfers between devices with their start and end apart: 19, of which 5 were waited for; matrix products, arithmetic and copies ran while one was open for 3% of the time, Pallas kernels for 40%

profile of v4, /device:TPU:0, one launch (start us, length us, event | category | flops | bytes accessed | tf_op | source)
XLA Modules:
  0.0 266.7 jit_solution(15143383629953639675)
XLA Ops:
  0.7 4.0 %slice_bitcast_fusion = (bf16[192,4096]{1,0:T(8,128)(2,1)}, bf16[192,4096]{1,0:T(8,128)(2,1)}) fusion(bf16[1,192,8192]{2,1,0:T(8,128)(2,1)} %param.9), kind=kLoop, calls=%fused_computation.1 | loop fusion | bytes 6291456 | tf_op jit(solution)/shard_map/squeeze | solution.py:395
  4.7 3.3 %collective-permute-start = (bf16[192,4096]{1,0:T(8,128)(2,1)}, bf16[192,4096]{1,0:T(8,128)(2,1)S(1)}, u32[]{:S(2)}, u32[]{:S(2)}) collective-permute-start(bf16[192,4096]{1,0:T(8,128)(2,1)} %get-tuple-element.96), channel_id=1, source_target_pairs={{4,0},{8,4},{12,8},{16,12},{20,16},{24,20},{28,24},{0,28},{5,1},{9... | collective-permute-start | bytes 4718600 | tf_op jit(solution)/shard_map/ppermute | solution.py:398
  8.0 0.1 slice.9
  8.1 0.1 reshape_squeeze.4
  8.2 0.1 tile.5.row_info_ref.refs_7_.refs_10_
  8.3 0.2 copy.25.ids_ref.refs_6_.refs_9_
  8.5 0.7 dynamic-slice_bitcast_fusion
  9.2 0.2 convert_reduce_fusion
  9.4 0.0 copy-start.18
  9.4 0.0 copy-start.14
  9.4 2.2 pad_maximum_fusion
  11.6 0.0 copy-start
  11.6 14.6 %collective-permute-done.refs_0_ = bf16[192,4096]{1,0:T(8,128)(2,1)S(1)} collective-permute-done((bf16[192,4096]{1,0:T(8,128)(2,1)}, bf16[192,4096]{1,0:T(8,128)(2,1)S(1)}, u32[]{:S(2)}, u32[]{:S(2)}) %collective-permute-start) | collective-permute-done | bytes 1572896 | tf_op jit(solution)/shard_map/ppermute | solution.py:398
  26.3 3.6 %collective-permute-start.7 = (bf16[16,2048]{1,0:T(8,128)(2,1)S(1)}, bf16[16,2048]{1,0:T(8,128)(2,1)S(1)}, u32[]{:S(2)}, u32[]{:S(2)}) collective-permute-start(bf16[16,2048]{1,0:T(8,128)(2,1)S(1)} %bitcast.44), channel_id=1, source_target_pairs={{0,3},{1,0},{2,1},{3,2},{4,7},{5,4},{6,5},{7,6},{8,11},{9,8},{10,9... | collective-permute-start | bytes 196616 | tf_op jit(solution)/shard_map/ppermute | solution.py:386
  29.9 0.1 pad_add_fusion.1.scalars_ref
  29.9 0.0 collective-permute-start.8
  29.9 1.0 collective-permute-start.9
  31.0 1.9 collective-permute-start.3
  32.8 1.3 collective-permute-start.2
  34.1 0.0 collective-permute-done.7
  34.1 5.1 %collective-permute-start.1 = (bf16[192,4096]{1,0:T(8,128)(2,1)S(1)}, bf16[192,4096]{1,0:T(8,128)(2,1)S(1)}, u32[]{:S(2)}, u32[]{:S(2)}) collective-permute-start(bf16[192,4096]{1,0:T(8,128)(2,1)S(1)} %collective-permute-done.refs_0_), channel_id=1, source_target_pairs={{0,1},{1,2},{2,3},{4,5},{5,6},{6,7},{8,9},{9,10},{10,11},{12,13},{... | collective-permute-start | bytes 4718600 | tf_op jit(solution)/shard_map/ppermute | solution.py:414
  39.2 0.0 collective-permute-done.8
  39.3 0.0 collective-permute-done.9
  39.4 11.3 %collective-permute-done.3.refs_1_ = bf16[192,4096]{1,0:T(8,128)(2,1)S(1)} collective-permute-done((bf16[192,4096]{1,0:T(8,128)(2,1)S(1)}, bf16[192,4096]{1,0:T(8,128)(2,1)S(1)}, u32[]{:S(2)}, u32[]{:S(2)}) %collective-permute-start.3) | collective-permute-done | bytes 1572896 | tf_op jit(solution)/shard_map/ppermute | solution.py:398
  50.7 2.8 %collective-permute-start.4 = (bf16[768,2560]{1,0:T(8,128)(2,1)S(1)}, bf16[768,2560]{1,0:T(8,128)(2,1)}, u32[]{:S(2)}, u32[]{:S(2)}) collective-permute-start(bf16[768,2560]{1,0:T(8,128)(2,1)S(1)} %pad_maximum_fusion), channel_id=1, source_target_pairs={{0,28},{4,24},{8,20},{12,16},{16,12},{20,8},{24,4},{28,0},{1,29},{... | collective-permute-start | bytes 11796488 | tf_op jit(solution)/shard_map/ppermute | solution.py:432
  53.6 1.3 collective-permute-start.5
  54.8 5.1 %collective-permute-start.6 = (bf16[192,4096]{1,0:T(8,128)(2,1)S(1)}, bf16[192,4096]{1,0:T(8,128)(2,1)S(1)}, u32[]{:S(2)}, u32[]{:S(2)}) collective-permute-start(bf16[192,4096]{1,0:T(8,128)(2,1)S(1)} %collective-permute-done.3.refs_1_), channel_id=1, source_target_pairs={{0,1},{1,2},{2,3},{4,5},{5,6},{6,7},{8,9},{9,10},{10,11},{12,13},{... | collective-permute-start | bytes 4718600 | tf_op jit(solution)/shard_map/ppermute | solution.py:414
  60.0 17.6 %projection_0_2.1 = (bf16[192,2048]{1,0:T(8,128)(2,1)S(1)}, f32[16,192]{1,0:T(8,128)S(1)}, bf16[192,2048]{1,0:T(8,128)(2,1)S(1)}) custom-call(s32[13]{0:T(128)S(1)} %pad_add_fusion.1.scalars_ref, bf16[192,4096]{1,0:T(8,128)(2,1)S(1)} %collective-permute-done.refs_0_, bf16[192,4096]{1,0:T(8,128)(2,1)S(1)} %collective-permute-done.3.refs_1_, ...), custom_call_target="tpu_custom_call" | custom-call | flops 17999998976 | bytes 1 | tf_op jit(solution)/shard_map/projection_0_2/pallas_call | solution.py:525
  77.6 0.0 collective-permute-done.2.refs_0_
  77.6 0.0 collective-permute-done.1.refs_2_
  77.6 1.4 broadcast_select_fusion.1
  79.0 0.8 collective-permute-start.11
  79.7 1.3 collective-permute-start.10
  81.0 25.2 %collective-permute-done.5.refs_1_ = bf16[192,4096]{1,0:T(8,128)(2,1)S(1)} collective-permute-done((bf16[192,4096]{1,0:T(8,128)(2,1)S(1)}, bf16[192,4096]{1,0:T(8,128)(2,1)S(1)}, u32[]{:S(2)}, u32[]{:S(2)}) %collective-permute-start.5) | collective-permute-done | bytes 1572896 | tf_op jit(solution)/shard_map/ppermute | solution.py:415
  106.2 0.0 collective-permute-done.6.refs_3_
  106.2 1.9 broadcast_select_fusion
  108.1 1.3 collective-permute-start.13
  109.4 0.8 collective-permute-start.15
  110.2 17.6 %projection_1_2.1 = (bf16[192,2048]{1,0:T(8,128)(2,1)S(1)}, f32[16,192]{1,0:T(8,128)S(1)}, bf16[192,2048]{1,0:T(8,128)(2,1)S(1)}) custom-call(s32[13]{0:T(128)S(1)} %pad_add_fusion.1.scalars_ref, bf16[192,4096]{1,0:T(8,128)(2,1)S(1)} %collective-permute-done.2.refs_0_, bf16[192,4096]{1,0:T(8,128)(2,1)S(1)} %collective-permute-done.5.refs_1_, ...), custom_call_target="tpu_custom_call" | custom-call | flops 17999998976 | bytes 1 | tf_op jit(solution)/shard_map/projection_1_2/pallas_call | solution.py:525
  127.8 0.9 copy-done.12
  128.7 0.0 collective-permute-done.11.rest_2_.refs_1_.refs_2_
  128.7 11.2 %collective-permute-done.10.rest_1_.refs_2_ = bf16[192,4096]{1,0:T(8,128)(2,1)S(1)} collective-permute-done((bf16[192,4096]{1,0:T(8,128)(2,1)}, bf16[192,4096]{1,0:T(8,128)(2,1)S(1)}, u32[]{:S(2)}, u32[]{:S(2)}) %collective-permute-start.10) | collective-permute-done | bytes 1572896 | tf_op jit(solution)/shard_map/ppermute | solution.py:427
  139.9 20.9 %forward.1 = (bf16[768,2048]{1,0:T(8,128)(2,1)S(1)}, f32[4,2,1,1536]{3,2,1,0:T(1,128)S(1)}, f32[4,16,192]{2,1,0:T(8,128)S(1)}) custom-call(s32[13]{0:T(128)S(1)} %pad_add_fusion.1.scalars_ref, bf16[768,2560]{1,0:T(8,128)(2,1)} %collective-permute-done.4.q_ref.k_ref.v_ref.refs_2_.refs_4_.refs_5_.refs_7_.refs_8_, ...), custom_call_target="tpu_custom_call" | custom-call | flops 20000000000 | bytes 1 | tf_op jit(solution)/shard_map/forward/pallas_call | solution.py:566
  160.8 3.5 %collective-permute-start.16 = (f32[4,16,192]{2,1,0:T(8,128)S(1)}, f32[4,16,192]{2,1,0:T(8,128)S(1)}, u32[]{:S(2)}, u32[]{:S(2)}) collective-permute-start(f32[4,16,192]{2,1,0:T(8,128)S(1)} %get-tuple-element.77), channel_id=1, source_target_pairs={{0,1},{1,2},{2,3},{3,0},{4,5},{5,6},{6,7},{7,4},{8,9},{9,10},{10,1... | collective-permute-start | bytes 147464 | tf_op jit(solution)/shard_map/ppermute | solution.py:603
  164.3 2.3 collective-permute-start.17
  166.6 2.6 collective-permute-start.18
  169.2 5.8 %backward_0.1 = (bf16[768,2048]{1,0:T(8,128)(2,1)}, f32[768,256]{1,0:T(8,128)S(1)}, f32[768,256]{1,0:T(8,128)S(1)}, f32[16,2048]{1,0:T(8,128)S(1)}) custom-call(s32[13]{0:T(128)S(1)} %pad_add_fusion.1.scalars_ref, bf16[192,2048]{1,0:T(8,128)(2,1)S(1)} %get-tuple-element.59.refs_0_, f32[16,192]{1,0:T(8,128)S(1)} %get-tuple-element.51.refs_7_.refs_1_, ...), custom_call_target="tpu_custom_call" | custom-call | flops 8000000000 | bytes 1 | tf_op jit(solution)/shard_map/backward_0/pallas_call | solution.py:686
  175.0 0.0 collective-permute-done.13.refs_13_.refs_3_
  175.0 1.1 copy-done.1
  176.2 1.3 collective-permute-start.12
  177.5 1.4 copy-done.2
  178.9 7.7 %backward_1.1 = (bf16[768,2048]{1,0:T(8,128)(2,1)}, f32[768,256]{1,0:T(8,128)S(1)}, f32[768,256]{1,0:T(8,128)S(1)}, f32[16,2048]{1,0:T(8,128)S(1)}) custom-call(s32[13]{0:T(128)S(1)} %pad_add_fusion.1.scalars_ref, bf16[192,2048]{1,0:T(8,128)(2,1)S(1)} %get-tuple-element.57.refs_0_, ...), custom_call_target="tpu_custom_call", output_to_operand_aliasing={{0}: (10, {})} | custom-call | flops 8000000000 | bytes 1 | tf_op jit(solution)/shard_map/backward_1/pallas_call | solution.py:686
  186.6 17.6 %projection_2_2.1 = (bf16[192,2048]{1,0:T(8,128)(2,1)S(1)}, f32[16,192]{1,0:T(8,128)S(1)}, bf16[192,2048]{1,0:T(8,128)(2,1)S(1)}) custom-call(s32[13]{0:T(128)S(1)} %pad_add_fusion.1.scalars_ref, bf16[192,4096]{1,0:T(8,128)(2,1)S(1)} %collective-permute-done.2.refs_0_, bf16[192,4096]{1,0:T(8,128)(2,1)S(1)} %collective-permute-done.5.refs_1_, ...), custom_call_target="tpu_custom_call" | custom-call | flops 17999998976 | bytes 1 | tf_op jit(solution)/shard_map/projection_2_2/pallas_call | solution.py:525
  204.2 1.5 collective-permute-start.14
  205.8 1.9 copy-done.4
  207.7 1.1 copy-done.7
  208.8 1.1 copy-done.9
  209.9 7.7 %backward_2.1 = (bf16[768,2048]{1,0:T(8,128)(2,1)}, f32[768,256]{1,0:T(8,128)S(1)}, f32[768,256]{1,0:T(8,128)S(1)}, f32[16,2048]{1,0:T(8,128)S(1)}) custom-call(s32[13]{0:T(128)S(1)} %pad_add_fusion.1.scalars_ref, bf16[192,2048]{1,0:T(8,128)(2,1)S(1)} %get-tuple-element.68.refs_0_, ...), custom_call_target="tpu_custom_call", output_to_operand_aliasing={{0}: (10, {})} | custom-call | flops 8000000000 | bytes 1 | tf_op jit(solution)/shard_map/backward_2/pallas_call | solution.py:686
  217.7 0.0 collective-permute-done.12.refs_0_
  217.7 10.4 %projection_3_1.1 = (f32[192,2048]{1,0:T(8,128)S(1)}, f32[16,192]{1,0:T(8,128)S(1)}) custom-call(s32[13]{0:T(128)S(1)} %pad_add_fusion.1.scalars_ref, bf16[192,4096]{1,0:T(8,128)(2,1)S(1)} %collective-permute-done.12.refs_0_, bf16[192,4096]{1,0:T(8,128)(2,1)S(1)} %collective-permute-done.11.rest_2_.refs_1_.refs_2_, bf16[2048,8192]{1,0:T(8,128)(2,1)} %bitcast.39, ...), custom_call_target="tpu_custom_call" | custom-call | flops 8999999488 | bytes 1 | tf_op jit(solution)/shard_map/projection_3_1/pallas_call | solution.py:525
  228.1 1.4 up_map.1.refs_2_
  229.5 16.2 %collective-permute-done.14.refs_1_ = bf16[192,4096]{1,0:T(8,128)(2,1)S(1)} collective-permute-done((bf16[192,4096]{1,0:T(8,128)(2,1)}, bf16[192,4096]{1,0:T(8,128)(2,1)S(1)}, u32[]{:S(2)}, u32[]{:S(2)}) %collective-permute-start.14) | collective-permute-done | bytes 1572896 | tf_op jit(solution)/shard_map/ppermute | solution.py:427
  245.7 11.0 %projection_3_2.1 = (bf16[192,2048]{1,0:T(8,128)(2,1)S(1)}, f32[16,192]{1,0:T(8,128)S(1)}, bf16[192,2048]{1,0:T(8,128)(2,1)S(1)}) custom-call(s32[13]{0:T(128)S(1)} %pad_add_fusion.1.scalars_ref, bf16[192,4096]{1,0:T(8,128)(2,1)S(1)} %collective-permute-done.12.refs_0_, bf16[192,4096]{1,0:T(8,128)(2,1)S(1)} %collective-permute-done.14.refs_1_, ...), custom_call_target="tpu_custom_call" | custom-call | flops 8999999488 | bytes 1 | tf_op jit(solution)/shard_map/projection_3_2/pallas_call | solution.py:525
  256.7 9.8 %backward_3.1 = (bf16[768,2048]{1,0:T(8,128)(2,1)}, bf16[768,256]{1,0:T(8,128)(2,1)}, bf16[768,256]{1,0:T(8,128)(2,1)}, f32[16,2048]{1,0:T(8,128)}, f32[16,2048]{1,0:T(8,128)}) custom-call(s32[13]{0:T(128)S(1)} %pad_add_fusion.1.scalars_ref, bf16[192,2048]{1,0:T(8,128)(2,1)S(1)} %get-tuple-element.76.refs_0_, ...), custom_call_target="tpu_custom_call", output_to_operand_aliasing={{0}: (13, {})} | custom-call | flops 8000000000 | bytes 1 | tf_op jit(solution)/shard_map/backward_3/pallas_call | solution.py:686
  (51 shorter events, 0.2 us)
Async XLA Ops:
  0.6 7.4 %copy-start.19 = (s32[1,768]{1,0:T(1,128)S(1)}, s32[1,768]{1,0:T(1,128)}, u32[]{:S(2)}) copy-start(s32[1,768]{1,0:T(1,128)} %param.16) | copy-start | bytes 9220
  0.6 8.8 %copy-start.17 = (bf16[1,768,256]{2,1,0:T(8,128)(2,1)S(1)}, bf16[1,768,256]{2,1,0:T(8,128)(2,1)}, u32[]{:S(2)}) copy-start(bf16[1,768,256]{2,1,0:T(8,128)(2,1)} %param.14) | copy-start | bytes 1179652
  0.7 8.7 %copy-start.16 = (bf16[1,768,256]{2,1,0:T(8,128)(2,1)S(1)}, bf16[1,768,256]{2,1,0:T(8,128)(2,1)}, u32[]{:S(2)}) copy-start(bf16[1,768,256]{2,1,0:T(8,128)(2,1)} %param.15) | copy-start | bytes 1179652
  4.7 21.6 %collective-permute-start = (bf16[192,4096]{1,0:T(8,128)(2,1)}, bf16[192,4096]{1,0:T(8,128)(2,1)S(1)}, u32[]{:S(2)}, u32[]{:S(2)}) collective-permute-start(bf16[192,4096]{1,0:T(8,128)(2,1)} %get-tuple-element.96), channel_id=1, source_target_pairs={{4,0},{8,4},{12,8},{16,12},{20,16},{24,20},{28,24},{0,28},{5,1},{9... | collective-permute-start | bytes 4718600 | tf_op jit(solution)/shard_map/ppermute | solution.py:398
  9.4 16.9 %copy-start.18 = (bf16[1,16,2048]{2,1,0:T(8,128)(2,1)S(1)}, bf16[1,16,2048]{2,1,0:T(8,128)(2,1)}, u32[]{:S(2)}) copy-start(bf16[1,16,2048]{2,1,0:T(8,128)(2,1)} %param.12) | copy-start | bytes 196612
  9.4 21.5 %copy-start.14 = (bf16[192,4096]{1,0:T(8,128)(2,1)S(1)}, bf16[192,4096]{1,0:T(8,128)(2,1)}, u32[]{:S(2)}) copy-start(bf16[192,4096]{1,0:T(8,128)(2,1)} %get-tuple-element.48) | copy-start | bytes 4718596
  11.6 48.3 %copy-start = (bf16[1,16,2048]{2,1,0:T(8,128)(2,1)S(1)}, bf16[1,16,2048]{2,1,0:T(8,128)(2,1)}, u32[]{:S(2)}) copy-start(bf16[1,16,2048]{2,1,0:T(8,128)(2,1)} %param.11) | copy-start | bytes 196612
  26.3 7.8 %collective-permute-start.7 = (bf16[16,2048]{1,0:T(8,128)(2,1)S(1)}, bf16[16,2048]{1,0:T(8,128)(2,1)S(1)}, u32[]{:S(2)}, u32[]{:S(2)}) collective-permute-start(bf16[16,2048]{1,0:T(8,128)(2,1)S(1)} %bitcast.44), channel_id=1, source_target_pairs={{0,3},{1,0},{2,1},{3,2},{4,7},{5,4},{6,5},{7,6},{8,11},{9,8},{10,9... | collective-permute-start | bytes 196616 | tf_op jit(solution)/shard_map/ppermute | solution.py:386
  29.9 9.3 %collective-permute-start.8 = (bf16[16,2048]{1,0:T(8,128)(2,1)S(1)}, bf16[16,2048]{1,0:T(8,128)(2,1)S(1)}, u32[]{:S(2)}, u32[]{:S(2)}) collective-permute-start(bf16[16,2048]{1,0:T(8,128)(2,1)S(1)} %bitcast.45), channel_id=1, source_target_pairs={{0,2},{1,3},{2,0},{3,1},{4,6},{5,7},{6,4},{7,5},{8,10},{9,11},{10,... | collective-permute-start | bytes 196616 | tf_op jit(solution)/shard_map/ppermute | solution.py:386
  29.9 9.3 %collective-permute-start.9 = (bf16[16,2048]{1,0:T(8,128)(2,1)S(1)}, bf16[16,2048]{1,0:T(8,128)(2,1)S(1)}, u32[]{:S(2)}, u32[]{:S(2)}) collective-permute-start(bf16[16,2048]{1,0:T(8,128)(2,1)S(1)} %bitcast.46), channel_id=1, source_target_pairs={{0,1},{1,2},{2,3},{3,0},{4,5},{5,6},{6,7},{7,4},{8,9},{9,10},{10,1... | collective-permute-start | bytes 196616 | tf_op jit(solution)/shard_map/ppermute | solution.py:386
  31.0 19.8 %collective-permute-start.3 = (bf16[192,4096]{1,0:T(8,128)(2,1)S(1)}, bf16[192,4096]{1,0:T(8,128)(2,1)S(1)}, u32[]{:S(2)}, u32[]{:S(2)}) collective-permute-start(bf16[192,4096]{1,0:T(8,128)(2,1)S(1)} %copy-done.14), channel_id=1, source_target_pairs={{4,0},{8,4},{12,8},{16,12},{20,16},{24,20},{28,24},{0,28},{5,1},{9... | collective-permute-start | bytes 4718600 | tf_op jit(solution)/shard_map/ppermute | solution.py:398
  32.8 44.8 %collective-permute-start.2 = (bf16[192,4096]{1,0:T(8,128)(2,1)S(1)}, bf16[192,4096]{1,0:T(8,128)(2,1)S(1)}, u32[]{:S(2)}, u32[]{:S(2)}) collective-permute-start(bf16[192,4096]{1,0:T(8,128)(2,1)S(1)} %collective-permute-done.refs_0_), channel_id=1, source_target_pairs={{1,0},{2,1},{3,2},{5,4},{6,5},{7,6},{9,8},{10,9},{11,10},{13,12},{... | collective-permute-start | bytes 4718600 | tf_op jit(solution)/shard_map/ppermute | solution.py:415
  34.1 43.5 %collective-permute-start.1 = (bf16[192,4096]{1,0:T(8,128)(2,1)S(1)}, bf16[192,4096]{1,0:T(8,128)(2,1)S(1)}, u32[]{:S(2)}, u32[]{:S(2)}) collective-permute-start(bf16[192,4096]{1,0:T(8,128)(2,1)S(1)} %collective-permute-done.refs_0_), channel_id=1, source_target_pairs={{0,1},{1,2},{2,3},{4,5},{5,6},{6,7},{8,9},{9,10},{10,11},{12,13},{... | collective-permute-start | bytes 4718600 | tf_op jit(solution)/shard_map/ppermute | solution.py:414
  50.7 89.2 %collective-permute-start.4 = (bf16[768,2560]{1,0:T(8,128)(2,1)S(1)}, bf16[768,2560]{1,0:T(8,128)(2,1)}, u32[]{:S(2)}, u32[]{:S(2)}) collective-permute-start(bf16[768,2560]{1,0:T(8,128)(2,1)S(1)} %pad_maximum_fusion), channel_id=1, source_target_pairs={{0,28},{4,24},{8,20},{12,16},{16,12},{20,8},{24,4},{28,0},{1,29},{... | collective-permute-start | bytes 11796488 | tf_op jit(solution)/shard_map/ppermute | solution.py:432
  53.6 52.6 %collective-permute-start.5 = (bf16[192,4096]{1,0:T(8,128)(2,1)S(1)}, bf16[192,4096]{1,0:T(8,128)(2,1)S(1)}, u32[]{:S(2)}, u32[]{:S(2)}) collective-permute-start(bf16[192,4096]{1,0:T(8,128)(2,1)S(1)} %collective-permute-done.3.refs_1_), channel_id=1, source_target_pairs={{1,0},{2,1},{3,2},{5,4},{6,5},{7,6},{9,8},{10,9},{11,10},{13,12},{... | collective-permute-start | bytes 4718600 | tf_op jit(solution)/shard_map/ppermute | solution.py:415
  54.8 51.4 %collective-permute-start.6 = (bf16[192,4096]{1,0:T(8,128)(2,1)S(1)}, bf16[192,4096]{1,0:T(8,128)(2,1)S(1)}, u32[]{:S(2)}, u32[]{:S(2)}) collective-permute-start(bf16[192,4096]{1,0:T(8,128)(2,1)S(1)} %collective-permute-done.3.refs_1_), channel_id=1, source_target_pairs={{0,1},{1,2},{2,3},{4,5},{5,6},{6,7},{8,9},{9,10},{10,11},{12,13},{... | collective-permute-start | bytes 4718600 | tf_op jit(solution)/shard_map/ppermute | solution.py:414
  77.6 1.4 copy-start.10
  79.0 48.8 %copy-start.15 = (bf16[192,4096]{1,0:T(8,128)(2,1)}, bf16[192,4096]{1,0:T(8,128)(2,1)S(1)}, u32[]{:S(2)}) copy-start(bf16[192,4096]{1,0:T(8,128)(2,1)S(1)} %get-tuple-element.56) | copy-start | bytes 4718596
  79.0 49.7 %collective-permute-start.11 = (bf16[192,4096]{1,0:T(8,128)(2,1)S(1)}, bf16[192,4096]{1,0:T(8,128)(2,1)S(1)}, u32[]{:S(2)}, u32[]{:S(2)}) collective-permute-start(bf16[192,4096]{1,0:T(8,128)(2,1)S(1)} %get-tuple-element.56), channel_id=1, source_target_pairs={{1,2},{2,1},{5,6},{6,5},{9,10},{10,9},{13,14},{14,13},{17,18},{18,... | collective-permute-start | bytes 4718600 | tf_op jit(solution)/shard_map/ppermute | solution.py:427
  79.7 60.2 %collective-permute-start.10 = (bf16[192,4096]{1,0:T(8,128)(2,1)}, bf16[192,4096]{1,0:T(8,128)(2,1)S(1)}, u32[]{:S(2)}, u32[]{:S(2)}) collective-permute-start(bf16[192,4096]{1,0:T(8,128)(2,1)} %get-tuple-element.53), channel_id=1, source_target_pairs={{1,0},{2,3},{5,4},{6,7},{9,8},{10,11},{13,12},{14,15},{17,16},{18,... | collective-permute-start | bytes 4718600 | tf_op jit(solution)/shard_map/ppermute | solution.py:427
  108.1 66.9 %collective-permute-start.13 = (bf16[192,4096]{1,0:T(8,128)(2,1)}, bf16[192,4096]{1,0:T(8,128)(2,1)S(1)}, u32[]{:S(2)}, u32[]{:S(2)}) collective-permute-start(bf16[192,4096]{1,0:T(8,128)(2,1)} %get-tuple-element.64), channel_id=1, source_target_pairs={{1,0},{2,3},{5,4},{6,7},{9,8},{10,11},{13,12},{14,15},{17,16},{18,... | collective-permute-start | bytes 4718600 | tf_op jit(solution)/shard_map/ppermute | solution.py:427
  109.4 120.1 %collective-permute-start.15 = (bf16[192,4096]{1,0:T(8,128)(2,1)}, bf16[192,4096]{1,0:T(8,128)(2,1)S(1)}, u32[]{:S(2)}, u32[]{:S(2)}) collective-permute-start(bf16[192,4096]{1,0:T(8,128)(2,1)} %get-tuple-element.67), channel_id=1, source_target_pairs={{1,2},{2,1},{5,6},{6,5},{9,10},{10,9},{13,14},{14,13},{17,18},{18,... | collective-permute-start | bytes 4718600 | tf_op jit(solution)/shard_map/ppermute | solution.py:427
  127.8 0.9 copy-start.12
  160.8 16.7 %copy-start.3 = (bf16[768,2048]{1,0:T(8,128)(2,1)}, bf16[768,2048]{1,0:T(8,128)(2,1)S(1)}, u32[]{:S(2)}) copy-start(bf16[768,2048]{1,0:T(8,128)(2,1)S(1)} %get-tuple-element.58.refs_3_.refs_6_) | copy-start | bytes 9437188
  160.8 43.4 %collective-permute-start.16 = (f32[4,16,192]{2,1,0:T(8,128)S(1)}, f32[4,16,192]{2,1,0:T(8,128)S(1)}, u32[]{:S(2)}, u32[]{:S(2)}) collective-permute-start(f32[4,16,192]{2,1,0:T(8,128)S(1)} %get-tuple-element.77), channel_id=1, source_target_pairs={{0,1},{1,2},{2,3},{3,0},{4,5},{5,6},{6,7},{7,4},{8,9},{9,10},{10,1... | collective-permute-start | bytes 147464 | tf_op jit(solution)/shard_map/ppermute | solution.py:603
  164.3 53.3 %collective-permute-start.17 = (f32[4,16,192]{2,1,0:T(8,128)S(1)}, f32[4,16,192]{2,1,0:T(8,128)S(1)}, u32[]{:S(2)}, u32[]{:S(2)}) collective-permute-start(f32[4,16,192]{2,1,0:T(8,128)S(1)} %get-tuple-element.77), channel_id=1, source_target_pairs={{0,2},{1,3},{2,0},{3,1},{4,6},{5,7},{6,4},{7,5},{8,10},{9,11},{10,... | collective-permute-start | bytes 147464 | tf_op jit(solution)/shard_map/ppermute | solution.py:603
  166.6 51.0 %collective-permute-start.18 = (f32[4,16,192]{2,1,0:T(8,128)S(1)}, f32[4,16,192]{2,1,0:T(8,128)S(1)}, u32[]{:S(2)}, u32[]{:S(2)}) collective-permute-start(f32[4,16,192]{2,1,0:T(8,128)S(1)} %get-tuple-element.77), channel_id=1, source_target_pairs={{0,3},{1,0},{2,1},{3,2},{4,7},{5,4},{6,5},{7,6},{8,11},{9,8},{10,9... | collective-permute-start | bytes 147464 | tf_op jit(solution)/shard_map/ppermute | solution.py:603
  175.0 1.1 copy-start.1
  176.2 41.5 %collective-permute-start.12 = (bf16[192,4096]{1,0:T(8,128)(2,1)}, bf16[192,4096]{1,0:T(8,128)(2,1)S(1)}, u32[]{:S(2)}, u32[]{:S(2)}) collective-permute-start(bf16[192,4096]{1,0:T(8,128)(2,1)} %copy-done.15), channel_id=1, source_target_pairs={{1,3},{2,0},{5,7},{6,4},{9,11},{10,8},{13,15},{14,12},{17,19},{18,... | collective-permute-start | bytes 4718600 | tf_op jit(solution)/shard_map/ppermute | solution.py:427
  177.5 1.4 copy-start.2
  186.6 17.6 %copy-start.6 = (f32[768,256]{1,0:T(8,128)}, f32[768,256]{1,0:T(8,128)S(1)}, u32[]{:S(2)}) copy-start(f32[768,256]{1,0:T(8,128)S(1)} %get-tuple-element.71.refs_10_) | copy-start | bytes 2359300
  186.6 17.6 %copy-start.8 = (f32[768,256]{1,0:T(8,128)}, f32[768,256]{1,0:T(8,128)S(1)}, u32[]{:S(2)}) copy-start(f32[768,256]{1,0:T(8,128)S(1)} %get-tuple-element.72.refs_11_) | copy-start | bytes 2359300
  204.2 41.5 %collective-permute-start.14 = (bf16[192,4096]{1,0:T(8,128)(2,1)}, bf16[192,4096]{1,0:T(8,128)(2,1)S(1)}, u32[]{:S(2)}, u32[]{:S(2)}) collective-permute-start(bf16[192,4096]{1,0:T(8,128)(2,1)} %get-tuple-element.67), channel_id=1, source_target_pairs={{1,3},{2,0},{5,7},{6,4},{9,11},{10,8},{13,15},{14,12},{17,19},{18,... | collective-permute-start | bytes 4718600 | tf_op jit(solution)/shard_map/ppermute | solution.py:427
  205.8 1.9 copy-start.4
  207.7 1.1 copy-start.7
  208.8 1.1 copy-start.9
  217.7 10.4 %copy-start.11 = (bf16[192,2048]{1,0:T(8,128)(2,1)S(1)}, bf16[192,2048]{1,0:T(8,128)(2,1)}, u32[]{:S(2)}) copy-start(bf16[192,2048]{1,0:T(8,128)(2,1)} %copy-done.10) | copy-start | bytes 2359300
  217.7 10.4 %copy-start.13 = (bf16[192,2048]{1,0:T(8,128)(2,1)S(1)}, bf16[192,2048]{1,0:T(8,128)(2,1)}, u32[]{:S(2)}) copy-start(bf16[192,2048]{1,0:T(8,128)(2,1)} %copy-done.12) | copy-start | bytes 2359300
  245.7 11.0 %copy-start.5 = (bf16[768,2048]{1,0:T(8,128)(2,1)S(1)}, bf16[768,2048]{1,0:T(8,128)(2,1)}, u32[]{:S(2)}) copy-start(bf16[768,2048]{1,0:T(8,128)(2,1)} %copy-done.3) | copy-start | bytes 9437188

commit v5 on v4

--- a/solution.py
+++ b/solution.py
@@ -414,7 +414,7 @@
         rising.append([lax.ppermute(after(p, token), "fsdp", up_pairs) for p in rising[-1]])
         falling.append([lax.ppermute(after(p, token), "fsdp", down_pairs) for p in falling[-1]])
 
-    def cross(piece, kind, token):
+    def cross(piece, kind, token, columns=slice(None)):
         routes = {
             "near": [(1, 0), (2, 3)],
             "middle": [(1, 2), (2, 1)],
@@ -422,7 +422,7 @@
         }
         rose, fell = rising[1][piece], falling[1][piece]
         first = member == (2 if kind == "near" else 1)
-        part = jnp.where(first, rose, fell)
+        part = jnp.where(first, rose, fell)[:, columns]
         crossing.setdefault(kind, []).append(
             lax.ppermute(after(part, token), "fsdp", routes[kind])
         )
@@ -463,7 +463,11 @@
             else:
                 way, k = name.split()
                 parts = (rising if way == "rising" else falling)[int(k)]
-            groups.append([(part, 0, part.shape[1]) for part in parts])
+            group = [(part, 0, part.shape[1]) for part in parts]
+            if line == 4 and order == line - 2 and len(group) == 2:
+                half = widths[1] // 2
+                group = [group[0], (parts[1], 0, half), (parts[1], half, half)]
+            groups.append(group)
         return groups
 
     rows_f = total // 4
@@ -534,7 +538,7 @@
                 scratch_shapes=scratch,
             ),
             out_shape=out_shape,
-            **options(f"projection_{order + 1}_{high}", 18 * width / model_width),
+            **options(f"projection_{order + 1}_to_{high}", 18 * width / model_width),
         )(scalars, *operands)
 
     projected = [projection(-1, [])]
@@ -601,6 +605,8 @@
     for d in range(1, line):
         route = [(i, (i + d) % line) for i in range(line)]
         rank_context = rank_context + lax.ppermute(rank_portion, "fsdp", route)
+        if d == 1:
+            begun = rank_context
 
     rows = shard
     heads = group
@@ -707,14 +713,19 @@
     for order in range(line - 2):
         if order:
             projected.append(projection(order, [state[3]]))
-        pins = [crossing["near"][1]] if line == 4 and order == 0 else []
+        pins = [crossing["near"][1] if order == 0 else begun] if line == 4 else []
         state = backward(order, state, projected[order + 1], after=pins)
         if line != 4:
             pass_on(state[3])
         elif order == 0:
-            cross(1, "far", state[3])
-
-    sums = projection(line - 2, [state[3]], 0, 1)
+            half = widths[1] // 2
+            cross(1, "far", state[3], slice(0, half))
+            cross(1, "far", state[3], slice(half, None))
+
+    last_piece = len(choices(line - 2)[0]) - 1
+    sums = ()
+    for p in range(last_piece):
+        sums = projection(line - 2, [state[3]], p, p + 1, sums)
 
     count = line - 1
     up_map = pl.pallas_call(
@@ -732,7 +743,7 @@
         out_shape=jax.ShapeDtypeStruct((rank, local_width), f32),
         **options("up_map", 3),
     )(scalars, *([ranks] * count), *[p[2] for p in projected], sums[1])
-    end = projection(line - 2, [], 1, 2, sums)
+    end = projection(line - 2, [], last_piece, None, sums)
     query_gradient, key_gradient, value_gradient, down_map, up_map = backward(
         line - 2, state, end, up_map
     )

time: 267 us -> 264 us (0.989)
  waiting for transfers between devices: 78.6 us -> 65.7 us
  Pallas kernels: 128 us -> 131 us
  local copies, waits for them, and re-layouts: 12.9 us -> 15.6 us
    ppermute x6 -> x7, waiting for transfers between devices: 27.4 us -> 14.6 us  [cross(): lax.ppermute(after(part, token), 'fsdp', routes[kind])]
    pallas_call x5 -> x6, Pallas kernels: 74.2 us -> 77.5 us  [projection(): pl.pallas_call(functools.partial(projection_kernel, (3 + 2 * order, place...]
    slice x0 -> x1, local copies, waits for them, and re-layouts: none -> 2.7 us  [cross(): part = jnp.where(first, rose, fell)[:, columns]]
    ppermute x6 -> x7, starting transfers between devices: 6.88 us -> 8.17 us  [cross(): lax.ppermute(after(part, token), 'fsdp', routes[kind])]
    unnamed x47 -> x45, local copies, waits for them, and re-layouts: 7.69 us -> 7.69 us
  transfers between devices with their start and end apart: 19 -> 20, of which waited for: 5 -> 6; matrix products, arithmetic and copies ran while one was open for 3% -> 4% of each run, Pallas kernels for 40% -> 44%
where the time goes in v5:
time: 264 us; the launch traced here: 261 us
  Pallas kernels  131 us (50%)
  waiting for transfers between devices  65.7 us (25%)
  starting transfers between devices  41.9 us (16%)
  local copies, waits for them, and re-layouts  15.6 us (6%)
  other arithmetic  5.72 us (2%)
    pallas_call x6, Pallas kernels, projection(): pl.pallas_call(functools.partial(projection_kernel, (3 + 2 * order, place...  77.5 us
    pallas_call x4, Pallas kernels, backward(): pl.pallas_call(functools.partial(backward_kernel, (here, grain, first, la...  31.1 us
    ppermute x2, waiting for transfers between devices, per_device(): own.append(lax.ppermute(part, 'pipe', from_next))  26 us
    ppermute x2, waiting for transfers between devices, pass_on(): lax.ppermute(after(p, token), 'fsdp', down_pairs)  25.2 us
    pallas_call x1, Pallas kernels, per_device(): pl.pallas_call(functools.partial(forward_kernel, grain), grid_spec=pltpu....  20.9 us
    ppermute x7, waiting for transfers between devices, cross(): lax.ppermute(after(part, token), 'fsdp', routes[kind])  14.6 us
    ppermute x2, starting transfers between devices, pass_on(): lax.ppermute(after(p, token), 'fsdp', up_pairs)  10.2 us
    ppermute x3, starting transfers between devices, per_device(): rank_context = rank_context + lax.ppermute(rank_portion, 'fsdp', route)  8.39 us
  transfers between devices with their start and end apart: 20, of which 6 were waited for; matrix products, arithmetic and copies ran while one was open for 4% of the time, Pallas kernels for 44%

profile of v5, /device:TPU:0, one launch (start us, length us, event | category | flops | bytes accessed | tf_op | source)
XLA Modules:
  0.0 261.0 jit_solution(10724575600520187948)
XLA Ops:
  0.7 4.0 %slice_bitcast_fusion = (bf16[192,4096]{1,0:T(8,128)(2,1)}, bf16[192,4096]{1,0:T(8,128)(2,1)}) fusion(bf16[1,192,8192]{2,1,0:T(8,128)(2,1)} %param.9), kind=kLoop, calls=%fused_computation.1 | loop fusion | bytes 6291456 | tf_op jit(solution)/shard_map/squeeze | solution.py:395
  4.7 3.3 %collective-permute-start = (bf16[192,4096]{1,0:T(8,128)(2,1)}, bf16[192,4096]{1,0:T(8,128)(2,1)S(1)}, u32[]{:S(2)}, u32[]{:S(2)}) collective-permute-start(bf16[192,4096]{1,0:T(8,128)(2,1)} %get-tuple-element.104), channel_id=1, source_target_pairs={{4,0},{8,4},{12,8},{16,12},{20,16},{24,20},{28,24},{0,28},{5,1},{9... | collective-permute-start | bytes 4718600 | tf_op jit(solution)/shard_map/ppermute | solution.py:398
  8.0 0.1 slice.15
  8.1 0.1 reshape_squeeze.4
  8.2 0.1 tile.5.row_info_ref.refs_7_.refs_10_
  8.3 0.2 copy.25.ids_ref.refs_6_.refs_9_
  8.5 0.7 dynamic-slice_bitcast_fusion
  9.2 0.2 convert_reduce_fusion
  9.4 0.0 copy-start.17
  9.4 0.0 copy-start.13
  9.4 2.2 pad_maximum_fusion
  11.6 0.0 copy-start
  11.6 14.6 %collective-permute-done.refs_0_ = bf16[192,4096]{1,0:T(8,128)(2,1)S(1)} collective-permute-done((bf16[192,4096]{1,0:T(8,128)(2,1)}, bf16[192,4096]{1,0:T(8,128)(2,1)S(1)}, u32[]{:S(2)}, u32[]{:S(2)}) %collective-permute-start) | collective-permute-done | bytes 1572896 | tf_op jit(solution)/shard_map/ppermute | solution.py:398
  26.3 3.6 %collective-permute-start.7 = (bf16[16,2048]{1,0:T(8,128)(2,1)S(1)}, bf16[16,2048]{1,0:T(8,128)(2,1)S(1)}, u32[]{:S(2)}, u32[]{:S(2)}) collective-permute-start(bf16[16,2048]{1,0:T(8,128)(2,1)S(1)} %bitcast.46), channel_id=1, source_target_pairs={{0,3},{1,0},{2,1},{3,2},{4,7},{5,4},{6,5},{7,6},{8,11},{9,8},{10,9... | collective-permute-start | bytes 196616 | tf_op jit(solution)/shard_map/ppermute | solution.py:386
  29.9 0.1 pad_add_fusion.1.scalars_ref
  29.9 1.0 collective-permute-start.9
  31.0 1.9 collective-permute-start.3
  32.8 1.3 collective-permute-start.2
  34.1 0.0 collective-permute-done.7
  34.1 5.1 %collective-permute-start.1 = (bf16[192,4096]{1,0:T(8,128)(2,1)S(1)}, bf16[192,4096]{1,0:T(8,128)(2,1)S(1)}, u32[]{:S(2)}, u32[]{:S(2)}) collective-permute-start(bf16[192,4096]{1,0:T(8,128)(2,1)S(1)} %collective-permute-done.refs_0_), channel_id=1, source_target_pairs={{0,1},{1,2},{2,3},{4,5},{5,6},{6,7},{8,9},{9,10},{10,11},{12,13},{... | collective-permute-start | bytes 4718600 | tf_op jit(solution)/shard_map/ppermute | solution.py:414
  39.4 11.3 %collective-permute-done.3.refs_1_ = bf16[192,4096]{1,0:T(8,128)(2,1)S(1)} collective-permute-done((bf16[192,4096]{1,0:T(8,128)(2,1)S(1)}, bf16[192,4096]{1,0:T(8,128)(2,1)S(1)}, u32[]{:S(2)}, u32[]{:S(2)}) %collective-permute-start.3) | collective-permute-done | bytes 1572896 | tf_op jit(solution)/shard_map/ppermute | solution.py:398
  50.8 2.8 %collective-permute-start.4 = (bf16[768,2560]{1,0:T(8,128)(2,1)S(1)}, bf16[768,2560]{1,0:T(8,128)(2,1)}, u32[]{:S(2)}, u32[]{:S(2)}) collective-permute-start(bf16[768,2560]{1,0:T(8,128)(2,1)S(1)} %pad_maximum_fusion), channel_id=1, source_target_pairs={{0,28},{4,24},{8,20},{12,16},{16,12},{20,8},{24,4},{28,0},{1,29},{... | collective-permute-start | bytes 11796488 | tf_op jit(solution)/shard_map/ppermute | solution.py:432
  53.6 1.3 collective-permute-start.5
  54.8 5.1 %collective-permute-start.6 = (bf16[192,4096]{1,0:T(8,128)(2,1)S(1)}, bf16[192,4096]{1,0:T(8,128)(2,1)S(1)}, u32[]{:S(2)}, u32[]{:S(2)}) collective-permute-start(bf16[192,4096]{1,0:T(8,128)(2,1)S(1)} %collective-permute-done.3.refs_1_), channel_id=1, source_target_pairs={{0,1},{1,2},{2,3},{4,5},{5,6},{6,7},{8,9},{9,10},{10,11},{12,13},{... | collective-permute-start | bytes 4718600 | tf_op jit(solution)/shard_map/ppermute | solution.py:414
  60.0 17.6 %projection_0_to_2.1 = (bf16[192,2048]{1,0:T(8,128)(2,1)S(1)}, f32[16,192]{1,0:T(8,128)S(1)}, bf16[192,2048]{1,0:T(8,128)(2,1)S(1)}) custom-call(s32[13]{0:T(128)S(1)} %pad_add_fusion.1.scalars_ref, bf16[192,4096]{1,0:T(8,128)(2,1)S(1)} %collective-permute-done.refs_0_, bf16[192,4096]{1,0:T(8,128)(2,1)S(1)} %collective-permute-done.3.refs_1_, ...), custom_call_target="tpu_custom_call" | custom-call | flops 17999998976 | bytes 1 | tf_op jit(solution)/shard_map/projection_0_to_2/pallas_call | solution.py:529
  77.6 0.0 collective-permute-done.1.refs_2_
  77.6 1.4 broadcast_select_fusion.1
  79.0 0.8 collective-permute-start.11
  79.7 1.3 collective-permute-start.10
  81.0 25.2 %collective-permute-done.5.refs_1_ = bf16[192,4096]{1,0:T(8,128)(2,1)S(1)} collective-permute-done((bf16[192,4096]{1,0:T(8,128)(2,1)S(1)}, bf16[192,4096]{1,0:T(8,128)(2,1)S(1)}, u32[]{:S(2)}, u32[]{:S(2)}) %collective-permute-start.5) | collective-permute-done | bytes 1572896 | tf_op jit(solution)/shard_map/ppermute | solution.py:415
  106.2 0.0 collective-permute-done.6.refs_3_
  106.2 1.9 broadcast_select_fusion
  108.1 1.3 collective-permute-start.13
  109.4 0.8 collective-permute-start.16
  110.1 2.7 %fusion = (bf16[192,2048]{1,0:T(8,128)(2,1)}, bf16[192,2048]{1,0:T(8,128)(2,1)}) fusion(bf16[192,4096]{1,0:T(8,128)(2,1)} %get-tuple-element.71), kind=kLoop, calls=%fused_computation.22 | loop fusion | bytes 3145728 | tf_op jit(solution)/shard_map/slice | solution.py:425
  112.8 17.6 %projection_1_to_2.1 = (bf16[192,2048]{1,0:T(8,128)(2,1)S(1)}, f32[16,192]{1,0:T(8,128)S(1)}, bf16[192,2048]{1,0:T(8,128)(2,1)S(1)}) custom-call(s32[13]{0:T(128)S(1)} %pad_add_fusion.1.scalars_ref, bf16[192,4096]{1,0:T(8,128)(2,1)S(1)} %collective-permute-done.2.refs_0_, bf16[192,4096]{1,0:T(8,128)(2,1)S(1)} %collective-permute-done.5.refs_1_, ...), custom_call_target="tpu_custom_call" | custom-call | flops 17999998976 | bytes 1 | tf_op jit(solution)/shard_map/projection_1_to_2/pallas_call | solution.py:529
  130.4 0.9 copy-done.11
  131.3 0.0 collective-permute-done.11.rest_2_.refs_1_.refs_2_.refs_3_
  131.3 8.6 %collective-permute-done.10.rest_1_.refs_2_ = bf16[192,4096]{1,0:T(8,128)(2,1)S(1)} collective-permute-done((bf16[192,4096]{1,0:T(8,128)(2,1)}, bf16[192,4096]{1,0:T(8,128)(2,1)S(1)}, u32[]{:S(2)}, u32[]{:S(2)}) %collective-permute-start.10) | collective-permute-done | bytes 1572896 | tf_op jit(solution)/shard_map/ppermute | solution.py:427
  139.9 0.0 collective-permute-done.4.q_ref.k_ref.v_ref.refs_2_.refs_4_.refs_5_.refs_7_.refs_8_
  139.9 20.9 %forward.1 = (bf16[768,2048]{1,0:T(8,128)(2,1)S(1)}, f32[4,2,1,1536]{3,2,1,0:T(1,128)S(1)}, f32[4,16,192]{2,1,0:T(8,128)S(1)}) custom-call(s32[13]{0:T(128)S(1)} %pad_add_fusion.1.scalars_ref, bf16[768,2560]{1,0:T(8,128)(2,1)} %collective-permute-done.4.q_ref.k_ref.v_ref.refs_2_.refs_4_.refs_5_.refs_7_.refs_8_, ...), custom_call_target="tpu_custom_call" | custom-call | flops 20000000000 | bytes 1 | tf_op jit(solution)/shard_map/forward/pallas_call | solution.py:570
  160.8 3.5 %collective-permute-start.17 = (f32[4,16,192]{2,1,0:T(8,128)S(1)}, f32[4,16,192]{2,1,0:T(8,128)S(1)}, u32[]{:S(2)}, u32[]{:S(2)}) collective-permute-start(f32[4,16,192]{2,1,0:T(8,128)S(1)} %get-tuple-element.77), channel_id=1, source_target_pairs={{0,1},{1,2},{2,3},{3,0},{4,5},{5,6},{6,7},{7,4},{8,9},{9,10},{10,1... | collective-permute-start | bytes 147464 | tf_op jit(solution)/shard_map/ppermute | solution.py:607
  164.3 2.3 collective-permute-start.18
  166.6 2.6 collective-permute-start.19
  169.2 5.8 %backward_0.1 = (bf16[768,2048]{1,0:T(8,128)(2,1)}, f32[768,256]{1,0:T(8,128)S(1)}, f32[768,256]{1,0:T(8,128)S(1)}, f32[16,2048]{1,0:T(8,128)S(1)}) custom-call(s32[13]{0:T(128)S(1)} %pad_add_fusion.1.scalars_ref, bf16[192,2048]{1,0:T(8,128)(2,1)S(1)} %get-tuple-element.62.refs_0_, f32[16,192]{1,0:T(8,128)S(1)} %get-tuple-element.54.refs_7_.refs_1_, ...), custom_call_target="tpu_custom_call" | custom-call | flops 8000000000 | bytes 1 | tf_op jit(solution)/shard_map/backward_0/pallas_call | solution.py:692
  175.0 1.1 copy-done.1
  176.2 1.3 collective-permute-start.12
  177.5 1.4 copy-done.2
  178.9 7.7 %backward_1.1 = (bf16[768,2048]{1,0:T(8,128)(2,1)}, f32[768,256]{1,0:T(8,128)S(1)}, f32[768,256]{1,0:T(8,128)S(1)}, f32[16,2048]{1,0:T(8,128)S(1)}) custom-call(s32[13]{0:T(128)S(1)} %pad_add_fusion.1.scalars_ref, bf16[192,2048]{1,0:T(8,128)(2,1)S(1)} %get-tuple-element.60.refs_0_, ...), custom_call_target="tpu_custom_call", output_to_operand_aliasing={{0}: (10, {})} | custom-call | flops 8000000000 | bytes 1 | tf_op jit(solution)/shard_map/backward_1/pallas_call | solution.py:692
  186.6 17.6 %projection_2_to_2.1 = (bf16[192,2048]{1,0:T(8,128)(2,1)S(1)}, f32[16,192]{1,0:T(8,128)S(1)}, bf16[192,2048]{1,0:T(8,128)(2,1)S(1)}) custom-call(s32[13]{0:T(128)S(1)} %pad_add_fusion.1.scalars_ref, bf16[192,4096]{1,0:T(8,128)(2,1)S(1)} %collective-permute-done.2.refs_0_, bf16[192,4096]{1,0:T(8,128)(2,1)S(1)} %collective-permute-done.5.refs_1_, ...), custom_call_target="tpu_custom_call" | custom-call | flops 17999998976 | bytes 1 | tf_op jit(solution)/shard_map/projection_2_to_2/pallas_call | solution.py:529
  204.3 0.0 collective-permute-done.17
  204.3 1.3 collective-permute-start.14
  205.6 1.5 collective-permute-start.15
  207.1 1.9 copy-done.4
  209.0 1.1 copy-done.6
  210.2 1.1 copy-done.8
  211.3 9.7 %backward_2.1 = (bf16[768,2048]{1,0:T(8,128)(2,1)}, f32[768,256]{1,0:T(8,128)S(1)}, f32[768,256]{1,0:T(8,128)S(1)}, f32[16,2048]{1,0:T(8,128)S(1)}) custom-call(s32[13]{0:T(128)S(1)} %pad_add_fusion.1.scalars_ref, bf16[192,2048]{1,0:T(8,128)(2,1)S(1)} %get-tuple-element.72.refs_0_, ...), custom_call_target="tpu_custom_call", output_to_operand_aliasing={{0}: (10, {})} | custom-call | flops 8000000000 | bytes 1 | tf_op jit(solution)/shard_map/backward_2/pallas_call | solution.py:692
  220.9 10.4 %projection_3_to_1.1 = (f32[192,2048]{1,0:T(8,128)S(1)}, f32[16,192]{1,0:T(8,128)S(1)}) custom-call(s32[13]{0:T(128)S(1)} %pad_add_fusion.1.scalars_ref, bf16[192,4096]{1,0:T(8,128)(2,1)S(1)} %collective-permute-done.12.refs_0_, bf16[192,4096]{1,0:T(8,128)(2,1)S(1)} %collective-permute-done.11.rest_2_.refs_1_.refs_2_.refs_3_, bf16[2048,8192]{1,0:T(8,128)(2,1)} %bitcast.40, ...), custom_call_target="tpu_custom_call" | custom-call | flops 8999999488 | bytes 1 | tf_op jit(solution)/shard_map/projection_3_to_1/pallas_call | solution.py:529
  231.4 2.0 collective-permute-done.14.refs_1_
  233.4 7.0 %projection_3_to_2.1 = (f32[192,2048]{1,0:T(8,128)S(1)}, f32[16,192]{1,0:T(8,128)S(1)}) custom-call(s32[13]{0:T(128)S(1)} %pad_add_fusion.1.scalars_ref, bf16[192,4096]{1,0:T(8,128)(2,1)S(1)} %collective-permute-done.12.refs_0_, bf16[192,2048]{1,0:T(8,128)(2,1)S(1)} %collective-permute-done.14.refs_1_, ...), custom_call_target="tpu_custom_call" | custom-call | flops 4499999744 | bytes 1 | tf_op jit(solution)/shard_map/projection_3_to_2/pallas_call | solution.py:529
  240.4 1.3 up_map.1.refs_2_
  241.7 4.0 %collective-permute-done.15.refs_2_ = bf16[192,2048]{1,0:T(8,128)(2,1)S(1)} collective-permute-done((bf16[192,2048]{1,0:T(8,128)(2,1)}, bf16[192,2048]{1,0:T(8,128)(2,1)S(1)}, u32[]{:S(2)}, u32[]{:S(2)}) %collective-permute-start.15) | collective-permute-done | bytes 786464 | tf_op jit(solution)/shard_map/ppermute | solution.py:427
  245.7 7.3 %projection_3_to_3.1 = (bf16[192,2048]{1,0:T(8,128)(2,1)S(1)}, f32[16,192]{1,0:T(8,128)S(1)}, bf16[192,2048]{1,0:T(8,128)(2,1)S(1)}) custom-call(s32[13]{0:T(128)S(1)} %pad_add_fusion.1.scalars_ref, bf16[192,4096]{1,0:T(8,128)(2,1)S(1)} %collective-permute-done.12.refs_0_, bf16[192,2048]{1,0:T(8,128)(2,1)S(1)} %collective-permute-done.14.refs_1_, ...), custom_call_target="tpu_custom_call" | custom-call | flops 4499999744 | bytes 1 | tf_op jit(solution)/shard_map/projection_3_to_3/pallas_call | solution.py:529
  253.0 7.9 %backward_3.1 = (bf16[768,2048]{1,0:T(8,128)(2,1)}, bf16[768,256]{1,0:T(8,128)(2,1)}, bf16[768,256]{1,0:T(8,128)(2,1)}, f32[16,2048]{1,0:T(8,128)}, f32[16,2048]{1,0:T(8,128)}) custom-call(s32[13]{0:T(128)S(1)} %pad_add_fusion.1.scalars_ref, bf16[192,2048]{1,0:T(8,128)(2,1)S(1)} %get-tuple-element.83.refs_0_, ...), custom_call_target="tpu_custom_call", output_to_operand_aliasing={{0}: (13, {})} | custom-call | flops 8000000000 | bytes 1 | tf_op jit(solution)/shard_map/backward_3/pallas_call | solution.py:692
  (53 shorter events, 0.2 us)
Async XLA Ops:
  0.6 7.4 %copy-start.18 = (s32[1,768]{1,0:T(1,128)S(1)}, s32[1,768]{1,0:T(1,128)}, u32[]{:S(2)}) copy-start(s32[1,768]{1,0:T(1,128)} %param.16) | copy-start | bytes 9220
  0.6 8.8 %copy-start.16 = (bf16[1,768,256]{2,1,0:T(8,128)(2,1)S(1)}, bf16[1,768,256]{2,1,0:T(8,128)(2,1)}, u32[]{:S(2)}) copy-start(bf16[1,768,256]{2,1,0:T(8,128)(2,1)} %param.14) | copy-start | bytes 1179652
  0.7 8.8 %copy-start.15 = (bf16[1,768,256]{2,1,0:T(8,128)(2,1)S(1)}, bf16[1,768,256]{2,1,0:T(8,128)(2,1)}, u32[]{:S(2)}) copy-start(bf16[1,768,256]{2,1,0:T(8,128)(2,1)} %param.15) | copy-start | bytes 1179652
  4.7 21.6 %collective-permute-start = (bf16[192,4096]{1,0:T(8,128)(2,1)}, bf16[192,4096]{1,0:T(8,128)(2,1)S(1)}, u32[]{:S(2)}, u32[]{:S(2)}) collective-permute-start(bf16[192,4096]{1,0:T(8,128)(2,1)} %get-tuple-element.104), channel_id=1, source_target_pairs={{4,0},{8,4},{12,8},{16,12},{20,16},{24,20},{28,24},{0,28},{5,1},{9... | collective-permute-start | bytes 4718600 | tf_op jit(solution)/shard_map/ppermute | solution.py:398
  9.4 16.9 %copy-start.17 = (bf16[1,16,2048]{2,1,0:T(8,128)(2,1)S(1)}, bf16[1,16,2048]{2,1,0:T(8,128)(2,1)}, u32[]{:S(2)}) copy-start(bf16[1,16,2048]{2,1,0:T(8,128)(2,1)} %param.12) | copy-start | bytes 196612
  9.4 21.5 %copy-start.13 = (bf16[192,4096]{1,0:T(8,128)(2,1)S(1)}, bf16[192,4096]{1,0:T(8,128)(2,1)}, u32[]{:S(2)}) copy-start(bf16[192,4096]{1,0:T(8,128)(2,1)} %get-tuple-element.51) | copy-start | bytes 4718596
  11.6 48.3 %copy-start = (bf16[1,16,2048]{2,1,0:T(8,128)(2,1)S(1)}, bf16[1,16,2048]{2,1,0:T(8,128)(2,1)}, u32[]{:S(2)}) copy-start(bf16[1,16,2048]{2,1,0:T(8,128)(2,1)} %param.11) | copy-start | bytes 196612
  26.3 7.8 %collective-permute-start.7 = (bf16[16,2048]{1,0:T(8,128)(2,1)S(1)}, bf16[16,2048]{1,0:T(8,128)(2,1)S(1)}, u32[]{:S(2)}, u32[]{:S(2)}) collective-permute-start(bf16[16,2048]{1,0:T(8,128)(2,1)S(1)} %bitcast.46), channel_id=1, source_target_pairs={{0,3},{1,0},{2,1},{3,2},{4,7},{5,4},{6,5},{7,6},{8,11},{9,8},{10,9... | collective-permute-start | bytes 196616 | tf_op jit(solution)/shard_map/ppermute | solution.py:386
  29.9 9.3 %collective-permute-start.8 = (bf16[16,2048]{1,0:T(8,128)(2,1)S(1)}, bf16[16,2048]{1,0:T(8,128)(2,1)S(1)}, u32[]{:S(2)}, u32[]{:S(2)}) collective-permute-start(bf16[16,2048]{1,0:T(8,128)(2,1)S(1)} %bitcast.47), channel_id=1, source_target_pairs={{0,2},{1,3},{2,0},{3,1},{4,6},{5,7},{6,4},{7,5},{8,10},{9,11},{10,... | collective-permute-start | bytes 196616 | tf_op jit(solution)/shard_map/ppermute | solution.py:386
  29.9 9.3 %collective-permute-start.9 = (bf16[16,2048]{1,0:T(8,128)(2,1)S(1)}, bf16[16,2048]{1,0:T(8,128)(2,1)S(1)}, u32[]{:S(2)}, u32[]{:S(2)}) collective-permute-start(bf16[16,2048]{1,0:T(8,128)(2,1)S(1)} %bitcast.48), channel_id=1, source_target_pairs={{0,1},{1,2},{2,3},{3,0},{4,5},{5,6},{6,7},{7,4},{8,9},{9,10},{10,1... | collective-permute-start | bytes 196616 | tf_op jit(solution)/shard_map/ppermute | solution.py:386
  31.0 19.8 %collective-permute-start.3 = (bf16[192,4096]{1,0:T(8,128)(2,1)S(1)}, bf16[192,4096]{1,0:T(8,128)(2,1)S(1)}, u32[]{:S(2)}, u32[]{:S(2)}) collective-permute-start(bf16[192,4096]{1,0:T(8,128)(2,1)S(1)} %copy-done.13), channel_id=1, source_target_pairs={{4,0},{8,4},{12,8},{16,12},{20,16},{24,20},{28,24},{0,28},{5,1},{9... | collective-permute-start | bytes 4718600 | tf_op jit(solution)/shard_map/ppermute | solution.py:398
  32.8 44.8 %collective-permute-start.2 = (bf16[192,4096]{1,0:T(8,128)(2,1)S(1)}, bf16[192,4096]{1,0:T(8,128)(2,1)S(1)}, u32[]{:S(2)}, u32[]{:S(2)}) collective-permute-start(bf16[192,4096]{1,0:T(8,128)(2,1)S(1)} %collective-permute-done.refs_0_), channel_id=1, source_target_pairs={{1,0},{2,1},{3,2},{5,4},{6,5},{7,6},{9,8},{10,9},{11,10},{13,12},{... | collective-permute-start | bytes 4718600 | tf_op jit(solution)/shard_map/ppermute | solution.py:415
  34.1 43.5 %collective-permute-start.1 = (bf16[192,4096]{1,0:T(8,128)(2,1)S(1)}, bf16[192,4096]{1,0:T(8,128)(2,1)S(1)}, u32[]{:S(2)}, u32[]{:S(2)}) collective-permute-start(bf16[192,4096]{1,0:T(8,128)(2,1)S(1)} %collective-permute-done.refs_0_), channel_id=1, source_target_pairs={{0,1},{1,2},{2,3},{4,5},{5,6},{6,7},{8,9},{9,10},{10,11},{12,13},{... | collective-permute-start | bytes 4718600 | tf_op jit(solution)/shard_map/ppermute | solution.py:414
  50.8 89.2 %collective-permute-start.4 = (bf16[768,2560]{1,0:T(8,128)(2,1)S(1)}, bf16[768,2560]{1,0:T(8,128)(2,1)}, u32[]{:S(2)}, u32[]{:S(2)}) collective-permute-start(bf16[768,2560]{1,0:T(8,128)(2,1)S(1)} %pad_maximum_fusion), channel_id=1, source_target_pairs={{0,28},{4,24},{8,20},{12,16},{16,12},{20,8},{24,4},{28,0},{1,29},{... | collective-permute-start | bytes 11796488 | tf_op jit(solution)/shard_map/ppermute | solution.py:432
  53.6 52.6 %collective-permute-start.5 = (bf16[192,4096]{1,0:T(8,128)(2,1)S(1)}, bf16[192,4096]{1,0:T(8,128)(2,1)S(1)}, u32[]{:S(2)}, u32[]{:S(2)}) collective-permute-start(bf16[192,4096]{1,0:T(8,128)(2,1)S(1)} %collective-permute-done.3.refs_1_), channel_id=1, source_target_pairs={{1,0},{2,1},{3,2},{5,4},{6,5},{7,6},{9,8},{10,9},{11,10},{13,12},{... | collective-permute-start | bytes 4718600 | tf_op jit(solution)/shard_map/ppermute | solution.py:415
  54.8 51.4 %collective-permute-start.6 = (bf16[192,4096]{1,0:T(8,128)(2,1)S(1)}, bf16[192,4096]{1,0:T(8,128)(2,1)S(1)}, u32[]{:S(2)}, u32[]{:S(2)}) collective-permute-start(bf16[192,4096]{1,0:T(8,128)(2,1)S(1)} %collective-permute-done.3.refs_1_), channel_id=1, source_target_pairs={{0,1},{1,2},{2,3},{4,5},{5,6},{6,7},{8,9},{9,10},{10,11},{12,13},{... | collective-permute-start | bytes 4718600 | tf_op jit(solution)/shard_map/ppermute | solution.py:414
  77.6 1.4 copy-start.9
  79.0 33.8 %copy-start.14 = (bf16[192,4096]{1,0:T(8,128)(2,1)}, bf16[192,4096]{1,0:T(8,128)(2,1)S(1)}, u32[]{:S(2)}) copy-start(bf16[192,4096]{1,0:T(8,128)(2,1)S(1)} %get-tuple-element.59) | copy-start | bytes 4718596
  79.0 52.4 %collective-permute-start.11 = (bf16[192,4096]{1,0:T(8,128)(2,1)S(1)}, bf16[192,4096]{1,0:T(8,128)(2,1)S(1)}, u32[]{:S(2)}, u32[]{:S(2)}) collective-permute-start(bf16[192,4096]{1,0:T(8,128)(2,1)S(1)} %get-tuple-element.59), channel_id=1, source_target_pairs={{1,2},{2,1},{5,6},{6,5},{9,10},{10,9},{13,14},{14,13},{17,18},{18,... | collective-permute-start | bytes 4718600 | tf_op jit(solution)/shard_map/ppermute | solution.py:427
  79.7 60.2 %collective-permute-start.10 = (bf16[192,4096]{1,0:T(8,128)(2,1)}, bf16[192,4096]{1,0:T(8,128)(2,1)S(1)}, u32[]{:S(2)}, u32[]{:S(2)}) collective-permute-start(bf16[192,4096]{1,0:T(8,128)(2,1)} %get-tuple-element.56), channel_id=1, source_target_pairs={{1,0},{2,3},{5,4},{6,7},{9,8},{10,11},{13,12},{14,15},{17,16},{18,... | collective-permute-start | bytes 4718600 | tf_op jit(solution)/shard_map/ppermute | solution.py:427
  108.1 67.0 %collective-permute-start.13 = (bf16[192,4096]{1,0:T(8,128)(2,1)}, bf16[192,4096]{1,0:T(8,128)(2,1)S(1)}, u32[]{:S(2)}, u32[]{:S(2)}) collective-permute-start(bf16[192,4096]{1,0:T(8,128)(2,1)} %get-tuple-element.67), channel_id=1, source_target_pairs={{1,0},{2,3},{5,4},{6,7},{9,8},{10,11},{13,12},{14,15},{17,16},{18,... | collective-permute-start | bytes 4718600 | tf_op jit(solution)/shard_map/ppermute | solution.py:427
  109.4 122.0 %collective-permute-start.16 = (bf16[192,4096]{1,0:T(8,128)(2,1)}, bf16[192,4096]{1,0:T(8,128)(2,1)S(1)}, u32[]{:S(2)}, u32[]{:S(2)}) collective-permute-start(bf16[192,4096]{1,0:T(8,128)(2,1)} %get-tuple-element.71), channel_id=1, source_target_pairs={{1,2},{2,1},{5,6},{6,5},{9,10},{10,9},{13,14},{14,13},{17,18},{18,... | collective-permute-start | bytes 4718600 | tf_op jit(solution)/shard_map/ppermute | solution.py:427
  130.4 0.9 copy-start.11
  160.8 16.7 %copy-start.3 = (bf16[768,2048]{1,0:T(8,128)(2,1)}, bf16[768,2048]{1,0:T(8,128)(2,1)S(1)}, u32[]{:S(2)}) copy-start(bf16[768,2048]{1,0:T(8,128)(2,1)S(1)} %get-tuple-element.61.refs_3_.refs_6_) | copy-start | bytes 9437188
  160.8 43.5 %collective-permute-start.17 = (f32[4,16,192]{2,1,0:T(8,128)S(1)}, f32[4,16,192]{2,1,0:T(8,128)S(1)}, u32[]{:S(2)}, u32[]{:S(2)}) collective-permute-start(f32[4,16,192]{2,1,0:T(8,128)S(1)} %get-tuple-element.77), channel_id=1, source_target_pairs={{0,1},{1,2},{2,3},{3,0},{4,5},{5,6},{6,7},{7,4},{8,9},{9,10},{10,1... | collective-permute-start | bytes 147464 | tf_op jit(solution)/shard_map/ppermute | solution.py:607
  164.3 41.2 %collective-permute-start.18 = (f32[4,16,192]{2,1,0:T(8,128)S(1)}, f32[4,16,192]{2,1,0:T(8,128)S(1)}, u32[]{:S(2)}, u32[]{:S(2)}) collective-permute-start(f32[4,16,192]{2,1,0:T(8,128)S(1)} %get-tuple-element.77), channel_id=1, source_target_pairs={{0,2},{1,3},{2,0},{3,1},{4,6},{5,7},{6,4},{7,5},{8,10},{9,11},{10,... | collective-permute-start | bytes 147464 | tf_op jit(solution)/shard_map/ppermute | solution.py:607
  166.6 40.5 %collective-permute-start.19 = (f32[4,16,192]{2,1,0:T(8,128)S(1)}, f32[4,16,192]{2,1,0:T(8,128)S(1)}, u32[]{:S(2)}, u32[]{:S(2)}) collective-permute-start(f32[4,16,192]{2,1,0:T(8,128)S(1)} %get-tuple-element.77), channel_id=1, source_target_pairs={{0,3},{1,0},{2,1},{3,2},{4,7},{5,4},{6,5},{7,6},{8,11},{9,8},{10,9... | collective-permute-start | bytes 147464 | tf_op jit(solution)/shard_map/ppermute | solution.py:607
  175.0 1.1 copy-start.1
  176.2 44.8 %collective-permute-start.12 = (bf16[192,4096]{1,0:T(8,128)(2,1)}, bf16[192,4096]{1,0:T(8,128)(2,1)S(1)}, u32[]{:S(2)}, u32[]{:S(2)}) collective-permute-start(bf16[192,4096]{1,0:T(8,128)(2,1)} %copy-done.14), channel_id=1, source_target_pairs={{1,3},{2,0},{5,7},{6,4},{9,11},{10,8},{13,15},{14,12},{17,19},{18,... | collective-permute-start | bytes 4718600 | tf_op jit(solution)/shard_map/ppermute | solution.py:427
  177.5 1.4 copy-start.2
  186.6 17.6 %copy-start.5 = (f32[768,256]{1,0:T(8,128)}, f32[768,256]{1,0:T(8,128)S(1)}, u32[]{:S(2)}) copy-start(f32[768,256]{1,0:T(8,128)S(1)} %get-tuple-element.75.refs_10_) | copy-start | bytes 2359300
  186.6 17.6 %copy-start.7 = (f32[768,256]{1,0:T(8,128)}, f32[768,256]{1,0:T(8,128)S(1)}, u32[]{:S(2)}) copy-start(f32[768,256]{1,0:T(8,128)S(1)} %get-tuple-element.76.refs_11_) | copy-start | bytes 2359300
  204.3 29.1 %collective-permute-start.14 = (bf16[192,2048]{1,0:T(8,128)(2,1)}, bf16[192,2048]{1,0:T(8,128)(2,1)S(1)}, u32[]{:S(2)}, u32[]{:S(2)}) collective-permute-start(bf16[192,2048]{1,0:T(8,128)(2,1)} %get-tuple-element.69), channel_id=1, source_target_pairs={{1,3},{2,0},{5,7},{6,4},{9,11},{10,8},{13,15},{14,12},{17,19},{18,... | collective-permute-start | bytes 2359304 | tf_op jit(solution)/shard_map/ppermute | solution.py:427
  205.6 40.1 %collective-permute-start.15 = (bf16[192,2048]{1,0:T(8,128)(2,1)}, bf16[192,2048]{1,0:T(8,128)(2,1)S(1)}, u32[]{:S(2)}, u32[]{:S(2)}) collective-permute-start(bf16[192,2048]{1,0:T(8,128)(2,1)} %get-tuple-element.70), channel_id=1, source_target_pairs={{1,3},{2,0},{5,7},{6,4},{9,11},{10,8},{13,15},{14,12},{17,19},{18,... | collective-permute-start | bytes 2359304 | tf_op jit(solution)/shard_map/ppermute | solution.py:427
  207.1 1.9 copy-start.4
  209.0 1.1 copy-start.6
  210.2 1.1 copy-start.8
  233.4 7.0 %copy-start.10 = (bf16[192,2048]{1,0:T(8,128)(2,1)S(1)}, bf16[192,2048]{1,0:T(8,128)(2,1)}, u32[]{:S(2)}) copy-start(bf16[192,2048]{1,0:T(8,128)(2,1)} %copy-done.9) | copy-start | bytes 2359300
  233.4 7.0 %copy-start.12 = (bf16[192,2048]{1,0:T(8,128)(2,1)S(1)}, bf16[192,2048]{1,0:T(8,128)(2,1)}, u32[]{:S(2)}) copy-start(bf16[192,2048]{1,0:T(8,128)(2,1)} %copy-done.11) | copy-start | bytes 2359300
